TPU v7x, 512 devices: a whole 4x4x16 slice. The times are simulated.
512 devices in a mesh: view: 16 (over y, z_hi), space: 32 (over x, z_lo, core).
Axes of the slice: x: 4, y: 4, z: 16 (z_hi: 4, z_lo: 4; z = z_hi * 4 + z_lo), core: 2. Of those that a mesh axis runs over, the one named last changes fastest.
Arguments:
- latent: bfloat16 [64, 8, 32, 128], P('view', None, 'space'), may hold values from -12 to 12
- camera_edges: int32 [96, 2], replicated, may hold values from 0 to 63, as said below
- conv_in_weight: bfloat16 [3, 3, 8, 1024], replicated, may hold values from -0.75 to 0.75
- query_weight: bfloat16 [1024, 512], replicated, may hold values from -8.75 to 8.75
- key_value_weight: bfloat16 [1024, 1024], replicated, may hold values from -0.1875 to 0.1875
- out_weight: bfloat16 [512, 1024], replicated, may hold values from -0.25 to 0.25
- conv_out_weight: bfloat16 [3, 3, 8, 1024], replicated, may hold values from -0.0625 to 0.0625
Outputs:
- prediction: float32 [64, 8, 32, 128], P('view', None, 'space')
Inputs may be any that keep to these rules, and one draw needn't show every extreme that they name: `camera_edges`: each row is a pair (a, b) with b = (a + d) mod 64 for some d from 1 to 2; no pair appears twice.
All inputs are finite; a program needn't handle non-finite values.
Results may differ from a plain program's by a relative error of at most 0.028.
Values may be sent and summed in bfloat16 or wider, within the bound.
No kernel may reach another device: no remote copies, remote signals or barrier semaphores. Data moves between devices by JAX's collectives and lax.ppermute only.
A program may use at most 64 MiB of HBM per device.

v0:
```python
import math

import jax
import jax.numpy as jnp
from jax import lax
from jax.sharding import PartitionSpec as P

HEADS = 8
HD = 64
REACH = 2


NEG_FILL = -1e30


def extended(cells, sides, width, closed):
    for axis, dim in sides:
        count = lax.axis_size(axis)
        ends = count if closed else count - 1
        head = lax.slice_in_dim(cells, 0, width, axis=dim)
        tail = lax.slice_in_dim(cells, cells.shape[dim] - width, cells.shape[dim], axis=dim)
        cells = jnp.concatenate(
            [
                lax.ppermute(tail, axis, [(i, (i + 1) % count) for i in range(ends)]),
                cells,
                lax.ppermute(head, axis, [((i + 1) % count, i) for i in range(ends)]),
            ],
            axis=dim,
        )
    return cells


def conv_in_apply(framed, weight, row_count):
    padded = jnp.pad(framed, ((0, 0), (0, 0), (0, 0), (1, 1)))
    columns = framed.shape[3]
    pieces = [padded[:, :, i : i + row_count, j : j + columns] for i in range(3) for j in range(3)]
    stacked = jnp.stack(pieces, axis=1)
    patches = jnp.transpose(stacked, (0, 3, 4, 1, 2)).reshape(
        framed.shape[0], row_count, columns, 9 * framed.shape[1]
    )
    flattened = weight.reshape(9 * weight.shape[2], weight.shape[3])
    return jnp.dot(patches, flattened, preferred_element_type=jnp.float32).astype(jnp.bfloat16)


def normalize(hidden):
    widened = hidden.astype(jnp.float32)
    scaling = lax.rsqrt(jnp.mean(widened * widened, axis=-1, keepdims=True) + 1e-06)
    return (widened * scaling).astype(jnp.bfloat16)


def conv_out_apply(padded, weight):
    row_count = padded.shape[1] - 2
    columns = padded.shape[2] - 2
    summed = jnp.zeros((padded.shape[0], weight.shape[2], row_count, columns), jnp.float32)
    for i in range(3):
        for j in range(3):
            window = padded[:, i : i + row_count, j : j + columns]
            summed = summed + jnp.einsum(
                "vrwd,cd->vcrw", window, weight[i, j], preferred_element_type=jnp.float32
            )
    return summed


def soft_attend(scores, near_values, form):
    largest = jnp.max(scores, axis=(2, 3), keepdims=True)
    raised = jnp.exp(scores - largest)
    summed = jnp.sum(raised, axis=(2, 3), keepdims=True)
    soft_weights = (raised / summed).astype(jnp.bfloat16)
    return jnp.einsum(form, soft_weights, near_values, preferred_element_type=jnp.float32).astype(
        jnp.bfloat16
    )


def on_device(
    latent,
    camera_edges,
    conv_in_weight,
    query_weight,
    key_value_weight,
    out_weight,
    conv_out_weight,
):
    local_views = latent.shape[0]
    row_count = latent.shape[2]
    columns = latent.shape[3]
    token_count = row_count * columns
    view_span = local_views + 2 * REACH
    framed = extended(latent, (("space", 2),), 1, False)
    hidden = conv_in_apply(framed, conv_in_weight, row_count)
    normed = normalize(hidden)
    key_values = jnp.dot(normed, key_value_weight, preferred_element_type=jnp.float32).astype(
        jnp.bfloat16
    )
    nearby = extended(key_values, (("view", 0),), REACH, True)
    queries = jnp.dot(normed, query_weight, preferred_element_type=jnp.float32).astype(jnp.bfloat16)
    total_views = local_views * lax.axis_size("view")
    first_view = lax.axis_index("view") * local_views
    own_ids = first_view + jnp.arange(local_views, dtype=jnp.int32)
    near_ids = (first_view - REACH + jnp.arange(view_span, dtype=jnp.int32)) % total_views
    source = camera_edges[:, 0][:, None, None]
    target = camera_edges[:, 1][:, None, None]
    linked = jnp.any(
        (source == own_ids[None, :, None]) & (target == near_ids[None, None, :])
        | (target == own_ids[None, :, None]) & (source == near_ids[None, None, :]),
        axis=0,
    )
    slot_ids = jnp.arange(view_span, dtype=jnp.int32)[None, :]
    place_ids = jnp.arange(local_views, dtype=jnp.int32)[:, None]
    allowed = linked | (slot_ids == place_ids + REACH)
    near_split = nearby.reshape(view_span, token_count, 2, HEADS, HD)
    head_keys = jnp.transpose(near_split[:, :, 0], (2, 0, 1, 3))
    head_values = jnp.transpose(near_split[:, :, 1], (2, 0, 1, 3))
    head_queries = jnp.transpose(queries.reshape(local_views, token_count, HEADS, HD), (2, 0, 1, 3))
    scaling = 1.0 / math.sqrt(HD)

    def one_head(operands):
        head_query, head_key, head_value = operands
        scores = (
            jnp.einsum("vte,use->vtus", head_query, head_key, preferred_element_type=jnp.float32)
            * scaling
        )
        scores = jnp.where(allowed[:, None, :, None], scores, NEG_FILL)
        return soft_attend(scores, head_value, "vtus,use->vte")

    mixed_heads = lax.map(one_head, (head_queries, head_keys, head_values))
    attended = jnp.transpose(mixed_heads, (1, 2, 0, 3)).reshape(
        local_views, row_count, columns, HEADS * HD
    )
    branch = jnp.dot(attended, out_weight, preferred_element_type=jnp.float32)
    hidden_next = (hidden.astype(jnp.float32) + branch).astype(jnp.bfloat16)
    rimmed = extended(hidden_next, (("space", 1),), 1, False)
    padded = jnp.pad(rimmed, ((0, 0), (0, 0), (1, 1), (0, 0)))
    return conv_out_apply(padded, conv_out_weight)


def solution(mesh):
    placed = (P("view", None, "space", None), P(), P(), P(), P(), P(), P())
    return jax.shard_map(
        on_device,
        mesh=mesh,
        in_specs=placed,
        out_specs=P("view", None, "space", None),
        check_vma=False,
    )
```

profile of v0, /device:TPU:6, one launch (start us, length us, event | category | flops | bytes accessed | tf_op | source)
XLA Modules:
  0.0 150.6 jit_solution(12926265207256990826)
XLA Ops:
  0.0 6.4 %collective-permute-start.1 = (bf16[4,8,1,128]{3,1,2,0:T(8,128)(2,1)}, bf16[4,8,1,128]{3,1,2,0:T(8,128)(2,1)S(1)}, u32[]{:S(2)}, u32[]{:S(2)}) collective-permute-start(bf16[4,8,1,128]{3,1,2,0:T(8,128)(2,1)} %param.9), channel_id=1, source_target_pairs={{1,0},{2,1},{3,2},{4,3},{5,4},{6,5},{7,6},{8,7},{9,8},{10,9},{11,1... | collective-permute-start | bytes 24584 | tf_op jit(solution)/shard_map/ppermute | solution.py:26
  6.4 1.9 %collective-permute-start = (bf16[4,8,1,128]{3,1,0,2:T(8,128)(2,1)}, bf16[4,8,1,128]{3,1,0,2:T(8,128)(2,1)S(1)}, u32[]{:S(2)}, u32[]{:S(2)}) collective-permute-start(bf16[4,8,1,128]{3,1,0,2:T(8,128)(2,1)} %bitcast.226), channel_id=1, source_target_pairs={{0,1},{1,2},{2,3},{3,4},{4,5},{5,6},{6,7},{7,8},{8,9},{9,10},{10,1... | collective-permute-start | bytes 24584 | tf_op jit(solution)/shard_map/ppermute | solution.py:24
  9.4 4.9 %collective-permute-done = bf16[4,8,1,128]{3,1,0,2:T(8,128)(2,1)S(1)} collective-permute-done((bf16[4,8,1,128]{3,1,0,2:T(8,128)(2,1)}, bf16[4,8,1,128]{3,1,0,2:T(8,128)(2,1)S(1)}, u32[]{:S(2)}, u32[]{:S(2)}) %collective-permute-start) | collective-permute-done | bytes 8224 | tf_op jit(solution)/shard_map/ppermute | solution.py:24
  16.0 1.5 fusion.23
  20.9 9.1 %collective-permute-start.2 = (bf16[2,1,128,1024]{3,2,0,1:T(8,128)(2,1)}, bf16[2,1,128,1024]{3,2,0,1:T(8,128)(2,1)}, u32[]{:S(2)}, u32[]{:S(2)}) collective-permute-start(bf16[2,1,128,1024]{3,2,0,1:T(8,128)(2,1)} %get-tuple-element.66), channel_id=1, source_target_pairs={{0,32},{32,64},{64,96},{96,128},{128,160},{160,192},{192,224},{224... | collective-permute-start | bytes 1572872 | tf_op jit(solution)/shard_map/ppermute | solution.py:24
  30.0 5.3 %collective-permute-start.3 = (bf16[2,1,128,1024]{3,2,0,1:T(8,128)(2,1)}, bf16[2,1,128,1024]{3,2,0,1:T(8,128)(2,1)}, u32[]{:S(2)}, u32[]{:S(2)}) collective-permute-start(bf16[2,1,128,1024]{3,2,0,1:T(8,128)(2,1)} %get-tuple-element.67), channel_id=1, source_target_pairs={{32,0},{64,32},{96,64},{128,96},{160,128},{192,160},{224,192},{256... | collective-permute-start | bytes 1572872 | tf_op jit(solution)/shard_map/ppermute | solution.py:26
  35.4 2.3 %copy.40 = bf16[4,128,1024]{1,2,0:T(8,128)(2,1)} copy(bf16[4,128,1024]{2,1,0:T(8,128)(2,1)} %copy-done.1) | data formatting | bytes 2097152 | tf_op jit(solution)/shard_map/convert_element_type | solution.py:91
  37.7 2.8 %convolution_convert_fusion.1 = bf16[4,128,512]{2,1,0:T(8,128)(2,1)} fusion(bf16[1024,512]{1,0:T(8,128)(2,1)} %param.12, bf16[4,128,1024]{2,1,0:T(8,128)(2,1)S(1)} %get-tuple-element.75, f32[4,128]{1,0:T(4,128)S(1)} %add_rsqrt_fusion), kind=kOutput, calls=%fused_computation.40 | convolution fusion | flops 538705920 | bytes 2623488 | tf_op jit(solution)/shard_map/dot_general | solution.py:95
  40.4 2.0 %copy.38 = bf16[4,128,512]{1,2,0:T(8,128)(2,1)} copy(bf16[4,128,512]{2,1,0:T(8,128)(2,1)} %convolution_convert_fusion.1) | data formatting | bytes 1048576 | tf_op jit(solution)/shard_map/convert_element_type | solution.py:95
  42.5 21.1 %collective-permute-done.2 = bf16[2,1,128,1024]{3,2,0,1:T(8,128)(2,1)} collective-permute-done((bf16[2,1,128,1024]{3,2,0,1:T(8,128)(2,1)}, bf16[2,1,128,1024]{3,2,0,1:T(8,128)(2,1)}, u32[]{:S(2)}, u32[]{:S(2)}) %collective-permute-start.2) | collective-permute-done | bytes 524320 | tf_op jit(solution)/shard_map/ppermute | solution.py:24
  63.6 2.1 %copy.39 = bf16[2,1,128,1024]{2,3,0,1:T(8,128)(2,1)} copy(bf16[2,1,128,1024]{3,2,0,1:T(8,128)(2,1)} %collective-permute-done.2) | data formatting | bytes 1048576 | tf_op jit(solution)/shard_map/ppermute | solution.py:24
  65.7 12.1 %collective-permute-done.3 = bf16[2,1,128,1024]{3,2,0,1:T(8,128)(2,1)} collective-permute-done((bf16[2,1,128,1024]{3,2,0,1:T(8,128)(2,1)}, bf16[2,1,128,1024]{3,2,0,1:T(8,128)(2,1)}, u32[]{:S(2)}, u32[]{:S(2)}) %collective-permute-start.3) | collective-permute-done | bytes 524320 | tf_op jit(solution)/shard_map/ppermute | solution.py:26
  77.8 2.0 %copy.41 = bf16[2,1,128,1024]{2,3,0,1:T(8,128)(2,1)} copy(bf16[2,1,128,1024]{3,2,0,1:T(8,128)(2,1)} %collective-permute-done.3) | data formatting | bytes 1048576 | tf_op jit(solution)/shard_map/ppermute | solution.py:26
  79.8 1.8 %pad_maximum_fusion = bf16[8,128,2,8,64]{1,4,3,2,0:T(8,128)(2,1)S(1)} fusion(bf16[2,128,2,8,64]{1,4,3,2,0:T(8,128)(2,1)} %bitcast.223, bf16[4,128,2,8,64]{1,4,3,2,0:T(8,128)(2,1)} %bitcast.221, bf16[2,128,2,8,64]{1,4,3,2,0:T(8,128)(2,1)} %bitcast.222), kind=kLoop, calls=%fused_computation.35 | loop fusion | flops 2097152 | bytes 4194304 | tf_op jit(solution)/shard_map/concatenate | solution.py:22
  81.6 1.6 %slice_bitcast_fusion.20 = (bf16[8,8,128,64]{2,3,0,1:T(8,128)(2,1)}, bf16[8,8,128,64]{2,3,0,1:T(8,128)(2,1)}) fusion(bf16[8,128,2,8,64]{1,4,3,2,0:T(8,128)(2,1)S(1)} %pad_maximum_fusion), kind=kLoop, calls=%fused_computation.60 | loop fusion | bytes 4194304 | tf_op jit(solution)/shard_map/transpose | solution.py:112
  83.2 33.8 %while.10 = (s32[]{:T(128)}, bf16[8,4,128,64]{2,3,0,1:T(8,128)(2,1)}, pred[4,8]{1,0:T(4,128)(4,1)S(1)}, bf16[8,4,128,64]{2,3,0,1:T(8,128)(2,1)}, bf16[8,8,128,64...) while((s32[]{:T(128)}, bf16[8,4,128,64]{2,3,0,1:T(8,128)(2,1)}, ...), condition=%wide.region_5.6_spmd, body=%wide.region_2.5_spmd.sunk | while | flops 140540928 | bytes 6697133 | solution.py:125
  83.2 1.4 fusion.89
  85.2 2.2 %fusion.91 = bf16[8,4,128,64]{2,3,0,1:T(8,128)(2,1)} fusion(bf16[8,4,128,64]{2,3,0,1:T(8,128)(2,1)} %get-tuple-element.125, s32[]{:T(128)} %get-tuple-element.124, f32[4,128,8,128]{1,3,2,0:T(8,128)S(1)} %get-tuple-element.115, f32[4,128]{1,0:T(4,128)S(1)} %fusion.90, f32[4,128]{1,0:T(4,128)S(1)} %get-tuple-element.116, ...), kind=kOutput, calls=%fused_computation.8.clone.1 | convolution fusion | flops 69763072 | bytes 2298912 | tf_op jit(solution)/shard_map/while/body/eval_jaxpr/vtus,use->vte/dot_general | solution.py:69
  87.4 1.4 fusion.89
  89.4 2.2 %fusion.91 = bf16[8,4,128,64]{2,3,0,1:T(8,128)(2,1)} fusion(bf16[8,4,128,64]{2,3,0,1:T(8,128)(2,1)} %get-tuple-element.125, s32[]{:T(128)} %get-tuple-element.124, f32[4,128,8,128]{1,3,2,0:T(8,128)S(1)} %get-tuple-element.115, f32[4,128]{1,0:T(4,128)S(1)} %fusion.90, f32[4,128]{1,0:T(4,128)S(1)} %get-tuple-element.116, ...), kind=kOutput, calls=%fused_computation.8.clone.1 | convolution fusion | flops 69763072 | bytes 2298912 | tf_op jit(solution)/shard_map/while/body/eval_jaxpr/vtus,use->vte/dot_general | solution.py:69
  91.6 1.4 fusion.89
  93.6 2.2 %fusion.91 = bf16[8,4,128,64]{2,3,0,1:T(8,128)(2,1)} fusion(bf16[8,4,128,64]{2,3,0,1:T(8,128)(2,1)} %get-tuple-element.125, s32[]{:T(128)} %get-tuple-element.124, f32[4,128,8,128]{1,3,2,0:T(8,128)S(1)} %get-tuple-element.115, f32[4,128]{1,0:T(4,128)S(1)} %fusion.90, f32[4,128]{1,0:T(4,128)S(1)} %get-tuple-element.116, ...), kind=kOutput, calls=%fused_computation.8.clone.1 | convolution fusion | flops 69763072 | bytes 2298912 | tf_op jit(solution)/shard_map/while/body/eval_jaxpr/vtus,use->vte/dot_general | solution.py:69
  95.9 1.4 fusion.89
  97.9 2.2 %fusion.91 = bf16[8,4,128,64]{2,3,0,1:T(8,128)(2,1)} fusion(bf16[8,4,128,64]{2,3,0,1:T(8,128)(2,1)} %get-tuple-element.125, s32[]{:T(128)} %get-tuple-element.124, f32[4,128,8,128]{1,3,2,0:T(8,128)S(1)} %get-tuple-element.115, f32[4,128]{1,0:T(4,128)S(1)} %fusion.90, f32[4,128]{1,0:T(4,128)S(1)} %get-tuple-element.116, ...), kind=kOutput, calls=%fused_computation.8.clone.1 | convolution fusion | flops 69763072 | bytes 2298912 | tf_op jit(solution)/shard_map/while/body/eval_jaxpr/vtus,use->vte/dot_general | solution.py:69
  102.1 2.2 %fusion.91 = bf16[8,4,128,64]{2,3,0,1:T(8,128)(2,1)} fusion(bf16[8,4,128,64]{2,3,0,1:T(8,128)(2,1)} %get-tuple-element.125, s32[]{:T(128)} %get-tuple-element.124, f32[4,128,8,128]{1,3,2,0:T(8,128)S(1)} %get-tuple-element.115, f32[4,128]{1,0:T(4,128)S(1)} %fusion.90, f32[4,128]{1,0:T(4,128)S(1)} %get-tuple-element.116, ...), kind=kOutput, calls=%fused_computation.8.clone.1 | convolution fusion | flops 69763072 | bytes 2298912 | tf_op jit(solution)/shard_map/while/body/eval_jaxpr/vtus,use->vte/dot_general | solution.py:69
  106.3 2.2 %fusion.91 = bf16[8,4,128,64]{2,3,0,1:T(8,128)(2,1)} fusion(bf16[8,4,128,64]{2,3,0,1:T(8,128)(2,1)} %get-tuple-element.125, s32[]{:T(128)} %get-tuple-element.124, f32[4,128,8,128]{1,3,2,0:T(8,128)S(1)} %get-tuple-element.115, f32[4,128]{1,0:T(4,128)S(1)} %fusion.90, f32[4,128]{1,0:T(4,128)S(1)} %get-tuple-element.116, ...), kind=kOutput, calls=%fused_computation.8.clone.1 | convolution fusion | flops 69763072 | bytes 2298912 | tf_op jit(solution)/shard_map/while/body/eval_jaxpr/vtus,use->vte/dot_general | solution.py:69
  110.6 2.2 %fusion.91 = bf16[8,4,128,64]{2,3,0,1:T(8,128)(2,1)} fusion(bf16[8,4,128,64]{2,3,0,1:T(8,128)(2,1)} %get-tuple-element.125, s32[]{:T(128)} %get-tuple-element.124, f32[4,128,8,128]{1,3,2,0:T(8,128)S(1)} %get-tuple-element.115, f32[4,128]{1,0:T(4,128)S(1)} %fusion.90, f32[4,128]{1,0:T(4,128)S(1)} %get-tuple-element.116, ...), kind=kOutput, calls=%fused_computation.8.clone.1 | convolution fusion | flops 69763072 | bytes 2298912 | tf_op jit(solution)/shard_map/while/body/eval_jaxpr/vtus,use->vte/dot_general | solution.py:69
  114.8 2.2 %fusion.91 = bf16[8,4,128,64]{2,3,0,1:T(8,128)(2,1)} fusion(bf16[8,4,128,64]{2,3,0,1:T(8,128)(2,1)} %get-tuple-element.125, s32[]{:T(128)} %get-tuple-element.124, f32[4,128,8,128]{1,3,2,0:T(8,128)S(1)} %get-tuple-element.115, f32[4,128]{1,0:T(4,128)S(1)} %fusion.90, f32[4,128]{1,0:T(4,128)S(1)} %get-tuple-element.116, ...), kind=kOutput, calls=%fused_computation.8.clone.1 | convolution fusion | flops 69763072 | bytes 2298912 | tf_op jit(solution)/shard_map/while/body/eval_jaxpr/vtus,use->vte/dot_general | solution.py:69
  117.0 2.1 %fusion.25 = bf16[4,128,1024]{2,1,0:T(8,128)(2,1)S(1)} fusion(bf16[4,128,1024]{2,1,0:T(8,128)(2,1)S(1)} %get-tuple-element.75, bf16[4,128,512]{1,2,0:T(8,128)(2,1)} %bitcast.42, bf16[512,1024]{1,0:T(8,128)(2,1)} %param.14), kind=kOutput, calls=%fused_computation.34 | convolution fusion | flops 538443776 | bytes 3670016 | tf_op jit(solution)/shard_map/dot_general | solution.py:129
  119.2 1.9 %collective-permute-start.4 = (bf16[4,1,128,1024]{3,2,0,1:T(8,128)(2,1)S(1)}, bf16[4,1,128,1024]{3,2,0,1:T(8,128)(2,1)S(1)}, u32[]{:S(2)}, u32[]{:S(2)}) collective-permute-start(bf16[4,1,128,1024]{3,2,0,1:T(8,128)(2,1)S(1)} %bitcast.218), channel_id=1, source_target_pairs={{0,1},{1,2},{2,3},{3,4},{4,5},{5,6},{6,7},{7,8},{8,9},{9,10},{10,1... | collective-permute-start | bytes 3145736 | tf_op jit(solution)/shard_map/ppermute | solution.py:24
  121.1 6.3 %collective-permute-start.5 = (bf16[4,1,128,1024]{3,2,0,1:T(8,128)(2,1)S(1)}, bf16[4,1,128,1024]{3,2,0,1:T(8,128)(2,1)S(1)}, u32[]{:S(2)}, u32[]{:S(2)}) collective-permute-start(bf16[4,1,128,1024]{3,2,0,1:T(8,128)(2,1)S(1)} %bitcast.219), channel_id=1, source_target_pairs={{1,0},{2,1},{3,2},{4,3},{5,4},{6,5},{7,6},{8,7},{9,8},{10,9},{11,1... | collective-permute-start | bytes 3145736 | tf_op jit(solution)/shard_map/ppermute | solution.py:26
  127.8 17.9 %collective-permute-done.4 = bf16[4,1,128,1024]{3,2,0,1:T(8,128)(2,1)S(1)} collective-permute-done((bf16[4,1,128,1024]{3,2,0,1:T(8,128)(2,1)S(1)}, bf16[4,1,128,1024]{3,2,0,1:T(8,128)(2,1)S(1)}, u32[]{:S(2)}, u32[]{:S(2)}) %collective-permute-start.4) | collective-permute-done | bytes 1048608 | tf_op jit(solution)/shard_map/ppermute | solution.py:24
  (52 shorter events, 21.9 us)
Async XLA Ops:
  0.0 17.5 %copy-start = (bf16[1024,1024]{1,0:T(8,128)(2,1)S(1)}, bf16[1024,1024]{1,0:T(8,128)(2,1)}, u32[]{:S(2)}) copy-start(bf16[1024,1024]{1,0:T(8,128)(2,1)} %param.13) | copy-start | bytes 6291460
  0.0 14.2 %collective-permute-start.1 = (bf16[4,8,1,128]{3,1,2,0:T(8,128)(2,1)}, bf16[4,8,1,128]{3,1,2,0:T(8,128)(2,1)S(1)}, u32[]{:S(2)}, u32[]{:S(2)}) collective-permute-start(bf16[4,8,1,128]{3,1,2,0:T(8,128)(2,1)} %param.9), channel_id=1, source_target_pairs={{1,0},{2,1},{3,2},{4,3},{5,4},{6,5},{7,6},{8,7},{9,8},{10,9},{11,1... | collective-permute-start | bytes 24584 | tf_op jit(solution)/shard_map/ppermute | solution.py:26
  6.4 7.9 %collective-permute-start = (bf16[4,8,1,128]{3,1,0,2:T(8,128)(2,1)}, bf16[4,8,1,128]{3,1,0,2:T(8,128)(2,1)S(1)}, u32[]{:S(2)}, u32[]{:S(2)}) collective-permute-start(bf16[4,8,1,128]{3,1,0,2:T(8,128)(2,1)} %bitcast.226), channel_id=1, source_target_pairs={{0,1},{1,2},{2,3},{3,4},{4,5},{5,6},{6,7},{7,8},{8,9},{9,10},{10,1... | collective-permute-start | bytes 24584 | tf_op jit(solution)/shard_map/ppermute | solution.py:24
  18.8 1.0 copy-start.1
  20.9 42.7 %collective-permute-start.2 = (bf16[2,1,128,1024]{3,2,0,1:T(8,128)(2,1)}, bf16[2,1,128,1024]{3,2,0,1:T(8,128)(2,1)}, u32[]{:S(2)}, u32[]{:S(2)}) collective-permute-start(bf16[2,1,128,1024]{3,2,0,1:T(8,128)(2,1)} %get-tuple-element.66), channel_id=1, source_target_pairs={{0,32},{32,64},{64,96},{96,128},{128,160},{160,192},{192,224},{224... | collective-permute-start | bytes 1572872 | tf_op jit(solution)/shard_map/ppermute | solution.py:24
  30.0 47.8 %collective-permute-start.3 = (bf16[2,1,128,1024]{3,2,0,1:T(8,128)(2,1)}, bf16[2,1,128,1024]{3,2,0,1:T(8,128)(2,1)}, u32[]{:S(2)}, u32[]{:S(2)}) collective-permute-start(bf16[2,1,128,1024]{3,2,0,1:T(8,128)(2,1)} %get-tuple-element.67), channel_id=1, source_target_pairs={{32,0},{64,32},{96,64},{128,96},{160,128},{192,160},{224,192},{256... | collective-permute-start | bytes 1572872 | tf_op jit(solution)/shard_map/ppermute | solution.py:26
  117.0 10.4 %copy-start.2 = (bf16[3,3,8,1024]{3,2,1,0:T(8,128)(2,1)S(1)}, bf16[3,3,8,1024]{3,2,1,0:T(8,128)(2,1)}, u32[]{:S(2)}) copy-start(bf16[3,3,8,1024]{3,2,1,0:T(8,128)(2,1)} %param.15) | copy-start | bytes 442372
  119.2 26.6 %collective-permute-start.4 = (bf16[4,1,128,1024]{3,2,0,1:T(8,128)(2,1)S(1)}, bf16[4,1,128,1024]{3,2,0,1:T(8,128)(2,1)S(1)}, u32[]{:S(2)}, u32[]{:S(2)}) collective-permute-start(bf16[4,1,128,1024]{3,2,0,1:T(8,128)(2,1)S(1)} %bitcast.218), channel_id=1, source_target_pairs={{0,1},{1,2},{2,3},{3,4},{4,5},{5,6},{6,7},{7,8},{8,9},{9,10},{10,1... | collective-permute-start | bytes 3145736 | tf_op jit(solution)/shard_map/ppermute | solution.py:24
  121.1 24.6 %collective-permute-start.5 = (bf16[4,1,128,1024]{3,2,0,1:T(8,128)(2,1)S(1)}, bf16[4,1,128,1024]{3,2,0,1:T(8,128)(2,1)S(1)}, u32[]{:S(2)}, u32[]{:S(2)}) collective-permute-start(bf16[4,1,128,1024]{3,2,0,1:T(8,128)(2,1)S(1)} %bitcast.219), channel_id=1, source_target_pairs={{1,0},{2,1},{3,2},{4,3},{5,4},{6,5},{7,6},{8,7},{9,8},{10,9},{11,1... | collective-permute-start | bytes 3145736 | tf_op jit(solution)/shard_map/ppermute | solution.py:26
where the time goes:
time: 152 us; the launch traced here: 151 us
  waiting for transfers between devices  56 us (37%)
  matrix products  41.1 us (27%)
  starting transfers between devices  30.9 us (20%)
  local copies, waits for them, and re-layouts  13.8 us (9%)
  other arithmetic  8.61 us (6%)
    ppermute x3, waiting for transfers between devices, extended(): lax.ppermute(tail, axis, [(i, (i + 1) % count) for i in range(ends)])  43.9 us
    ppermute x3, starting transfers between devices, extended(): lax.ppermute(head, axis, [((i + 1) % count, i) for i in range(ends)])  18 us
    dot_general x8, matrix products, soft_attend(): jnp.einsum(form, soft_weights, near_values, preferred_element_type=jnp.fl...  17.7 us
    ppermute x3, starting transfers between devices, extended(): lax.ppermute(tail, axis, [(i, (i + 1) % count) for i in range(ends)])  12.9 us
    ppermute x3, waiting for transfers between devices, extended(): lax.ppermute(head, axis, [((i + 1) % count, i) for i in range(ends)])  12.1 us
    dot_general x8, matrix products, one_head(): jnp.einsum('vte,use->vtus', head_query, head_key, preferred_element_type=...  11.6 us
    reduce_sum x8, other arithmetic, soft_attend(): summed = jnp.sum(raised, axis=(2, 3), keepdims=True)  4.51 us
    dot_general x9, matrix products, conv_out_apply(): jnp.einsum('vrwd,cd->vcrw', window, weight[i, j], preferred_element_type=...  4.09 us
  transfers between devices with their start and end apart: 6, of which 4 were waited for; matrix products, arithmetic and copies ran while one was open for 7% of the time, Pallas kernels for 0%

commit v1 on v0

v1 whole, which is shorter than its diff:
```python
import functools
import math

import jax
import jax.numpy as jnp
from jax import lax
from jax.experimental import pallas as pl
from jax.experimental.pallas import tpu as pltpu
from jax.sharding import PartitionSpec as P

HEADS = 8
HD = 64
REACH = 2
TAPS = 72
DEEP = 256
NEG_FILL = -1e30
MIB = 1024 * 1024


def nt_dot(a, b, precision=None):
    return lax.dot_general(
        a, b, (((1,), (1,)), ((), ())), preferred_element_type=jnp.float32, precision=precision
    )


def high(x):
    return x.astype(jnp.bfloat16).astype(jnp.float32)


def split_lanes(x):
    lane = lax.broadcasted_iota(jnp.int32, x.shape, 1)
    first = high(x)
    rest = x - first
    second = high(rest)
    third = rest - second
    return jnp.where(lane < TAPS, first, jnp.where(lane < 2 * TAPS, second, third)).astype(
        jnp.bfloat16
    )


def flat_taps(ref):
    rows = [ref[i, j].astype(jnp.float32) for i in range(3) for j in range(3)]
    return jnp.concatenate(rows, axis=0)


def prepare_kernel(
    views, edges_hbm, conv_in_hbm, wq_hbm, wkv_hbm, wo_hbm, conv_out_hbm,
    gc, mq, mkv, nt, bias, edges_ref, conv_in, wq, wkv, wo, conv_out, sems,
):
    copies = [
        pltpu.make_async_copy(src, dst, sems.at[n])
        for n, (src, dst) in enumerate(
            (
                (edges_hbm, edges_ref),
                (conv_in_hbm, conv_in),
                (conv_out_hbm, conv_out),
                (wq_hbm, wq),
                (wkv_hbm, wkv),
                (wo_hbm, wo),
            )
        )
    ]
    for copy in copies:
        copy.start()
    local = bias.shape[0]
    span = bias.shape[1]
    total = views * local
    first = lax.axis_index("view") * local
    copies[0].wait()
    source = edges_ref[0:1, :]
    target = edges_ref[1:2, :]
    slot = lax.broadcasted_iota(jnp.int32, (span, 1), 0)
    near = first - REACH + slot
    near = jnp.where(near < 0, near + total, near)
    near = jnp.where(near >= total, near - total, near)
    for v in range(local):
        own = first + v
        hit = ((source == own) & (target == near)) | ((target == own) & (source == near))
        linked = jnp.max(hit.astype(jnp.float32), axis=1, keepdims=True)
        linked = jnp.where(slot == v + REACH, 1.0, linked)
        inside = (slot >= v) & (slot <= v + 2 * REACH)
        allowed = (linked > 0.5) & inside
        bias[v] = jnp.broadcast_to(jnp.where(allowed, 0.0, NEG_FILL), bias.shape[1:])
    copies[1].wait()
    wc = flat_taps(conv_in)
    wcb = wc.astype(jnp.bfloat16)
    copies[2].wait()
    wt = flat_taps(conv_out)
    pad = jnp.zeros((DEEP - 3 * TAPS, wc.shape[1]), jnp.float32)
    wc3 = jnp.concatenate([wc, wc, wc, pad], axis=0).astype(jnp.bfloat16)
    both = jnp.concatenate([wc, wt], axis=0).astype(jnp.bfloat16)
    wtb = wt.astype(jnp.bfloat16)
    gc[...] = split_lanes(nt_dot(both, wc3))
    copies[3].wait()
    mq[...] = jnp.dot(wcb, wq[...], preferred_element_type=jnp.float32)
    copies[4].wait()
    mkv[...] = jnp.dot(wcb, wkv[...], preferred_element_type=jnp.float32)
    copies[5].wait()
    nt[...] = nt_dot(wtb, wo[...])


def head_products(mq_ref, mkv_ref, nt_ref, aq, bb):
    lane = lax.broadcasted_iota(jnp.int32, (TAPS, 2 * HD), 1)
    even = (lane < HD).astype(jnp.float32)
    odd = 1.0 - even
    hpad = jnp.zeros((DEEP - 3 * TAPS, 2 * HD), jnp.float32)
    scale = math.log2(math.e) / math.sqrt(HD)
    for g in range(HEADS // 2):
        cols = slice(g * 2 * HD, (g + 1) * 2 * HD)
        vcols = slice(HEADS * HD + g * 2 * HD, HEADS * HD + (g + 1) * 2 * HD)
        q = mq_ref[:, cols] * scale
        k = mkv_ref[:, cols]
        v = mkv_ref[:, vcols]
        q3 = jnp.concatenate([q, q, q, hpad], axis=0)
        k2 = jnp.concatenate([k * even, k * odd], axis=0)
        v2 = jnp.concatenate([v * even, v * odd], axis=0)
        aq[(g + 1) * 2 * TAPS : (g + 2) * 2 * TAPS, :] = split_lanes(
            nt_dot(k2, q3, lax.Precision.HIGHEST)
        )
        b = nt_dot(nt_ref[:, cols], v2, lax.Precision.HIGHEST)
        bh = high(b)
        bb[g] = jnp.concatenate([bh, b - bh], axis=0).astype(jnp.bfloat16)


def shifted(x, by):
    lane = lax.broadcasted_iota(jnp.int32, x.shape, x.ndim - 1)
    width = x.shape[-1]
    if by == 1:
        return jnp.where(lane == 0, 0.0, pltpu.roll(x, 1, x.ndim - 1))
    return jnp.where(lane == width - 1, 0.0, pltpu.roll(x, width - 1, x.ndim - 1))


def is_even(axis):
    return lax.rem(lax.axis_index(axis), 2) == 0


def pack_kernel(own, first, second, after, rows, late, early):
    local = own.shape[0]
    even = is_even("space")
    kind = own.dtype
    for v in range(local):
        one = first[v].astype(jnp.float32)
        two = second[v].astype(jnp.float32)
        rows[v, 0] = jnp.where(even, two, one).astype(kind)
        rows[v, 1] = own[v]
        rows[v, 2] = jnp.where(even, one, two).astype(kind)
    even = is_even("view")
    for n in range(REACH):
        for i in range(3):
            tail = rows[local - REACH + n, i].astype(jnp.float32)
            lead = rows[n, i].astype(jnp.float32)
            early[n, i] = jnp.where(even, tail, lead).astype(kind)
            late[n, i] = jnp.where(even, lead, tail).astype(kind)


def patch_stack(rows):
    parts = []
    for row in rows:
        row = row.astype(jnp.float32)
        parts += [shifted(row, 1), row, shifted(row, -1)]
    patch = jnp.concatenate(parts, axis=0)
    pad = jnp.zeros((DEEP - 3 * TAPS, patch.shape[1]), jnp.float32)
    return jnp.concatenate([patch, patch, patch, pad], axis=0).astype(jnp.bfloat16)


def token_rate(gram_patches, patches):
    square = jnp.sum(gram_patches * patches, axis=0, keepdims=True) * (1.0 / 1024)
    return lax.rsqrt(jnp.maximum(square, 0.0) + 1e-6)


def store_keys(keyed, slots, ahead, kl, vl):
    w = keyed.shape[1] // len(slots)
    kh = high(keyed)
    low = keyed - kh
    sub = lax.broadcasted_iota(jnp.int32, (8, w), 0)
    for n, u in enumerate(slots):
        cols = slice(n * w, (n + 1) * w)
        place = slice(u * w, (u + 1) * w)
        onehot = (sub == u + ahead).astype(jnp.float32)
        h = kh[:, cols]
        r = low[:, cols]
        vl[:, place] = jnp.concatenate([h, jnp.ones((8, w), jnp.float32), r], axis=0).astype(
            jnp.bfloat16
        )
        tall = jnp.concatenate(
            [h, onehot, r, h, jnp.zeros((DEEP - 3 * TAPS - 8, w), jnp.float32)], axis=0
        )
        kl[place, :] = tall.T.astype(jnp.bfloat16)


def own_kernel(rows, gc, mq, mkv, nt, bias, qr, skip, kl, vl, bb, p3, aq):
    local, _, _, w = rows.shape
    aq[0 : 2 * TAPS, :] = gc[...]
    head_products(mq, mkv, nt, aq, bb)
    for v in range(local):
        p3[:, v * w : (v + 1) * w] = patch_stack([rows[v, i] for i in range(3)])
    asked = jnp.dot(aq[...], p3[...], preferred_element_type=jnp.float32)
    patches = p3[0:TAPS, :].astype(jnp.float32)
    rate = token_rate(asked[0:TAPS], patches)
    skip[...] = asked[TAPS : 2 * TAPS]
    store_keys(patches * rate, range(local), REACH, kl, vl)
    for v in range(local):
        for head in range(HEADS):
            q = asked[(head + 2) * TAPS : (head + 3) * TAPS, v * w : (v + 1) * w]
            q = q * rate[:, v * w : (v + 1) * w]
            h = high(q)
            qr[v, :, head * w : (head + 1) * w] = jnp.concatenate(
                [h, bias[v], h, q - h, jnp.zeros((DEEP - 3 * TAPS - 8, w), jnp.float32)], axis=0
            ).astype(jnp.bfloat16)


def mix_kernel(
    second, first, gc, bb, qr, skip, own_kl, own_vl,
    mine, late, early, p3, kl, vl, uh, ul, sc, ex,
):
    local, _, w = mine.shape
    even = is_even("view")
    for u in range(REACH):
        one = [first[u, i].astype(jnp.float32) for i in range(3)]
        two = [second[u, i].astype(jnp.float32) for i in range(3)]
        prev = [jnp.where(even, b, a) for a, b in zip(one, two)]
        nxt = [jnp.where(even, a, b) for a, b in zip(one, two)]
        p3[:, u * w : (u + 1) * w] = patch_stack(prev)
        p3[:, (REACH + u) * w : (REACH + u + 1) * w] = patch_stack(nxt)
    gram = jnp.dot(gc[0:TAPS, :], p3[...], preferred_element_type=jnp.float32)
    patches = p3[0:TAPS, :].astype(jnp.float32)
    rate = token_rate(gram, patches)
    slots = [*range(REACH), *range(REACH + local, 2 * REACH + local)]
    store_keys(patches * rate, slots, 0, kl, vl)
    inner = slice(REACH * w, (REACH + local) * w)
    kl[inner, :] = own_kl[...]
    vl[:, inner] = own_vl[...]
    reach = (2 * REACH + 1) * w
    sc[0] = jnp.dot(kl[0:reach, :], qr[0], preferred_element_type=jnp.float32)
    for v in range(local):
        if v + 1 < local:
            sc[(v + 1) % 2] = jnp.dot(
                kl[(v + 1) * w : (v + 1) * w + reach, :], qr[v + 1],
                preferred_element_type=jnp.float32,
            )
        for head in range(HEADS):
            cols = slice(head * w, (head + 1) * w)
            scores = sc[v % 2, :, cols]
            largest = jnp.max(scores, axis=0, keepdims=True)
            ex[v % 2, :, cols] = jnp.exp2(scores - largest).astype(jnp.bfloat16)
        gathered = jnp.dot(
            vl[:, v * w : v * w + reach], ex[v % 2], preferred_element_type=jnp.float32
        )
        mixed = (gathered[0:TAPS] + gathered[TAPS + 8 :]) / gathered[TAPS : TAPS + 1]
        for g in range(HEADS // 2):
            pair = mixed[:, g * 2 * w : (g + 1) * 2 * w]
            pair = jnp.concatenate([pair[:, :w], pair[:, w:]], axis=0)
            h = pair.astype(jnp.bfloat16)
            uh[g, :, v * w : (v + 1) * w] = h
            ul[g, :, v * w : (v + 1) * w] = (pair - h.astype(jnp.float32)).astype(jnp.bfloat16)
    z = skip[...]
    for g in range(HEADS // 2):
        y = jnp.dot(bb[g], uh[g], preferred_element_type=jnp.float32)
        z = z + y[:TAPS] + y[TAPS:]
        z = z + jnp.dot(bb[g, 0:TAPS, :], ul[g], preferred_element_type=jnp.float32)
    even = is_even("space")
    for v in range(local):
        parts = []
        for i in range(3):
            rows = z[i * 24 : (i + 1) * 24, v * w : (v + 1) * w]
            parts.append(shifted(rows[0:8], 1) + rows[8:16] + shifted(rows[16:24], -1))
        below, mine[v], above = parts
        early[v] = jnp.where(even, below, above)
        late[v] = jnp.where(even, above, below)


def pairs(count, start, closed):
    ends = count if closed else count - 1
    both = []
    for i in range(start, ends, 2):
        both += [(i, (i + 1) % count), ((i + 1) % count, i)]
    return both


def on_device(
    latent,
    camera_edges,
    conv_in_weight,
    query_weight,
    key_value_weight,
    out_weight,
    conv_out_weight,
):
    local, channels, _, w = latent.shape
    span = local + 2 * REACH
    views = lax.axis_size("view")
    space = lax.axis_size("space")
    x = latent.reshape(local, channels, w)
    row_first = lax.ppermute(x, "space", pairs(space, 0, False))
    row_second = lax.ppermute(x, "space", pairs(space, 1, False))

    f32, bf16 = jnp.float32, jnp.bfloat16
    whole = pl.BlockSpec(memory_space=pltpu.VMEM)
    far = pl.BlockSpec(memory_space=pltpu.HBM)
    loaded = (
        camera_edges.T,
        conv_in_weight,
        query_weight,
        key_value_weight,
        out_weight,
        conv_out_weight,
    )
    gc, mq, mkv, nt, bias = pl.pallas_call(
        functools.partial(prepare_kernel, views),
        in_specs=[far] * len(loaded),
        out_specs=[whole] * 5,
        out_shape=[
            pltpu.VMEM((2 * TAPS, DEEP), bf16),
            pltpu.VMEM((TAPS, HEADS * HD), f32),
            pltpu.VMEM((TAPS, 2 * HEADS * HD), f32),
            pltpu.VMEM((TAPS, HEADS * HD), f32),
            pltpu.VMEM((local, span, w), f32),
        ],
        scratch_shapes=[pltpu.VMEM(a.shape, a.dtype) for a in loaded]
        + [pltpu.SemaphoreType.DMA((len(loaded),))],
        compiler_params=pltpu.CompilerParams(vmem_limit_bytes=60 * MIB),
        cost_estimate=pl.CostEstimate(
            flops=3_000_000_000, bytes_accessed=5_000_000, transcendentals=0
        ),
    )(*loaded)

    part = jax.ShapeDtypeStruct((REACH, 3, channels, w), bf16)
    rows, late, early = pl.pallas_call(
        pack_kernel,
        in_specs=[whole] * 3 + [pl.BlockSpec(memory_space=pl.ANY)],
        out_specs=[whole] * 3,
        out_shape=[jax.ShapeDtypeStruct((local, 3, channels, w), bf16), part, part],
        compiler_params=pltpu.CompilerParams(vmem_limit_bytes=4 * MIB),
    )(x, row_first, row_second, bias)
    view_second = lax.ppermute(late, "view", pairs(views, 1, True))
    view_first = lax.ppermute(early, "view", pairs(views, 0, True))

    qr, skip, own_kl, own_vl, bb = pl.pallas_call(
        own_kernel,
        in_specs=[whole] * 6,
        out_specs=[whole] * 5,
        out_shape=[
            jax.ShapeDtypeStruct((local, DEEP, HEADS * w), bf16),
            jax.ShapeDtypeStruct((TAPS, local * w), f32),
            jax.ShapeDtypeStruct((local * w, DEEP), bf16),
            jax.ShapeDtypeStruct((2 * TAPS + 8, local * w), bf16),
            jax.ShapeDtypeStruct((HEADS // 2, 2 * TAPS, 2 * TAPS), bf16),
        ],
        scratch_shapes=[
            pltpu.VMEM((DEEP, local * w), bf16),
            pltpu.VMEM(((HEADS + 2) * TAPS, DEEP), bf16),
        ],
        compiler_params=pltpu.CompilerParams(vmem_limit_bytes=24 * MIB),
        cost_estimate=pl.CostEstimate(
            flops=3_000_000_000, bytes_accessed=1_000_000, transcendentals=0
        ),
    )(rows, gc, mq, mkv, nt, bias)

    plane = jax.ShapeDtypeStruct((local, channels, w), f32)
    mine, late, early = pl.pallas_call(
        mix_kernel,
        in_specs=[whole] * 8,
        out_specs=[whole] * 3,
        out_shape=[plane] * 3,
        scratch_shapes=[
            pltpu.VMEM((DEEP, 2 * REACH * w), bf16),
            pltpu.VMEM((span * w, DEEP), bf16),
            pltpu.VMEM((2 * TAPS + 8, span * w), bf16),
        ]
        + [pltpu.VMEM((HEADS // 2, 2 * TAPS, local * w), bf16)] * 2
        + [
            pltpu.VMEM((2, (2 * REACH + 1) * w, HEADS * w), f32),
            pltpu.VMEM((2, (2 * REACH + 1) * w, HEADS * w), bf16),
        ],
        compiler_params=pltpu.CompilerParams(vmem_limit_bytes=24 * MIB),
        cost_estimate=pl.CostEstimate(
            flops=6_000_000_000, bytes_accessed=1_000_000, transcendentals=3_000_000
        ),
    )(view_second, view_first, gc, bb, qr, skip, own_kl, own_vl)

    row_second = lax.ppermute(late, "space", pairs(space, 1, False))
    row_first = lax.ppermute(early, "space", pairs(space, 0, False))
    return (row_second + mine + row_first).reshape(local, channels, 1, w)


def solution(mesh):
    placed = (P("view", None, "space", None), P(), P(), P(), P(), P(), P())
    return jax.shard_map(
        on_device,
        mesh=mesh,
        in_specs=placed,
        out_specs=P("view", None, "space", None),
        check_vma=False,
    )
```

time: 152 us -> 46.8 us (0.31)
  waiting for transfers between devices: 56 us -> 7.41 us
  matrix products: 41.1 us -> 0 us
  local copies, waits for them, and re-layouts: 13.8 us -> 0.01 us
  Pallas kernels: 0 us -> 9.71 us
  other arithmetic: 8.61 us -> 0.61 us
  starting transfers between devices: 30.9 us -> 28.6 us
    ppermute x6, waiting for transfers between devices: 56 us -> 7.41 us  [the longest x1 4.66 us: on_device(): view_first = lax.ppermute(early, 'view', pairs(views, 0, True))]
    dot_general x29 -> x0, matrix products: 41.1 us -> none  [the longest x8 17.7 us: soft_attend(): jnp.einsum(form, soft_weights, near_values, preferred_element_type=jnp.fl...]
    pallas_call x0 -> x4, Pallas kernels: none -> 9.71 us  [the longest x1 4.6 us: on_device(): pl.pallas_call(mix_kernel, in_specs=[whole] * 8, out_specs=[whole] * 3, o...]
    reduce_sum x8 -> x0, other arithmetic: 4.51 us -> none  [soft_attend(): summed = jnp.sum(raised, axis=(2, 3), keepdims=True)]
    convert_element_type x2 -> x0, local copies, waits for them, and re-layouts: 4.29 us -> none  [the longest x1 2.26 us: on_device(): jnp.dot(normed, key_value_weight, preferred_element_type=jnp.float32)]
    ppermute x2 -> x0, local copies, waits for them, and re-layouts: 4.1 us -> none  [the longest x1 2.05 us: extended(): lax.ppermute(tail, axis, [(i, (i + 1) % count) for i in range(ends)])]
    concatenate x3 -> x0, other arithmetic: 3.7 us -> none  [extended(): jnp.concatenate([lax.ppermute(tail, axis, [(i, (i + 1) % count) for i in...]
    ppermute x6, starting transfers between devices: 30.9 us -> 28.6 us  [the longest x1 12.5 us: on_device(): view_second = lax.ppermute(late, 'view', pairs(views, 1, True))]
  transfers between devices with their start and end apart: 6 -> 6, of which waited for: 4 -> 2; matrix products, arithmetic and copies ran while one was open for 7% -> 0% of each run, Pallas kernels for 0% -> 11%
where the time goes in v1:
time: 46.8 us; the launch traced here: 46.5 us
  starting transfers between devices  28.6 us (61%)
  Pallas kernels  9.71 us (21%)
  waiting for transfers between devices  7.41 us (16%)
  other arithmetic  0.61 us (1%)
    ppermute x1, starting transfers between devices, on_device(): view_second = lax.ppermute(late, 'view', pairs(views, 1, True))  12.5 us
    ppermute x1, starting transfers between devices, on_device(): row_second = lax.ppermute(x, 'space', pairs(space, 1, False))  6.23 us
    ppermute x1, waiting for transfers between devices, on_device(): view_first = lax.ppermute(early, 'view', pairs(views, 0, True))  4.66 us
    pallas_call x1, Pallas kernels, on_device(): pl.pallas_call(mix_kernel, in_specs=[whole] * 8, out_specs=[whole] * 3, o...  4.6 us
    pallas_call x1, Pallas kernels, on_device(): pl.pallas_call(functools.partial(prepare_kernel, views), in_specs=[far] *...  3.08 us
    ppermute x1, starting transfers between devices, on_device(): row_second = lax.ppermute(late, 'space', pairs(space, 1, False))  3.08 us
    ppermute x1, starting transfers between devices, on_device(): view_first = lax.ppermute(early, 'view', pairs(views, 0, True))  3.01 us
    ppermute x1, waiting for transfers between devices, on_device(): row_second = lax.ppermute(late, 'space', pairs(space, 1, False))  2.74 us
  transfers between devices with their start and end apart: 6, of which 2 were waited for; matrix products, arithmetic and copies ran while one was open for 0% of the time, Pallas kernels for 11%

profile of v1, /device:TPU:6, one launch (start us, length us, event | category | flops | bytes accessed | tf_op | source)
XLA Modules:
  0.0 46.5 jit_solution(12769699900242535897)
XLA Ops:
  0.0 6.2 %collective-permute-start.1 = (bf16[4,8,128]{2,1,0:T(8,128)(2,1)}, bf16[4,8,128]{2,1,0:T(8,128)(2,1)S(1)}, u32[]{:S(2)}, u32[]{:S(2)}) collective-permute-start(bf16[4,8,128]{2,1,0:T(8,128)(2,1)} %bitcast.5), channel_id=1, source_target_pairs={{1,2},{2,1},{3,4},{4,3},{5,6},{6,5},{7,8},{8,7},{9,10},{10,9},{11,... | collective-permute-start | bytes 24584 | tf_op jit(solution)/shard_map/ppermute | solution.py:295
  6.2 1.9 %collective-permute-start = (bf16[4,8,128]{2,1,0:T(8,128)(2,1)}, bf16[4,8,128]{2,1,0:T(8,128)(2,1)S(1)}, u32[]{:S(2)}, u32[]{:S(2)}) collective-permute-start(bf16[4,8,128]{2,1,0:T(8,128)(2,1)} %bitcast.6), channel_id=1, source_target_pairs={{0,1},{1,0},{2,3},{3,2},{4,5},{5,4},{6,7},{7,6},{8,9},{9,8},{10,11... | collective-permute-start | bytes 24584 | tf_op jit(solution)/shard_map/ppermute | solution.py:294
  8.2 0.0 copy-start
  8.2 3.1 %shard_map.73 = (bf16[144,256]{1,0:T(8,128)(2,1)S(1)}, f32[72,512]{1,0:T(8,128)S(1)}, f32[72,1024]{1,0:T(8,128)S(1)}, f32[72,512]{1,0:T(8,128)S(1)}, f32[4,8,128]{2,1,0:T(8,128)S(1)}) custom-call(s32[2,96]{1,0:T(2,128)} %bitcast.8, bf16[3,3,8,1024]{3,2,1,0:T(8,128)(2,1)} %conv_in_hbm.1, bf16[1024,512]{1,0:T(8,128)(2,1)} %wq_hbm.1, ...), custom_call_target="tpu_custom_call" | custom-call | flops 3000000000 | bytes 5000000 | tf_op jit(solution)/shard_map/pallas_call | solution.py:308
  11.3 0.0 collective-permute-done.1.second
  11.3 0.0 collective-permute-done.first
  11.3 0.0 copy-done
  11.3 12.5 %collective-permute-start.2 = (bf16[2,3,8,128]{3,2,1,0:T(8,128)(2,1)S(1)}, bf16[2,3,8,128]{3,2,1,0:T(8,128)(2,1)S(1)}, u32[]{:S(2)}, u32[]{:S(2)}) collective-permute-start(bf16[2,3,8,128]{3,2,1,0:T(8,128)(2,1)S(1)} %get-tuple-element.22), channel_id=1, source_target_pairs={{32,64},{64,32},{96,128},{128,96},{160,192},{192,160},{224,256},{2... | collective-permute-start | bytes 36872 | tf_op jit(solution)/shard_map/ppermute | solution.py:335
  23.8 3.0 %collective-permute-start.3 = (bf16[2,3,8,128]{3,2,1,0:T(8,128)(2,1)S(1)}, bf16[2,3,8,128]{3,2,1,0:T(8,128)(2,1)S(1)}, u32[]{:S(2)}, u32[]{:S(2)}) collective-permute-start(bf16[2,3,8,128]{3,2,1,0:T(8,128)(2,1)S(1)} %get-tuple-element.23), channel_id=1, source_target_pairs={{0,32},{32,0},{64,96},{96,64},{128,160},{160,128},{192,224},{224,1... | collective-permute-start | bytes 36872 | tf_op jit(solution)/shard_map/ppermute | solution.py:336
  26.8 2.0 %shard_map.75 = (bf16[4,256,1024]{2,1,0:T(8,128)(2,1)S(1)}, f32[72,512]{1,0:T(8,128)S(1)}, bf16[512,256]{1,0:T(8,128)(2,1)S(1)}, bf16[152,512]{1,0:T(8,128)(2,1)S(1)}, bf16[4,144,144]{2,1,0:T(8,128)(2,1)S(1)}) custom-call(bf16[4,3,8,128]{3,2,1,0:T(8,128)(2,1)S(1)} %get-tuple-element.25.rows, bf16[144,256]{1,0:T(8,128)(2,1)S(1)} %get-tuple-element.24.gc, ...), custom_call_target="tpu_custom_call" | custom-call | flops 3000000000 | bytes 1000000 | tf_op jit(solution)/shard_map/pallas_call | solution.py:338
  28.9 0.0 collective-permute-done.2.second
  28.9 4.7 %collective-permute-done.3.first = bf16[2,3,8,128]{3,2,1,0:T(8,128)(2,1)S(1)} collective-permute-done((bf16[2,3,8,128]{3,2,1,0:T(8,128)(2,1)S(1)}, bf16[2,3,8,128]{3,2,1,0:T(8,128)(2,1)S(1)}, u32[]{:S(2)}, u32[]{:S(2)}) %collective-permute-start.3) | collective-permute-done | bytes 12320 | tf_op jit(solution)/shard_map/ppermute | solution.py:336
  33.5 4.6 %shard_map.76 = (f32[4,8,128]{2,1,0:T(8,128)S(1)}, f32[4,8,128]{2,1,0:T(8,128)S(1)}, f32[4,8,128]{2,1,0:T(8,128)S(1)}) custom-call(bf16[2,3,8,128]{3,2,1,0:T(8,128)(2,1)S(1)} %collective-permute-done.2.second, bf16[2,3,8,128]{3,2,1,0:T(8,128)(2,1)S(1)} %collective-permute-done.3.first, bf16[144,256]{1,0:T(8,128)(2,1)S(1)} %get-tuple-element.24.gc, ...), custom_call_target="tpu_custom_call" | custom-call | flops 6000000000 | bytes 1000000 | tf_op jit(solution)/shard_map/pallas_call | solution.py:360
  38.1 3.1 %collective-permute-start.4 = (f32[4,8,128]{2,1,0:T(8,128)S(1)}, f32[4,8,128]{2,1,0:T(8,128)S(1)}, u32[]{:S(2)}, u32[]{:S(2)}) collective-permute-start(f32[4,8,128]{2,1,0:T(8,128)S(1)} %get-tuple-element.34), channel_id=1, source_target_pairs={{1,2},{2,1},{3,4},{4,3},{5,6},{6,5},{7,8},{8,7},{9,10},{10,9},{11,... | collective-permute-start | bytes 49160 | tf_op jit(solution)/shard_map/ppermute | solution.py:381
  41.2 1.9 %collective-permute-start.5 = (f32[4,8,128]{2,1,0:T(8,128)S(1)}, f32[4,8,128]{2,1,0:T(8,128)S(1)}, u32[]{:S(2)}, u32[]{:S(2)}) collective-permute-start(f32[4,8,128]{2,1,0:T(8,128)S(1)} %get-tuple-element.36), channel_id=1, source_target_pairs={{0,1},{1,0},{2,3},{3,2},{4,5},{5,4},{6,7},{7,6},{8,9},{9,8},{10,11... | collective-permute-start | bytes 49160 | tf_op jit(solution)/shard_map/ppermute | solution.py:382
  43.1 2.7 %collective-permute-done.4 = f32[4,8,128]{2,1,0:T(8,128)S(1)} collective-permute-done((f32[4,8,128]{2,1,0:T(8,128)S(1)}, f32[4,8,128]{2,1,0:T(8,128)S(1)}, u32[]{:S(2)}, u32[]{:S(2)}) %collective-permute-start.4) | collective-permute-done | bytes 16416 | tf_op jit(solution)/shard_map/ppermute | solution.py:381
  45.9 0.0 collective-permute-done.5
  45.9 0.6 %add_add_fusion = f32[4,8,128]{2,1,0:T(8,128)} fusion(f32[4,8,128]{2,1,0:T(8,128)S(1)} %collective-permute-done.5, f32[4,8,128]{2,1,0:T(8,128)S(1)} %collective-permute-done.4, f32[4,8,128]{2,1,0:T(8,128)S(1)} %get-tuple-element.35), kind=kLoop, calls=%fused_computation | loop fusion | flops 8192 | bytes 65536 | tf_op jit(solution)/shard_map/add | solution.py:383
  (1 shorter events, 0.0 us)
Async XLA Ops:
  0.0 11.3 %collective-permute-start.1 = (bf16[4,8,128]{2,1,0:T(8,128)(2,1)}, bf16[4,8,128]{2,1,0:T(8,128)(2,1)S(1)}, u32[]{:S(2)}, u32[]{:S(2)}) collective-permute-start(bf16[4,8,128]{2,1,0:T(8,128)(2,1)} %bitcast.5), channel_id=1, source_target_pairs={{1,2},{2,1},{3,4},{4,3},{5,6},{6,5},{7,8},{8,7},{9,10},{10,9},{11,... | collective-permute-start | bytes 24584 | tf_op jit(solution)/shard_map/ppermute | solution.py:295
  6.2 5.0 %collective-permute-start = (bf16[4,8,128]{2,1,0:T(8,128)(2,1)}, bf16[4,8,128]{2,1,0:T(8,128)(2,1)S(1)}, u32[]{:S(2)}, u32[]{:S(2)}) collective-permute-start(bf16[4,8,128]{2,1,0:T(8,128)(2,1)} %bitcast.6), channel_id=1, source_target_pairs={{0,1},{1,0},{2,3},{3,2},{4,5},{5,4},{6,7},{7,6},{8,9},{9,8},{10,11... | collective-permute-start | bytes 24584 | tf_op jit(solution)/shard_map/ppermute | solution.py:294
  8.2 3.1 %copy-start = (bf16[4,8,1,128]{3,1,2,0:T(8,128)(2,1)S(1)}, bf16[4,8,1,128]{3,1,2,0:T(8,128)(2,1)}, u32[]{:S(2)}) copy-start(bf16[4,8,1,128]{3,1,2,0:T(8,128)(2,1)} %param.7) | copy-start | bytes 24580
  11.3 17.5 %collective-permute-start.2 = (bf16[2,3,8,128]{3,2,1,0:T(8,128)(2,1)S(1)}, bf16[2,3,8,128]{3,2,1,0:T(8,128)(2,1)S(1)}, u32[]{:S(2)}, u32[]{:S(2)}) collective-permute-start(bf16[2,3,8,128]{3,2,1,0:T(8,128)(2,1)S(1)} %get-tuple-element.22), channel_id=1, source_target_pairs={{32,64},{64,32},{96,128},{128,96},{160,192},{192,160},{224,256},{2... | collective-permute-start | bytes 36872 | tf_op jit(solution)/shard_map/ppermute | solution.py:335
  23.8 9.7 %collective-permute-start.3 = (bf16[2,3,8,128]{3,2,1,0:T(8,128)(2,1)S(1)}, bf16[2,3,8,128]{3,2,1,0:T(8,128)(2,1)S(1)}, u32[]{:S(2)}, u32[]{:S(2)}) collective-permute-start(bf16[2,3,8,128]{3,2,1,0:T(8,128)(2,1)S(1)} %get-tuple-element.23), channel_id=1, source_target_pairs={{0,32},{32,0},{64,96},{96,64},{128,160},{160,128},{192,224},{224,1... | collective-permute-start | bytes 36872 | tf_op jit(solution)/shard_map/ppermute | solution.py:336
  38.1 7.8 %collective-permute-start.4 = (f32[4,8,128]{2,1,0:T(8,128)S(1)}, f32[4,8,128]{2,1,0:T(8,128)S(1)}, u32[]{:S(2)}, u32[]{:S(2)}) collective-permute-start(f32[4,8,128]{2,1,0:T(8,128)S(1)} %get-tuple-element.34), channel_id=1, source_target_pairs={{1,2},{2,1},{3,4},{4,3},{5,6},{6,5},{7,8},{8,7},{9,10},{10,9},{11,... | collective-permute-start | bytes 49160 | tf_op jit(solution)/shard_map/ppermute | solution.py:381
  41.2 4.7 %collective-permute-start.5 = (f32[4,8,128]{2,1,0:T(8,128)S(1)}, f32[4,8,128]{2,1,0:T(8,128)S(1)}, u32[]{:S(2)}, u32[]{:S(2)}) collective-permute-start(f32[4,8,128]{2,1,0:T(8,128)S(1)} %get-tuple-element.36), channel_id=1, source_target_pairs={{0,1},{1,0},{2,3},{3,2},{4,5},{5,4},{6,7},{7,6},{8,9},{9,8},{10,11... | collective-permute-start | bytes 49160 | tf_op jit(solution)/shard_map/ppermute | solution.py:382

commit v2 on v1

v2 whole, which is shorter than its diff:
```python
import functools
import math

import jax
import jax.numpy as jnp
from jax import lax
from jax.experimental import pallas as pl
from jax.experimental.pallas import tpu as pltpu
from jax.sharding import PartitionSpec as P

HEADS = 8
HD = 64
REACH = 2
TAPS = 72
DEEP = 256
NEG_FILL = -1e30
MIB = 1024 * 1024


def nt_dot(a, b):
    return lax.dot_general(a, b, (((1,), (1,)), ((), ())), preferred_element_type=jnp.float32)


def high(x):
    return x.astype(jnp.bfloat16).astype(jnp.float32)


def split_lanes(x):
    lane = lax.broadcasted_iota(jnp.int32, x.shape, 1)
    first = high(x)
    rest = x - first
    second = high(rest)
    third = rest - second
    return jnp.where(lane < TAPS, first, jnp.where(lane < 2 * TAPS, second, third)).astype(
        jnp.bfloat16
    )


def flat_taps(ref):
    rows = [ref[i, j].astype(jnp.float32) for i in range(3) for j in range(3)]
    return jnp.concatenate(rows, axis=0)


def prepare_kernel(
    views, edges_hbm, conv_in_hbm, conv_out_hbm, wq_hbm, wkv_hbm, wo_hbm,
    gc, mq, mkv, nt, bias, edges_ref, conv_in, conv_out, wq, wk, wv, wo, sems,
):
    wide = HEADS * HD
    keys, values = slice(0, wide), slice(wide, 2 * wide)
    parts = (
        (edges_hbm, edges_ref),
        (conv_in_hbm, conv_in),
        (wq_hbm, wq),
        (wkv_hbm.at[:, keys], wk),
        (conv_out_hbm, conv_out),
        (wkv_hbm.at[:, values], wv),
        (wo_hbm, wo),
    )
    copies = [pltpu.make_async_copy(src, dst, sems.at[n]) for n, (src, dst) in enumerate(parts)]
    for copy in copies[:4]:
        copy.start()
    local = bias.shape[0]
    span = bias.shape[1]
    total = views * local
    first = lax.axis_index("view") * local
    copies[0].wait()
    source = edges_ref[0:1, :]
    target = edges_ref[1:2, :]
    slot = lax.broadcasted_iota(jnp.int32, (span, 1), 0)
    near = first - REACH + slot
    near = jnp.where(near < 0, near + total, near)
    near = jnp.where(near >= total, near - total, near)
    for v in range(local):
        own = first + v
        hit = ((source == own) & (target == near)) | ((target == own) & (source == near))
        linked = jnp.max(hit.astype(jnp.float32), axis=1, keepdims=True)
        linked = jnp.where(slot == v + REACH, 1.0, linked)
        inside = (slot >= v) & (slot <= v + 2 * REACH)
        allowed = (linked > 0.5) & inside
        bias[v] = jnp.broadcast_to(jnp.where(allowed, 0.0, NEG_FILL), bias.shape[1:])
    copies[1].wait()
    copies[4].start()
    wc = flat_taps(conv_in)
    wcb = wc.astype(jnp.bfloat16)
    copies[2].wait()
    copies[5].start()
    mq[...] = jnp.dot(wcb, wq[...], preferred_element_type=jnp.float32)
    copies[3].wait()
    copies[6].start()
    mkv[:, keys] = jnp.dot(wcb, wk[...], preferred_element_type=jnp.float32)
    copies[4].wait()
    wt = flat_taps(conv_out)
    pad = jnp.zeros((DEEP - 3 * TAPS, wc.shape[1]), jnp.float32)
    wc3 = jnp.concatenate([wc, wc, wc, pad], axis=0).astype(jnp.bfloat16)
    both = jnp.concatenate([wc, wt], axis=0).astype(jnp.bfloat16)
    gc[...] = split_lanes(nt_dot(both, wc3))
    copies[5].wait()
    mkv[:, values] = jnp.dot(wcb, wv[...], preferred_element_type=jnp.float32)
    copies[6].wait()
    nt[...] = nt_dot(wt.astype(jnp.bfloat16), wo[...])


def nt_dot_parts(a, b):
    ah, bh = high(a), high(b)
    left = jnp.concatenate([ah, a - ah, ah], axis=1).astype(jnp.bfloat16)
    right = jnp.concatenate([bh, bh, b - bh], axis=1).astype(jnp.bfloat16)
    return nt_dot(left, right)


def head_products(mq_ref, mkv_ref, nt_ref, aq, bb):
    lane = lax.broadcasted_iota(jnp.int32, (TAPS, 2 * HD), 1)
    even = (lane < HD).astype(jnp.float32)
    odd = 1.0 - even
    hpad = jnp.zeros((DEEP - 3 * TAPS, 2 * HD), jnp.float32)
    scale = math.log2(math.e) / math.sqrt(HD)
    for g in range(HEADS // 2):
        cols = slice(g * 2 * HD, (g + 1) * 2 * HD)
        vcols = slice(HEADS * HD + g * 2 * HD, HEADS * HD + (g + 1) * 2 * HD)
        q = mq_ref[:, cols] * scale
        k = mkv_ref[:, cols]
        v = mkv_ref[:, vcols]
        q3 = jnp.concatenate([q, q, q, hpad], axis=0)
        k2 = jnp.concatenate([k * even, k * odd], axis=0)
        v2 = jnp.concatenate([v * even, v * odd], axis=0)
        aq[(g + 1) * 2 * TAPS : (g + 2) * 2 * TAPS, :] = split_lanes(
            nt_dot_parts(k2, q3)
        )
        b = nt_dot_parts(nt_ref[:, cols], v2)
        bh = high(b)
        bb[g] = jnp.concatenate([bh, b - bh], axis=0).astype(jnp.bfloat16)


def shifted(x, by):
    lane = lax.broadcasted_iota(jnp.int32, x.shape, x.ndim - 1)
    width = x.shape[-1]
    if by == 1:
        return jnp.where(lane == 0, 0.0, pltpu.roll(x, 1, x.ndim - 1))
    return jnp.where(lane == width - 1, 0.0, pltpu.roll(x, width - 1, x.ndim - 1))


def is_even(axis):
    return lax.rem(lax.axis_index(axis), 2) == 0


def pack_kernel(own, first, second, after, rows, tail, lead):
    local = own.shape[0]
    even = is_even("space")
    kind = own.dtype
    for v in range(local):
        one = first[v].astype(jnp.float32)
        two = second[v].astype(jnp.float32)
        rows[v, 0] = jnp.where(even, two, one).astype(kind)
        rows[v, 1] = own[v]
        rows[v, 2] = jnp.where(even, one, two).astype(kind)
    for n in range(REACH):
        for i in range(3):
            tail[n, i] = rows[local - REACH + n, i]
            lead[n, i] = rows[n, i]


def patch_stack(rows):
    parts = []
    for row in rows:
        row = row.astype(jnp.float32)
        parts += [shifted(row, 1), row, shifted(row, -1)]
    patch = jnp.concatenate(parts, axis=0)
    pad = jnp.zeros((DEEP - 3 * TAPS, patch.shape[1]), jnp.float32)
    return jnp.concatenate([patch, patch, patch, pad], axis=0).astype(jnp.bfloat16)


def token_rate(gram_patches, patches):
    square = jnp.sum(gram_patches * patches, axis=0, keepdims=True) * (1.0 / 1024)
    return lax.rsqrt(jnp.maximum(square, 0.0) + 1e-6)


def store_keys(keyed, slots, kl, vl):
    w = keyed.shape[1] // len(slots)
    kh = high(keyed)
    low = keyed - kh
    sub = lax.broadcasted_iota(jnp.int32, (8, w), 0)
    for n, u in enumerate(slots):
        cols = slice(n * w, (n + 1) * w)
        onehot = (sub == u).astype(jnp.float32)
        h = kh[:, cols]
        r = low[:, cols]
        vl[:, cols] = jnp.concatenate([h, jnp.ones((8, w), jnp.float32), r], axis=0).astype(
            jnp.bfloat16
        )
        tall = jnp.concatenate(
            [h, onehot, r, h, jnp.zeros((DEEP - 3 * TAPS - 8, w), jnp.float32)], axis=0
        )
        kl[cols, :] = tall.T.astype(jnp.bfloat16)


def own_kernel(
    rows, gc, mq, mkv, nt, bias, qr, skip, bb, top, acc, p3, aq, kl, vl, sc, ex
):
    local, _, _, w = rows.shape
    aq[0 : 2 * TAPS, :] = gc[...]
    head_products(mq, mkv, nt, aq, bb)
    for v in range(local):
        p3[:, v * w : (v + 1) * w] = patch_stack([rows[v, i] for i in range(3)])
    asked = jnp.dot(aq[...], p3[...], preferred_element_type=jnp.float32)
    patches = p3[0:TAPS, :].astype(jnp.float32)
    rate = token_rate(asked[0:TAPS], patches)
    skip[...] = asked[TAPS : 2 * TAPS]
    store_keys(patches * rate, range(REACH, REACH + local), kl, vl)
    for v in range(local):
        for head in range(HEADS):
            q = asked[(head + 2) * TAPS : (head + 3) * TAPS, v * w : (v + 1) * w]
            q = q * rate[:, v * w : (v + 1) * w]
            h = high(q)
            qr[v, :, head * w : (head + 1) * w] = jnp.concatenate(
                [h, bias[v], h, q - h, jnp.zeros((DEEP - 3 * TAPS - 8, w), jnp.float32)], axis=0
            ).astype(jnp.bfloat16)
    spans = [(max(v - REACH, 0) * w, min(v + REACH + 1, local) * w) for v in range(local)]

    def scored(v):
        lo, hi = spans[v]
        sc[v % 2, 0 : hi - lo, :] = jnp.dot(
            kl[lo:hi, :], qr[v], preferred_element_type=jnp.float32
        )

    scored(0)
    for v in range(local):
        if v + 1 < local:
            scored(v + 1)
        lo, hi = spans[v]
        for head in range(HEADS):
            cols = slice(head * w, (head + 1) * w)
            scores = sc[v % 2, 0 : hi - lo, cols]
            largest = jnp.max(scores, axis=0, keepdims=True)
            top[v : v + 1, cols] = largest
            ex[v % 2, 0 : hi - lo, cols] = jnp.exp2(scores - largest).astype(jnp.bfloat16)
        gathered = jnp.dot(
            vl[:, lo:hi], ex[v % 2, 0 : hi - lo, :], preferred_element_type=jnp.float32
        )
        acc[v, 0:TAPS, :] = gathered[0:TAPS] + gathered[TAPS + 8 :]
        acc[v, TAPS:, :] = gathered[TAPS : TAPS + 8]


def mix_kernel(
    prev, nxt, gc, bb, qr, skip, top, acc,
    mine, late, early, p3, kl, vl, uh, ul, sc, ex,
):
    local, _, w = mine.shape
    for u in range(REACH):
        p3[:, u * w : (u + 1) * w] = patch_stack([prev[u, i] for i in range(3)])
        p3[:, (REACH + u) * w : (REACH + u + 1) * w] = patch_stack([nxt[u, i] for i in range(3)])
    gram = jnp.dot(gc[0:TAPS, :], p3[...], preferred_element_type=jnp.float32)
    patches = p3[0:TAPS, :].astype(jnp.float32)
    rate = token_rate(gram, patches)
    slots = [*range(REACH), *range(REACH + local, 2 * REACH + local)]
    store_keys(patches * rate, slots, kl, vl)
    spans = []
    for v in range(local):
        near = [n for n, u in enumerate(slots) if v <= u <= v + 2 * REACH]
        spans.append((near[0] * w, (near[-1] + 1) * w))
    for v, (lo, hi) in enumerate(spans):
        sc[v, 0 : hi - lo, :] = jnp.dot(
            kl[lo:hi, :], qr[v], preferred_element_type=jnp.float32
        )
    for v, (lo, hi) in enumerate(spans):
        fades = []
        for head in range(HEADS):
            cols = slice(head * w, (head + 1) * w)
            scores = sc[v, 0 : hi - lo, cols]
            before = top[v : v + 1, cols]
            largest = jnp.maximum(jnp.max(scores, axis=0, keepdims=True), before)
            fades.append(jnp.exp2(before - largest))
            ex[v, 0 : hi - lo, cols] = jnp.exp2(scores - largest).astype(jnp.bfloat16)
        fade = jnp.concatenate(fades, axis=1)
        gathered = jnp.dot(
            vl[:, lo:hi], ex[v, 0 : hi - lo, :], preferred_element_type=jnp.float32
        )
        weight = gathered[TAPS : TAPS + 1] + acc[v, TAPS : TAPS + 1, :] * fade
        mixed = gathered[0:TAPS] + gathered[TAPS + 8 :] + acc[v, 0:TAPS, :] * fade
        mixed = mixed * (1.0 / weight)
        for g in range(HEADS // 2):
            pair = mixed[:, g * 2 * w : (g + 1) * 2 * w]
            pair = jnp.concatenate([pair[:, :w], pair[:, w:]], axis=0)
            h = pair.astype(jnp.bfloat16)
            uh[g, :, v * w : (v + 1) * w] = h
            ul[g, :, v * w : (v + 1) * w] = (pair - h.astype(jnp.float32)).astype(jnp.bfloat16)
    z = skip[...]
    for g in range(HEADS // 2):
        y = jnp.dot(bb[g], uh[g], preferred_element_type=jnp.float32)
        z = z + y[:TAPS] + y[TAPS:]
        z = z + jnp.dot(bb[g, 0:TAPS, :], ul[g], preferred_element_type=jnp.float32)
    even = is_even("space")
    for v in range(local):
        parts = []
        for i in range(3):
            rows = z[i * 24 : (i + 1) * 24, v * w : (v + 1) * w]
            parts.append(shifted(rows[0:8], 1) + rows[8:16] + shifted(rows[16:24], -1))
        below, mine[v], above = parts
        early[v] = jnp.where(even, below, above)
        late[v] = jnp.where(even, above, below)


def pairs(count, start):
    both = []
    for i in range(start, count - 1, 2):
        both += [(i, i + 1), (i + 1, i)]
    return both


def on_device(
    latent,
    camera_edges,
    conv_in_weight,
    query_weight,
    key_value_weight,
    out_weight,
    conv_out_weight,
):
    local, channels, _, w = latent.shape
    span = local + 2 * REACH
    views = lax.axis_size("view")
    space = lax.axis_size("space")
    x = latent.reshape(local, channels, w)
    row_first = lax.ppermute(x, "space", pairs(space, 0))
    row_second = lax.ppermute(x, "space", pairs(space, 1))

    f32, bf16 = jnp.float32, jnp.bfloat16
    whole = pl.BlockSpec(memory_space=pltpu.VMEM)
    far = pl.BlockSpec(memory_space=pltpu.HBM)
    loaded = (
        camera_edges.T,
        conv_in_weight,
        conv_out_weight,
        query_weight,
        key_value_weight,
        out_weight,
    )
    gc, mq, mkv, nt, bias = pl.pallas_call(
        functools.partial(prepare_kernel, views),
        in_specs=[far] * len(loaded),
        out_specs=[whole] * 5,
        out_shape=[
            pltpu.VMEM((2 * TAPS, DEEP), bf16),
            pltpu.VMEM((TAPS, HEADS * HD), f32),
            pltpu.VMEM((TAPS, 2 * HEADS * HD), f32),
            pltpu.VMEM((TAPS, HEADS * HD), f32),
            pltpu.VMEM((local, span, w), f32),
        ],
        scratch_shapes=[
            pltpu.VMEM(a.shape, a.dtype)
            for a in (*loaded[:4], query_weight, query_weight, out_weight)
        ]
        + [pltpu.SemaphoreType.DMA((7,))],
        compiler_params=pltpu.CompilerParams(vmem_limit_bytes=60 * MIB),
        cost_estimate=pl.CostEstimate(
            flops=3_000_000_000, bytes_accessed=5_000_000, transcendentals=0
        ),
    )(*loaded)

    part = jax.ShapeDtypeStruct((REACH, 3, channels, w), bf16)
    rows, tail, lead = pl.pallas_call(
        pack_kernel,
        in_specs=[whole] * 3 + [pl.BlockSpec(memory_space=pl.ANY)],
        out_specs=[whole] * 3,
        out_shape=[jax.ShapeDtypeStruct((local, 3, channels, w), bf16), part, part],
        compiler_params=pltpu.CompilerParams(vmem_limit_bytes=4 * MIB),
    )(x, row_first, row_second, bias)
    prev = lax.ppermute(tail, "view", [(i, (i + 1) % views) for i in range(views)])
    nxt = lax.ppermute(lead, "view", [((i + 1) % views, i) for i in range(views)])

    keys_scratch = [
        pltpu.VMEM((local * w, DEEP), bf16),
        pltpu.VMEM((2 * TAPS + 8, local * w), bf16),
    ]
    qr, skip, bb, top, acc = pl.pallas_call(
        own_kernel,
        in_specs=[whole] * 6,
        out_specs=[whole] * 5,
        out_shape=[
            jax.ShapeDtypeStruct((local, DEEP, HEADS * w), bf16),
            jax.ShapeDtypeStruct((TAPS, local * w), f32),
            jax.ShapeDtypeStruct((HEADS // 2, 2 * TAPS, 2 * TAPS), bf16),
            jax.ShapeDtypeStruct((local, HEADS * w), f32),
            jax.ShapeDtypeStruct((local, TAPS + 8, HEADS * w), f32),
        ],
        scratch_shapes=[
            pltpu.VMEM((DEEP, local * w), bf16),
            pltpu.VMEM(((HEADS + 2) * TAPS, DEEP), bf16),
            *keys_scratch,
            pltpu.VMEM((2, local * w, HEADS * w), f32),
            pltpu.VMEM((2, local * w, HEADS * w), bf16),
        ],
        compiler_params=pltpu.CompilerParams(vmem_limit_bytes=24 * MIB),
        cost_estimate=pl.CostEstimate(
            flops=4_000_000_000, bytes_accessed=1_000_000, transcendentals=2_000_000
        ),
    )(rows, gc, mq, mkv, nt, bias)

    plane = jax.ShapeDtypeStruct((local, channels, w), f32)
    mine, late, early = pl.pallas_call(
        mix_kernel,
        in_specs=[whole] * 8,
        out_specs=[whole] * 3,
        out_shape=[plane] * 3,
        scratch_shapes=[
            pltpu.VMEM((DEEP, 2 * REACH * w), bf16),
            *keys_scratch,
            pltpu.VMEM((HEADS // 2, 2 * TAPS, local * w), bf16),
            pltpu.VMEM((HEADS // 2, 2 * TAPS, local * w), bf16),
            pltpu.VMEM((local, REACH * w, HEADS * w), f32),
            pltpu.VMEM((local, REACH * w, HEADS * w), bf16),
        ],
        compiler_params=pltpu.CompilerParams(vmem_limit_bytes=24 * MIB),
        cost_estimate=pl.CostEstimate(
            flops=3_000_000_000, bytes_accessed=1_000_000, transcendentals=1_000_000
        ),
    )(prev, nxt, gc, bb, qr, skip, top, acc)

    row_second = lax.ppermute(late, "space", pairs(space, 1))
    row_first = lax.ppermute(early, "space", pairs(space, 0))
    return (row_second + mine + row_first).reshape(local, channels, 1, w)


def solution(mesh):
    placed = (P("view", None, "space", None), P(), P(), P(), P(), P(), P())
    return jax.shard_map(
        on_device,
        mesh=mesh,
        in_specs=placed,
        out_specs=P("view", None, "space", None),
        check_vma=False,
    )
```

time: 46.8 us -> 41.3 us (0.88)
  waiting for transfers between devices: 7.41 us -> 2.7 us
    ppermute x6, waiting for transfers between devices: 7.41 us -> 2.7 us  [the longest x1 2.03 us: on_device(): row_second = lax.ppermute(late, 'space', pairs(space, 1))]
    pallas_call x1, Pallas kernels: 4.6 us -> 2.21 us  [on_device(): pl.pallas_call(mix_kernel, in_specs=[whole] * 8, out_specs=[whole] * 3, o...]
    pallas_call x1, Pallas kernels: 2.01 us -> 3.49 us  [on_device(): pl.pallas_call(own_kernel, in_specs=[whole] * 6, out_specs=[whole] * 5, o...]
    pallas_call x1, Pallas kernels: 3.08 us -> 3.57 us  [on_device(): pl.pallas_call(functools.partial(prepare_kernel, views), in_specs=[far] *...]
  transfers between devices with their start and end apart: 6 -> 6, of which waited for: 2 -> 2; matrix products, arithmetic and copies ran while one was open for 0% -> 0% of each run, Pallas kernels for 11% -> 17%
where the time goes in v2:
time: 41.3 us; the launch traced here: 41 us
  starting transfers between devices  28.3 us (69%)
  Pallas kernels  9.3 us (23%)
  waiting for transfers between devices  2.7 us (7%)
  other arithmetic  0.61 us (1%)
    ppermute x1, starting transfers between devices, on_device(): lax.ppermute(tail, 'view', [(i, (i + 1) % views) for i in range(views)])  9.1 us
    ppermute x1, starting transfers between devices, on_device(): row_second = lax.ppermute(x, 'space', pairs(space, 1))  6.23 us
    ppermute x1, starting transfers between devices, on_device(): lax.ppermute(lead, 'view', [((i + 1) % views, i) for i in range(views)])  5.32 us
    ppermute x1, starting transfers between devices, on_device(): row_second = lax.ppermute(late, 'space', pairs(space, 1))  3.79 us
    pallas_call x1, Pallas kernels, on_device(): pl.pallas_call(functools.partial(prepare_kernel, views), in_specs=[far] *...  3.57 us
    pallas_call x1, Pallas kernels, on_device(): pl.pallas_call(own_kernel, in_specs=[whole] * 6, out_specs=[whole] * 5, o...  3.49 us
    pallas_call x1, Pallas kernels, on_device(): pl.pallas_call(mix_kernel, in_specs=[whole] * 8, out_specs=[whole] * 3, o...  2.21 us
    ppermute x1, waiting for transfers between devices, on_device(): row_second = lax.ppermute(late, 'space', pairs(space, 1))  2.03 us
  transfers between devices with their start and end apart: 6, of which 2 were waited for; matrix products, arithmetic and copies ran while one was open for 0% of the time, Pallas kernels for 17%

profile of v2, /device:TPU:6, one launch (start us, length us, event | category | flops | bytes accessed | tf_op | source)
XLA Modules:
  0.0 41.0 jit_solution(5791331776952314228)
XLA Ops:
  0.0 6.2 %collective-permute-start.1 = (bf16[4,8,128]{2,1,0:T(8,128)(2,1)}, bf16[4,8,128]{2,1,0:T(8,128)(2,1)S(1)}, u32[]{:S(2)}, u32[]{:S(2)}) collective-permute-start(bf16[4,8,128]{2,1,0:T(8,128)(2,1)} %bitcast.5), channel_id=1, source_target_pairs={{1,2},{2,1},{3,4},{4,3},{5,6},{6,5},{7,8},{8,7},{9,10},{10,9},{11,... | collective-permute-start | bytes 24584 | tf_op jit(solution)/shard_map/ppermute | solution.py:323
  6.2 1.9 %collective-permute-start = (bf16[4,8,128]{2,1,0:T(8,128)(2,1)}, bf16[4,8,128]{2,1,0:T(8,128)(2,1)S(1)}, u32[]{:S(2)}, u32[]{:S(2)}) collective-permute-start(bf16[4,8,128]{2,1,0:T(8,128)(2,1)} %bitcast.6), channel_id=1, source_target_pairs={{0,1},{1,0},{2,3},{3,2},{4,5},{5,4},{6,7},{7,6},{8,9},{9,8},{10,11... | collective-permute-start | bytes 24584 | tf_op jit(solution)/shard_map/ppermute | solution.py:322
  8.2 0.0 copy-start
  8.2 3.6 %shard_map.73 = (bf16[144,256]{1,0:T(8,128)(2,1)S(1)}, f32[72,512]{1,0:T(8,128)S(1)}, f32[72,1024]{1,0:T(8,128)S(1)}, f32[72,512]{1,0:T(8,128)S(1)}, f32[4,8,128]{2,1,0:T(8,128)S(1)}) custom-call(s32[2,96]{1,0:T(2,128)} %bitcast.8, bf16[3,3,8,1024]{3,2,1,0:T(8,128)(2,1)} %conv_in_hbm.1, bf16[3,3,8,1024]{3,2,1,0:T(8,128)(2,1)} %conv_out_hbm.1, ...), custom_call_target="tpu_custom_call" | custom-call | flops 3000000000 | bytes 5000000 | tf_op jit(solution)/shard_map/pallas_call | solution.py:336
  11.8 0.0 collective-permute-done.1.second
  11.8 0.0 collective-permute-done.first
  11.8 0.0 copy-done
  11.8 9.1 %collective-permute-start.2 = (bf16[2,3,8,128]{3,2,1,0:T(8,128)(2,1)S(1)}, bf16[2,3,8,128]{3,2,1,0:T(8,128)(2,1)S(1)}, u32[]{:S(2)}, u32[]{:S(2)}) collective-permute-start(bf16[2,3,8,128]{3,2,1,0:T(8,128)(2,1)S(1)} %get-tuple-element.22), channel_id=1, source_target_pairs={{0,32},{32,64},{64,96},{96,128},{128,160},{160,192},{192,224},{224... | collective-permute-start | bytes 36872 | tf_op jit(solution)/shard_map/ppermute | solution.py:366
  20.9 5.3 %collective-permute-start.3 = (bf16[2,3,8,128]{3,2,1,0:T(8,128)(2,1)S(1)}, bf16[2,3,8,128]{3,2,1,0:T(8,128)(2,1)S(1)}, u32[]{:S(2)}, u32[]{:S(2)}) collective-permute-start(bf16[2,3,8,128]{3,2,1,0:T(8,128)(2,1)S(1)} %get-tuple-element.23), channel_id=1, source_target_pairs={{32,0},{64,32},{96,64},{128,96},{160,128},{192,160},{224,192},{256... | collective-permute-start | bytes 36872 | tf_op jit(solution)/shard_map/ppermute | solution.py:367
  26.2 3.5 %shard_map.75 = (bf16[4,256,1024]{2,1,0:T(8,128)(2,1)S(1)}, f32[72,512]{1,0:T(8,128)S(1)}, bf16[4,144,144]{2,1,0:T(8,128)(2,1)S(1)}, f32[4,1024]{1,0:T(4,128)S(1)}, f32[4,80,1024]{2,1,0:T(8,128)S(1)}) custom-call(bf16[4,3,8,128]{3,2,1,0:T(8,128)(2,1)S(1)} %get-tuple-element.25.rows, bf16[144,256]{1,0:T(8,128)(2,1)S(1)} %get-tuple-element.24.gc, ...), custom_call_target="tpu_custom_call" | custom-call | flops 4000000000 | bytes 1000000 | tf_op jit(solution)/shard_map/pallas_call | solution.py:373
  29.7 0.0 collective-permute-done.2.prev
  29.8 0.7 %collective-permute-done.3.nxt = bf16[2,3,8,128]{3,2,1,0:T(8,128)(2,1)S(1)} collective-permute-done((bf16[2,3,8,128]{3,2,1,0:T(8,128)(2,1)S(1)}, bf16[2,3,8,128]{3,2,1,0:T(8,128)(2,1)S(1)}, u32[]{:S(2)}, u32[]{:S(2)}) %collective-permute-start.3) | collective-permute-done | bytes 12320 | tf_op jit(solution)/shard_map/ppermute | solution.py:367
  30.4 2.2 %shard_map.76 = (f32[4,8,128]{2,1,0:T(8,128)S(1)}, f32[4,8,128]{2,1,0:T(8,128)S(1)}, f32[4,8,128]{2,1,0:T(8,128)S(1)}) custom-call(bf16[2,3,8,128]{3,2,1,0:T(8,128)(2,1)S(1)} %collective-permute-done.2.prev, bf16[2,3,8,128]{3,2,1,0:T(8,128)(2,1)S(1)} %collective-permute-done.3.nxt, bf16[144,256]{1,0:T(8,128)(2,1)S(1)} %get-tuple-element.24.gc, ...), custom_call_target="tpu_custom_call" | custom-call | flops 3000000000 | bytes 1000000 | tf_op jit(solution)/shard_map/pallas_call | solution.py:398
  32.6 3.8 %collective-permute-start.4 = (f32[4,8,128]{2,1,0:T(8,128)S(1)}, f32[4,8,128]{2,1,0:T(8,128)S(1)}, u32[]{:S(2)}, u32[]{:S(2)}) collective-permute-start(f32[4,8,128]{2,1,0:T(8,128)S(1)} %get-tuple-element.34), channel_id=1, source_target_pairs={{1,2},{2,1},{3,4},{4,3},{5,6},{6,5},{7,8},{8,7},{9,10},{10,9},{11,... | collective-permute-start | bytes 49160 | tf_op jit(solution)/shard_map/ppermute | solution.py:417
  36.4 1.9 %collective-permute-start.5 = (f32[4,8,128]{2,1,0:T(8,128)S(1)}, f32[4,8,128]{2,1,0:T(8,128)S(1)}, u32[]{:S(2)}, u32[]{:S(2)}) collective-permute-start(f32[4,8,128]{2,1,0:T(8,128)S(1)} %get-tuple-element.36), channel_id=1, source_target_pairs={{0,1},{1,0},{2,3},{3,2},{4,5},{5,4},{6,7},{7,6},{8,9},{9,8},{10,11... | collective-permute-start | bytes 49160 | tf_op jit(solution)/shard_map/ppermute | solution.py:418
  38.4 2.0 %collective-permute-done.4 = f32[4,8,128]{2,1,0:T(8,128)S(1)} collective-permute-done((f32[4,8,128]{2,1,0:T(8,128)S(1)}, f32[4,8,128]{2,1,0:T(8,128)S(1)}, u32[]{:S(2)}, u32[]{:S(2)}) %collective-permute-start.4) | collective-permute-done | bytes 16416 | tf_op jit(solution)/shard_map/ppermute | solution.py:417
  40.4 0.0 collective-permute-done.5
  40.4 0.6 %add_add_fusion = f32[4,8,128]{2,1,0:T(8,128)} fusion(f32[4,8,128]{2,1,0:T(8,128)S(1)} %collective-permute-done.5, f32[4,8,128]{2,1,0:T(8,128)S(1)} %collective-permute-done.4, f32[4,8,128]{2,1,0:T(8,128)S(1)} %get-tuple-element.35), kind=kLoop, calls=%fused_computation | loop fusion | flops 8192 | bytes 65536 | tf_op jit(solution)/shard_map/add | solution.py:419
  (1 shorter events, 0.0 us)
Async XLA Ops:
  0.0 11.8 %collective-permute-start.1 = (bf16[4,8,128]{2,1,0:T(8,128)(2,1)}, bf16[4,8,128]{2,1,0:T(8,128)(2,1)S(1)}, u32[]{:S(2)}, u32[]{:S(2)}) collective-permute-start(bf16[4,8,128]{2,1,0:T(8,128)(2,1)} %bitcast.5), channel_id=1, source_target_pairs={{1,2},{2,1},{3,4},{4,3},{5,6},{6,5},{7,8},{8,7},{9,10},{10,9},{11,... | collective-permute-start | bytes 24584 | tf_op jit(solution)/shard_map/ppermute | solution.py:323
  6.2 5.5 %collective-permute-start = (bf16[4,8,128]{2,1,0:T(8,128)(2,1)}, bf16[4,8,128]{2,1,0:T(8,128)(2,1)S(1)}, u32[]{:S(2)}, u32[]{:S(2)}) collective-permute-start(bf16[4,8,128]{2,1,0:T(8,128)(2,1)} %bitcast.6), channel_id=1, source_target_pairs={{0,1},{1,0},{2,3},{3,2},{4,5},{5,4},{6,7},{7,6},{8,9},{9,8},{10,11... | collective-permute-start | bytes 24584 | tf_op jit(solution)/shard_map/ppermute | solution.py:322
  8.2 3.6 %copy-start = (bf16[4,8,1,128]{3,1,2,0:T(8,128)(2,1)S(1)}, bf16[4,8,1,128]{3,1,2,0:T(8,128)(2,1)}, u32[]{:S(2)}) copy-start(bf16[4,8,1,128]{3,1,2,0:T(8,128)(2,1)} %param.7) | copy-start | bytes 24580
  11.8 17.9 %collective-permute-start.2 = (bf16[2,3,8,128]{3,2,1,0:T(8,128)(2,1)S(1)}, bf16[2,3,8,128]{3,2,1,0:T(8,128)(2,1)S(1)}, u32[]{:S(2)}, u32[]{:S(2)}) collective-permute-start(bf16[2,3,8,128]{3,2,1,0:T(8,128)(2,1)S(1)} %get-tuple-element.22), channel_id=1, source_target_pairs={{0,32},{32,64},{64,96},{96,128},{128,160},{160,192},{192,224},{224... | collective-permute-start | bytes 36872 | tf_op jit(solution)/shard_map/ppermute | solution.py:366
  20.9 9.5 %collective-permute-start.3 = (bf16[2,3,8,128]{3,2,1,0:T(8,128)(2,1)S(1)}, bf16[2,3,8,128]{3,2,1,0:T(8,128)(2,1)S(1)}, u32[]{:S(2)}, u32[]{:S(2)}) collective-permute-start(bf16[2,3,8,128]{3,2,1,0:T(8,128)(2,1)S(1)} %get-tuple-element.23), channel_id=1, source_target_pairs={{32,0},{64,32},{96,64},{128,96},{160,128},{192,160},{224,192},{256... | collective-permute-start | bytes 36872 | tf_op jit(solution)/shard_map/ppermute | solution.py:367
  32.6 7.8 %collective-permute-start.4 = (f32[4,8,128]{2,1,0:T(8,128)S(1)}, f32[4,8,128]{2,1,0:T(8,128)S(1)}, u32[]{:S(2)}, u32[]{:S(2)}) collective-permute-start(f32[4,8,128]{2,1,0:T(8,128)S(1)} %get-tuple-element.34), channel_id=1, source_target_pairs={{1,2},{2,1},{3,4},{4,3},{5,6},{6,5},{7,8},{8,7},{9,10},{10,9},{11,... | collective-permute-start | bytes 49160 | tf_op jit(solution)/shard_map/ppermute | solution.py:417
  36.4 4.0 %collective-permute-start.5 = (f32[4,8,128]{2,1,0:T(8,128)S(1)}, f32[4,8,128]{2,1,0:T(8,128)S(1)}, u32[]{:S(2)}, u32[]{:S(2)}) collective-permute-start(f32[4,8,128]{2,1,0:T(8,128)S(1)} %get-tuple-element.36), channel_id=1, source_target_pairs={{0,1},{1,0},{2,3},{3,2},{4,5},{5,4},{6,7},{7,6},{8,9},{9,8},{10,11... | collective-permute-start | bytes 49160 | tf_op jit(solution)/shard_map/ppermute | solution.py:418

commit v3 on v2

--- a/solution.py
+++ b/solution.py
@@ -42,8 +42,8 @@
 
 
 def prepare_kernel(
-    views, edges_hbm, conv_in_hbm, conv_out_hbm, wq_hbm, wkv_hbm, wo_hbm,
-    gc, mq, mkv, nt, bias, edges_ref, conv_in, conv_out, wq, wk, wv, wo, sems,
+    views, edges_hbm, conv_in_hbm, conv_out_hbm, wq_hbm, wkv_hbm,
+    gc, mq, mkv, wt, bias, edges_ref, conv_in, conv_out, wq, wk, wv, sems,
 ):
     wide = HEADS * HD
     keys, values = slice(0, wide), slice(wide, 2 * wide)
@@ -54,10 +54,9 @@
         (wkv_hbm.at[:, keys], wk),
         (conv_out_hbm, conv_out),
         (wkv_hbm.at[:, values], wv),
-        (wo_hbm, wo),
     )
     copies = [pltpu.make_async_copy(src, dst, sems.at[n]) for n, (src, dst) in enumerate(parts)]
-    for copy in copies[:4]:
+    for copy in copies:
         copy.start()
     local = bias.shape[0]
     span = bias.shape[1]
@@ -79,25 +78,21 @@
         allowed = (linked > 0.5) & inside
         bias[v] = jnp.broadcast_to(jnp.where(allowed, 0.0, NEG_FILL), bias.shape[1:])
     copies[1].wait()
-    copies[4].start()
     wc = flat_taps(conv_in)
     wcb = wc.astype(jnp.bfloat16)
     copies[2].wait()
-    copies[5].start()
     mq[...] = jnp.dot(wcb, wq[...], preferred_element_type=jnp.float32)
     copies[3].wait()
-    copies[6].start()
     mkv[:, keys] = jnp.dot(wcb, wk[...], preferred_element_type=jnp.float32)
     copies[4].wait()
-    wt = flat_taps(conv_out)
+    taps = flat_taps(conv_out)
+    wt[...] = taps.astype(jnp.bfloat16)
     pad = jnp.zeros((DEEP - 3 * TAPS, wc.shape[1]), jnp.float32)
     wc3 = jnp.concatenate([wc, wc, wc, pad], axis=0).astype(jnp.bfloat16)
-    both = jnp.concatenate([wc, wt], axis=0).astype(jnp.bfloat16)
+    both = jnp.concatenate([wc, taps], axis=0).astype(jnp.bfloat16)
     gc[...] = split_lanes(nt_dot(both, wc3))
     copies[5].wait()
     mkv[:, values] = jnp.dot(wcb, wv[...], preferred_element_type=jnp.float32)
-    copies[6].wait()
-    nt[...] = nt_dot(wt.astype(jnp.bfloat16), wo[...])
 
 
 def nt_dot_parts(a, b):
@@ -107,7 +102,7 @@
     return nt_dot(left, right)
 
 
-def head_products(mq_ref, mkv_ref, nt_ref, aq, bb):
+def head_products(mq_ref, mkv_ref, nt, aq, bb):
     lane = lax.broadcasted_iota(jnp.int32, (TAPS, 2 * HD), 1)
     even = (lane < HD).astype(jnp.float32)
     odd = 1.0 - even
@@ -125,7 +120,7 @@
         aq[(g + 1) * 2 * TAPS : (g + 2) * 2 * TAPS, :] = split_lanes(
             nt_dot_parts(k2, q3)
         )
-        b = nt_dot_parts(nt_ref[:, cols], v2)
+        b = nt_dot_parts(nt[:, cols], v2)
         bh = high(b)
         bb[g] = jnp.concatenate([bh, b - bh], axis=0).astype(jnp.bfloat16)
 
@@ -193,11 +188,11 @@
 
 
 def own_kernel(
-    rows, gc, mq, mkv, nt, bias, qr, skip, bb, top, acc, p3, aq, kl, vl, sc, ex
+    rows, gc, mq, mkv, wt, wo, bias, qr, skip, bb, top, acc, p3, aq, kl, vl, sc, ex
 ):
     local, _, _, w = rows.shape
     aq[0 : 2 * TAPS, :] = gc[...]
-    head_products(mq, mkv, nt, aq, bb)
+    head_products(mq, mkv, nt_dot(wt[...], wo[...]), aq, bb)
     for v in range(local):
         p3[:, v * w : (v + 1) * w] = patch_stack([rows[v, i] for i in range(3)])
     asked = jnp.dot(aq[...], p3[...], preferred_element_type=jnp.float32)
@@ -331,9 +326,8 @@
         conv_out_weight,
         query_weight,
         key_value_weight,
-        out_weight,
     )
-    gc, mq, mkv, nt, bias = pl.pallas_call(
+    gc, mq, mkv, wt, bias = pl.pallas_call(
         functools.partial(prepare_kernel, views),
         in_specs=[far] * len(loaded),
         out_specs=[whole] * 5,
@@ -341,14 +335,14 @@
             pltpu.VMEM((2 * TAPS, DEEP), bf16),
             pltpu.VMEM((TAPS, HEADS * HD), f32),
             pltpu.VMEM((TAPS, 2 * HEADS * HD), f32),
-            pltpu.VMEM((TAPS, HEADS * HD), f32),
+            pltpu.VMEM((TAPS, out_weight.shape[1]), bf16),
             pltpu.VMEM((local, span, w), f32),
         ],
         scratch_shapes=[
             pltpu.VMEM(a.shape, a.dtype)
-            for a in (*loaded[:4], query_weight, query_weight, out_weight)
+            for a in (*loaded[:4], query_weight, query_weight)
         ]
-        + [pltpu.SemaphoreType.DMA((7,))],
+        + [pltpu.SemaphoreType.DMA((6,))],
         compiler_params=pltpu.CompilerParams(vmem_limit_bytes=60 * MIB),
         cost_estimate=pl.CostEstimate(
             flops=3_000_000_000, bytes_accessed=5_000_000, transcendentals=0
@@ -372,7 +366,7 @@
     ]
     qr, skip, bb, top, acc = pl.pallas_call(
         own_kernel,
-        in_specs=[whole] * 6,
+        in_specs=[whole] * 7,
         out_specs=[whole] * 5,
         out_shape=[
             jax.ShapeDtypeStruct((local, DEEP, HEADS * w), bf16),
@@ -392,7 +386,7 @@
         cost_estimate=pl.CostEstimate(
             flops=4_000_000_000, bytes_accessed=1_000_000, transcendentals=2_000_000
         ),
-    )(rows, gc, mq, mkv, nt, bias)
+    )(rows, gc, mq, mkv, wt, out_weight, bias)
 
     plane = jax.ShapeDtypeStruct((local, channels, w), f32)
     mine, late, early = pl.pallas_call(

time: 41.3 us -> 40.5 us (0.981)
  waiting for transfers between devices: 2.7 us -> 2.18 us
  Pallas kernels: 9.3 us -> 8.81 us
    pallas_call x1, Pallas kernels: 3.57 us -> 2.89 us  [on_device(): pl.pallas_call(functools.partial(prepare_kernel, views), in_specs=[far] *...]
  transfers between devices with their start and end apart: 6 -> 6, of which waited for: 2 -> 2; matrix products, arithmetic and copies ran while one was open for 0% -> 0% of each run, Pallas kernels for 17% -> 16%
where the time goes in v3:
time: 40.5 us; the launch traced here: 40.3 us
  starting transfers between devices  28.5 us (70%)
  Pallas kernels  8.81 us (22%)
  waiting for transfers between devices  2.18 us (5%)
  other arithmetic  0.61 us (2%)
    ppermute x1, starting transfers between devices, on_device(): lax.ppermute(tail, 'view', [(i, (i + 1) % views) for i in range(views)])  9.09 us
    ppermute x1, starting transfers between devices, on_device(): row_second = lax.ppermute(x, 'space', pairs(space, 1))  6.23 us
    ppermute x1, starting transfers between devices, on_device(): lax.ppermute(lead, 'view', [((i + 1) % views, i) for i in range(views)])  5.32 us
    ppermute x1, starting transfers between devices, on_device(): row_second = lax.ppermute(late, 'space', pairs(space, 1))  4.05 us
    pallas_call x1, Pallas kernels, on_device(): pl.pallas_call(own_kernel, in_specs=[whole] * 7, out_specs=[whole] * 5, o...  3.74 us
    pallas_call x1, Pallas kernels, on_device(): pl.pallas_call(functools.partial(prepare_kernel, views), in_specs=[far] *...  2.89 us
    pallas_call x1, Pallas kernels, on_device(): pl.pallas_call(mix_kernel, in_specs=[whole] * 8, out_specs=[whole] * 3, o...  2.16 us
    ppermute x1, starting transfers between devices, on_device(): row_first = lax.ppermute(early, 'space', pairs(space, 0))  1.92 us
  transfers between devices with their start and end apart: 6, of which 2 were waited for; matrix products, arithmetic and copies ran while one was open for 0% of the time, Pallas kernels for 16%

profile of v3, /device:TPU:6, one launch (start us, length us, event | category | flops | bytes accessed | tf_op | source)
XLA Modules:
  0.0 40.3 jit_solution(1947450308210074917)
XLA Ops:
  0.0 6.2 %collective-permute-start.1 = (bf16[4,8,128]{2,1,0:T(8,128)(2,1)}, bf16[4,8,128]{2,1,0:T(8,128)(2,1)S(1)}, u32[]{:S(2)}, u32[]{:S(2)}) collective-permute-start(bf16[4,8,128]{2,1,0:T(8,128)(2,1)} %bitcast.5), channel_id=1, source_target_pairs={{1,2},{2,1},{3,4},{4,3},{5,6},{6,5},{7,8},{8,7},{9,10},{10,9},{11,... | collective-permute-start | bytes 24584 | tf_op jit(solution)/shard_map/ppermute | solution.py:318
  6.2 1.9 %collective-permute-start = (bf16[4,8,128]{2,1,0:T(8,128)(2,1)}, bf16[4,8,128]{2,1,0:T(8,128)(2,1)S(1)}, u32[]{:S(2)}, u32[]{:S(2)}) collective-permute-start(bf16[4,8,128]{2,1,0:T(8,128)(2,1)} %bitcast.6), channel_id=1, source_target_pairs={{0,1},{1,0},{2,3},{3,2},{4,5},{5,4},{6,7},{7,6},{8,9},{9,8},{10,11... | collective-permute-start | bytes 24584 | tf_op jit(solution)/shard_map/ppermute | solution.py:317
  8.2 0.0 copy-start
  8.2 0.0 copy-start.1
  8.2 2.9 %shard_map.73 = (bf16[144,256]{1,0:T(8,128)(2,1)S(1)}, f32[72,512]{1,0:T(8,128)S(1)}, f32[72,1024]{1,0:T(8,128)S(1)}, bf16[72,1024]{1,0:T(8,128)(2,1)S(1)}, f32[4,8,128]{2,1,0:T(8,128)S(1)}) custom-call(s32[2,96]{1,0:T(2,128)} %bitcast.8, bf16[3,3,8,1024]{3,2,1,0:T(8,128)(2,1)} %conv_in_hbm.1, bf16[3,3,8,1024]{3,2,1,0:T(8,128)(2,1)} %conv_out_hbm.1, ...), custom_call_target="tpu_custom_call" | custom-call | flops 3000000000 | bytes 5000000 | tf_op jit(solution)/shard_map/pallas_call | solution.py:330
  11.1 0.0 collective-permute-done.1.second
  11.1 0.0 collective-permute-done.first
  11.1 0.0 copy-done
  11.1 9.1 %collective-permute-start.2 = (bf16[2,3,8,128]{3,2,1,0:T(8,128)(2,1)S(1)}, bf16[2,3,8,128]{3,2,1,0:T(8,128)(2,1)S(1)}, u32[]{:S(2)}, u32[]{:S(2)}) collective-permute-start(bf16[2,3,8,128]{3,2,1,0:T(8,128)(2,1)S(1)} %get-tuple-element.22), channel_id=1, source_target_pairs={{0,32},{32,64},{64,96},{96,128},{128,160},{160,192},{192,224},{224... | collective-permute-start | bytes 36872 | tf_op jit(solution)/shard_map/ppermute | solution.py:360
  20.2 5.3 %collective-permute-start.3 = (bf16[2,3,8,128]{3,2,1,0:T(8,128)(2,1)S(1)}, bf16[2,3,8,128]{3,2,1,0:T(8,128)(2,1)S(1)}, u32[]{:S(2)}, u32[]{:S(2)}) collective-permute-start(bf16[2,3,8,128]{3,2,1,0:T(8,128)(2,1)S(1)} %get-tuple-element.23), channel_id=1, source_target_pairs={{32,0},{64,32},{96,64},{128,96},{160,128},{192,160},{224,192},{256... | collective-permute-start | bytes 36872 | tf_op jit(solution)/shard_map/ppermute | solution.py:361
  25.6 0.0 copy-done.1
  25.6 3.7 %shard_map.75 = (bf16[4,256,1024]{2,1,0:T(8,128)(2,1)S(1)}, f32[72,512]{1,0:T(8,128)S(1)}, bf16[4,144,144]{2,1,0:T(8,128)(2,1)S(1)}, f32[4,1024]{1,0:T(4,128)S(1)}, f32[4,80,1024]{2,1,0:T(8,128)S(1)}) custom-call(bf16[4,3,8,128]{3,2,1,0:T(8,128)(2,1)S(1)} %get-tuple-element.25.rows, bf16[144,256]{1,0:T(8,128)(2,1)S(1)} %get-tuple-element.24.gc, ...), custom_call_target="tpu_custom_call" | custom-call | flops 4000000000 | bytes 1000000 | tf_op jit(solution)/shard_map/pallas_call | solution.py:367
  29.3 0.0 collective-permute-done.2.prev
  29.3 0.4 collective-permute-done.3.nxt
  29.7 2.2 %shard_map.76 = (f32[4,8,128]{2,1,0:T(8,128)S(1)}, f32[4,8,128]{2,1,0:T(8,128)S(1)}, f32[4,8,128]{2,1,0:T(8,128)S(1)}) custom-call(bf16[2,3,8,128]{3,2,1,0:T(8,128)(2,1)S(1)} %collective-permute-done.2.prev, bf16[2,3,8,128]{3,2,1,0:T(8,128)(2,1)S(1)} %collective-permute-done.3.nxt, bf16[144,256]{1,0:T(8,128)(2,1)S(1)} %get-tuple-element.24.gc, ...), custom_call_target="tpu_custom_call" | custom-call | flops 3000000000 | bytes 1000000 | tf_op jit(solution)/shard_map/pallas_call | solution.py:392
  31.9 4.0 %collective-permute-start.4 = (f32[4,8,128]{2,1,0:T(8,128)S(1)}, f32[4,8,128]{2,1,0:T(8,128)S(1)}, u32[]{:S(2)}, u32[]{:S(2)}) collective-permute-start(f32[4,8,128]{2,1,0:T(8,128)S(1)} %get-tuple-element.34), channel_id=1, source_target_pairs={{1,2},{2,1},{3,4},{4,3},{5,6},{6,5},{7,8},{8,7},{9,10},{10,9},{11,... | collective-permute-start | bytes 49160 | tf_op jit(solution)/shard_map/ppermute | solution.py:411
  36.0 1.9 %collective-permute-start.5 = (f32[4,8,128]{2,1,0:T(8,128)S(1)}, f32[4,8,128]{2,1,0:T(8,128)S(1)}, u32[]{:S(2)}, u32[]{:S(2)}) collective-permute-start(f32[4,8,128]{2,1,0:T(8,128)S(1)} %get-tuple-element.36), channel_id=1, source_target_pairs={{0,1},{1,0},{2,3},{3,2},{4,5},{5,4},{6,7},{7,6},{8,9},{9,8},{10,11... | collective-permute-start | bytes 49160 | tf_op jit(solution)/shard_map/ppermute | solution.py:412
  37.9 1.8 %collective-permute-done.4 = f32[4,8,128]{2,1,0:T(8,128)S(1)} collective-permute-done((f32[4,8,128]{2,1,0:T(8,128)S(1)}, f32[4,8,128]{2,1,0:T(8,128)S(1)}, u32[]{:S(2)}, u32[]{:S(2)}) %collective-permute-start.4) | collective-permute-done | bytes 16416 | tf_op jit(solution)/shard_map/ppermute | solution.py:411
  39.7 0.0 collective-permute-done.5
  39.7 0.6 %add_add_fusion = f32[4,8,128]{2,1,0:T(8,128)} fusion(f32[4,8,128]{2,1,0:T(8,128)S(1)} %collective-permute-done.5, f32[4,8,128]{2,1,0:T(8,128)S(1)} %collective-permute-done.4, f32[4,8,128]{2,1,0:T(8,128)S(1)} %get-tuple-element.35), kind=kLoop, calls=%fused_computation | loop fusion | flops 8192 | bytes 65536 | tf_op jit(solution)/shard_map/add | solution.py:413
  (1 shorter events, 0.0 us)
Async XLA Ops:
  0.0 11.1 %collective-permute-start.1 = (bf16[4,8,128]{2,1,0:T(8,128)(2,1)}, bf16[4,8,128]{2,1,0:T(8,128)(2,1)S(1)}, u32[]{:S(2)}, u32[]{:S(2)}) collective-permute-start(bf16[4,8,128]{2,1,0:T(8,128)(2,1)} %bitcast.5), channel_id=1, source_target_pairs={{1,2},{2,1},{3,4},{4,3},{5,6},{6,5},{7,8},{8,7},{9,10},{10,9},{11,... | collective-permute-start | bytes 24584 | tf_op jit(solution)/shard_map/ppermute | solution.py:318
  6.2 4.9 %collective-permute-start = (bf16[4,8,128]{2,1,0:T(8,128)(2,1)}, bf16[4,8,128]{2,1,0:T(8,128)(2,1)S(1)}, u32[]{:S(2)}, u32[]{:S(2)}) collective-permute-start(bf16[4,8,128]{2,1,0:T(8,128)(2,1)} %bitcast.6), channel_id=1, source_target_pairs={{0,1},{1,0},{2,3},{3,2},{4,5},{5,4},{6,7},{7,6},{8,9},{9,8},{10,11... | collective-permute-start | bytes 24584 | tf_op jit(solution)/shard_map/ppermute | solution.py:317
  8.2 2.9 %copy-start = (bf16[4,8,1,128]{3,1,2,0:T(8,128)(2,1)S(1)}, bf16[4,8,1,128]{3,1,2,0:T(8,128)(2,1)}, u32[]{:S(2)}) copy-start(bf16[4,8,1,128]{3,1,2,0:T(8,128)(2,1)} %param.7) | copy-start | bytes 24580
  8.2 17.4 %copy-start.1 = (bf16[512,1024]{1,0:T(8,128)(2,1)S(1)}, bf16[512,1024]{1,0:T(8,128)(2,1)}, u32[]{:S(2)}) copy-start(bf16[512,1024]{1,0:T(8,128)(2,1)} %wo.1) | copy-start | bytes 3145732
  11.1 18.2 %collective-permute-start.2 = (bf16[2,3,8,128]{3,2,1,0:T(8,128)(2,1)S(1)}, bf16[2,3,8,128]{3,2,1,0:T(8,128)(2,1)S(1)}, u32[]{:S(2)}, u32[]{:S(2)}) collective-permute-start(bf16[2,3,8,128]{3,2,1,0:T(8,128)(2,1)S(1)} %get-tuple-element.22), channel_id=1, source_target_pairs={{0,32},{32,64},{64,96},{96,128},{128,160},{160,192},{192,224},{224... | collective-permute-start | bytes 36872 | tf_op jit(solution)/shard_map/ppermute | solution.py:360
  20.2 9.5 %collective-permute-start.3 = (bf16[2,3,8,128]{3,2,1,0:T(8,128)(2,1)S(1)}, bf16[2,3,8,128]{3,2,1,0:T(8,128)(2,1)S(1)}, u32[]{:S(2)}, u32[]{:S(2)}) collective-permute-start(bf16[2,3,8,128]{3,2,1,0:T(8,128)(2,1)S(1)} %get-tuple-element.23), channel_id=1, source_target_pairs={{32,0},{64,32},{96,64},{128,96},{160,128},{192,160},{224,192},{256... | collective-permute-start | bytes 36872 | tf_op jit(solution)/shard_map/ppermute | solution.py:361
  31.9 7.8 %collective-permute-start.4 = (f32[4,8,128]{2,1,0:T(8,128)S(1)}, f32[4,8,128]{2,1,0:T(8,128)S(1)}, u32[]{:S(2)}, u32[]{:S(2)}) collective-permute-start(f32[4,8,128]{2,1,0:T(8,128)S(1)} %get-tuple-element.34), channel_id=1, source_target_pairs={{1,2},{2,1},{3,4},{4,3},{5,6},{6,5},{7,8},{8,7},{9,10},{10,9},{11,... | collective-permute-start | bytes 49160 | tf_op jit(solution)/shard_map/ppermute | solution.py:411
  36.0 3.7 %collective-permute-start.5 = (f32[4,8,128]{2,1,0:T(8,128)S(1)}, f32[4,8,128]{2,1,0:T(8,128)S(1)}, u32[]{:S(2)}, u32[]{:S(2)}) collective-permute-start(f32[4,8,128]{2,1,0:T(8,128)S(1)} %get-tuple-element.36), channel_id=1, source_target_pairs={{0,1},{1,0},{2,3},{3,2},{4,5},{5,4},{6,7},{7,6},{8,9},{9,8},{10,11... | collective-permute-start | bytes 49160 | tf_op jit(solution)/shard_map/ppermute | solution.py:412

commit v4 on v3

--- a/solution.py
+++ b/solution.py
@@ -43,17 +43,14 @@
 
 def prepare_kernel(
     views, edges_hbm, conv_in_hbm, conv_out_hbm, wq_hbm, wkv_hbm,
-    gc, mq, mkv, wt, bias, edges_ref, conv_in, conv_out, wq, wk, wv, sems,
+    gc, mq, mk, taps, bias, edges_ref, conv_in, conv_out, wq, wk, sems,
 ):
-    wide = HEADS * HD
-    keys, values = slice(0, wide), slice(wide, 2 * wide)
     parts = (
         (edges_hbm, edges_ref),
         (conv_in_hbm, conv_in),
         (wq_hbm, wq),
-        (wkv_hbm.at[:, keys], wk),
+        (wkv_hbm.at[:, : HEADS * HD], wk),
         (conv_out_hbm, conv_out),
-        (wkv_hbm.at[:, values], wv),
     )
     copies = [pltpu.make_async_copy(src, dst, sems.at[n]) for n, (src, dst) in enumerate(parts)]
     for copy in copies:
@@ -83,16 +80,13 @@
     copies[2].wait()
     mq[...] = jnp.dot(wcb, wq[...], preferred_element_type=jnp.float32)
     copies[3].wait()
-    mkv[:, keys] = jnp.dot(wcb, wk[...], preferred_element_type=jnp.float32)
+    mk[...] = jnp.dot(wcb, wk[...], preferred_element_type=jnp.float32)
     copies[4].wait()
-    taps = flat_taps(conv_out)
-    wt[...] = taps.astype(jnp.bfloat16)
+    wt = flat_taps(conv_out)
     pad = jnp.zeros((DEEP - 3 * TAPS, wc.shape[1]), jnp.float32)
     wc3 = jnp.concatenate([wc, wc, wc, pad], axis=0).astype(jnp.bfloat16)
-    both = jnp.concatenate([wc, taps], axis=0).astype(jnp.bfloat16)
-    gc[...] = split_lanes(nt_dot(both, wc3))
-    copies[5].wait()
-    mkv[:, values] = jnp.dot(wcb, wv[...], preferred_element_type=jnp.float32)
+    taps[...] = jnp.concatenate([wc, wt], axis=0).astype(jnp.bfloat16)
+    gc[...] = split_lanes(nt_dot(taps[...], wc3))
 
 
 def nt_dot_parts(a, b):
@@ -102,24 +96,29 @@
     return nt_dot(left, right)
 
 
-def head_products(mq_ref, mkv_ref, nt, aq, bb):
+def head_pair(g):
     lane = lax.broadcasted_iota(jnp.int32, (TAPS, 2 * HD), 1)
     even = (lane < HD).astype(jnp.float32)
-    odd = 1.0 - even
-    hpad = jnp.zeros((DEEP - 3 * TAPS, 2 * HD), jnp.float32)
+    return slice(g * 2 * HD, (g + 1) * 2 * HD), even, 1.0 - even
+
+
+def score_products(mq, mk, aq):
+    pad = jnp.zeros((DEEP - 3 * TAPS, 2 * HD), jnp.float32)
     scale = math.log2(math.e) / math.sqrt(HD)
     for g in range(HEADS // 2):
-        cols = slice(g * 2 * HD, (g + 1) * 2 * HD)
-        vcols = slice(HEADS * HD + g * 2 * HD, HEADS * HD + (g + 1) * 2 * HD)
-        q = mq_ref[:, cols] * scale
-        k = mkv_ref[:, cols]
-        v = mkv_ref[:, vcols]
-        q3 = jnp.concatenate([q, q, q, hpad], axis=0)
+        cols, even, odd = head_pair(g)
+        q = mq[:, cols] * scale
+        k = mk[:, cols]
+        q3 = jnp.concatenate([q, q, q, pad], axis=0)
         k2 = jnp.concatenate([k * even, k * odd], axis=0)
+        aq[(g + 1) * 2 * TAPS : (g + 2) * 2 * TAPS, :] = split_lanes(nt_dot_parts(k2, q3))
+
+
+def value_products(mv, nt, bb):
+    for g in range(HEADS // 2):
+        cols, even, odd = head_pair(g)
+        v = mv[:, cols]
         v2 = jnp.concatenate([v * even, v * odd], axis=0)
-        aq[(g + 1) * 2 * TAPS : (g + 2) * 2 * TAPS, :] = split_lanes(
-            nt_dot_parts(k2, q3)
-        )
         b = nt_dot_parts(nt[:, cols], v2)
         bh = high(b)
         bb[g] = jnp.concatenate([bh, b - bh], axis=0).astype(jnp.bfloat16)
@@ -188,11 +187,18 @@
 
 
 def own_kernel(
-    rows, gc, mq, mkv, wt, wo, bias, qr, skip, bb, top, acc, p3, aq, kl, vl, sc, ex
+    rows, gc, mq, mk, taps, bias, wkv_hbm, wo_hbm,
+    qr, skip, bb, top, acc, p3, aq, kl, vl, sc, ex, wv, wo, sems,
 ):
     local, _, _, w = rows.shape
+    copies = [
+        pltpu.make_async_copy(wkv_hbm.at[:, HEADS * HD :], wv, sems.at[0]),
+        pltpu.make_async_copy(wo_hbm, wo, sems.at[1]),
+    ]
+    for copy in copies:
+        copy.start()
     aq[0 : 2 * TAPS, :] = gc[...]
-    head_products(mq, mkv, nt_dot(wt[...], wo[...]), aq, bb)
+    score_products(mq, mk, aq)
     for v in range(local):
         p3[:, v * w : (v + 1) * w] = patch_stack([rows[v, i] for i in range(3)])
     asked = jnp.dot(aq[...], p3[...], preferred_element_type=jnp.float32)
@@ -232,6 +238,10 @@
         )
         acc[v, 0:TAPS, :] = gathered[0:TAPS] + gathered[TAPS + 8 :]
         acc[v, TAPS:, :] = gathered[TAPS : TAPS + 8]
+    copies[0].wait()
+    mv = jnp.dot(taps[0:TAPS, :], wv[...], preferred_element_type=jnp.float32)
+    copies[1].wait()
+    value_products(mv, nt_dot(taps[TAPS:, :], wo[...]), bb)
 
 
 def mix_kernel(
@@ -327,22 +337,22 @@
         query_weight,
         key_value_weight,
     )
-    gc, mq, mkv, wt, bias = pl.pallas_call(
+    gc, mq, mk, taps, bias = pl.pallas_call(
         functools.partial(prepare_kernel, views),
         in_specs=[far] * len(loaded),
         out_specs=[whole] * 5,
         out_shape=[
             pltpu.VMEM((2 * TAPS, DEEP), bf16),
             pltpu.VMEM((TAPS, HEADS * HD), f32),
-            pltpu.VMEM((TAPS, 2 * HEADS * HD), f32),
-            pltpu.VMEM((TAPS, out_weight.shape[1]), bf16),
+            pltpu.VMEM((TAPS, HEADS * HD), f32),
+            pltpu.VMEM((2 * TAPS, out_weight.shape[1]), bf16),
             pltpu.VMEM((local, span, w), f32),
         ],
         scratch_shapes=[
             pltpu.VMEM(a.shape, a.dtype)
-            for a in (*loaded[:4], query_weight, query_weight)
+            for a in (*loaded[:4], query_weight)
         ]
-        + [pltpu.SemaphoreType.DMA((6,))],
+        + [pltpu.SemaphoreType.DMA((5,))],
         compiler_params=pltpu.CompilerParams(vmem_limit_bytes=60 * MIB),
         cost_estimate=pl.CostEstimate(
             flops=3_000_000_000, bytes_accessed=5_000_000, transcendentals=0
@@ -354,7 +364,7 @@
         pack_kernel,
         in_specs=[whole] * 3 + [pl.BlockSpec(memory_space=pl.ANY)],
         out_specs=[whole] * 3,
-        out_shape=[jax.ShapeDtypeStruct((local, 3, channels, w), bf16), part, part],
+        out_shape=[pltpu.VMEM((local, 3, channels, w), bf16), part, part],
         compiler_params=pltpu.CompilerParams(vmem_limit_bytes=4 * MIB),
     )(x, row_first, row_second, bias)
     prev = lax.ppermute(tail, "view", [(i, (i + 1) % views) for i in range(views)])
@@ -366,14 +376,14 @@
     ]
     qr, skip, bb, top, acc = pl.pallas_call(
         own_kernel,
-        in_specs=[whole] * 7,
+        in_specs=[whole] * 6 + [far] * 2,
         out_specs=[whole] * 5,
         out_shape=[
-            jax.ShapeDtypeStruct((local, DEEP, HEADS * w), bf16),
-            jax.ShapeDtypeStruct((TAPS, local * w), f32),
-            jax.ShapeDtypeStruct((HEADS // 2, 2 * TAPS, 2 * TAPS), bf16),
-            jax.ShapeDtypeStruct((local, HEADS * w), f32),
-            jax.ShapeDtypeStruct((local, TAPS + 8, HEADS * w), f32),
+            pltpu.VMEM((local, DEEP, HEADS * w), bf16),
+            pltpu.VMEM((TAPS, local * w), f32),
+            pltpu.VMEM((HEADS // 2, 2 * TAPS, 2 * TAPS), bf16),
+            pltpu.VMEM((local, HEADS * w), f32),
+            pltpu.VMEM((local, TAPS + 8, HEADS * w), f32),
         ],
         scratch_shapes=[
             pltpu.VMEM((DEEP, local * w), bf16),
@@ -381,12 +391,15 @@
             *keys_scratch,
             pltpu.VMEM((2, local * w, HEADS * w), f32),
             pltpu.VMEM((2, local * w, HEADS * w), bf16),
+            pltpu.VMEM(query_weight.shape, bf16),
+            pltpu.VMEM(out_weight.shape, bf16),
+            pltpu.SemaphoreType.DMA((2,)),
         ],
-        compiler_params=pltpu.CompilerParams(vmem_limit_bytes=24 * MIB),
+        compiler_params=pltpu.CompilerParams(vmem_limit_bytes=49 * MIB),
         cost_estimate=pl.CostEstimate(
             flops=4_000_000_000, bytes_accessed=1_000_000, transcendentals=2_000_000
         ),
-    )(rows, gc, mq, mkv, wt, out_weight, bias)
+    )(rows, gc, mq, mk, taps, bias, key_value_weight, out_weight)
 
     plane = jax.ShapeDtypeStruct((local, channels, w), f32)
     mine, late, early = pl.pallas_call(

time: 40.5 us -> 40.3 us (level)
  waiting for transfers between devices: 2.18 us -> 1.44 us
    pallas_call x1, Pallas kernels: 3.74 us -> 4.43 us  [on_device(): pl.pallas_call(own_kernel, in_specs=[whole] * 6 + [far] * 2, out_specs=[w...]
    pallas_call x1, Pallas kernels: 2.89 us -> 2.3 us  [on_device(): pl.pallas_call(functools.partial(prepare_kernel, views), in_specs=[far] *...]
  transfers between devices with their start and end apart: 6 -> 6, of which waited for: 2 -> 1; matrix products, arithmetic and copies ran while one was open for 0% -> 0% of each run, Pallas kernels for 16% -> 17%
where the time goes in v4:
time: 40.3 us; the launch traced here: 40 us
  starting transfers between devices  28.9 us (72%)
  Pallas kernels  8.94 us (22%)
  waiting for transfers between devices  1.44 us (4%)
  other arithmetic  0.61 us (2%)
    ppermute x1, starting transfers between devices, on_device(): lax.ppermute(tail, 'view', [(i, (i + 1) % views) for i in range(views)])  9.1 us
    ppermute x1, starting transfers between devices, on_device(): row_second = lax.ppermute(x, 'space', pairs(space, 1))  6.23 us
    ppermute x1, starting transfers between devices, on_device(): lax.ppermute(lead, 'view', [((i + 1) % views, i) for i in range(views)])  5.36 us
    pallas_call x1, Pallas kernels, on_device(): pl.pallas_call(own_kernel, in_specs=[whole] * 6 + [far] * 2, out_specs=[w...  4.43 us
    ppermute x1, starting transfers between devices, on_device(): row_second = lax.ppermute(late, 'space', pairs(space, 1))  4.39 us
    pallas_call x1, Pallas kernels, on_device(): pl.pallas_call(functools.partial(prepare_kernel, views), in_specs=[far] *...  2.3 us
    pallas_call x1, Pallas kernels, on_device(): pl.pallas_call(mix_kernel, in_specs=[whole] * 8, out_specs=[whole] * 3, o...  2.18 us
    ppermute x1, starting transfers between devices, on_device(): row_first = lax.ppermute(early, 'space', pairs(space, 0))  1.92 us
  transfers between devices with their start and end apart: 6, of which 1 were waited for; matrix products, arithmetic and copies ran while one was open for 0% of the time, Pallas kernels for 17%

profile of v4, /device:TPU:6, one launch (start us, length us, event | category | flops | bytes accessed | tf_op | source)
XLA Modules:
  0.0 40.0 jit_solution(16738481143131022181)
XLA Ops:
  0.0 6.2 %collective-permute-start.1 = (bf16[4,8,128]{2,1,0:T(8,128)(2,1)}, bf16[4,8,128]{2,1,0:T(8,128)(2,1)S(1)}, u32[]{:S(2)}, u32[]{:S(2)}) collective-permute-start(bf16[4,8,128]{2,1,0:T(8,128)(2,1)} %bitcast.5), channel_id=1, source_target_pairs={{1,2},{2,1},{3,4},{4,3},{5,6},{6,5},{7,8},{8,7},{9,10},{10,9},{11,... | collective-permute-start | bytes 24584 | tf_op jit(solution)/shard_map/ppermute | solution.py:328
  6.2 1.9 %collective-permute-start = (bf16[4,8,128]{2,1,0:T(8,128)(2,1)}, bf16[4,8,128]{2,1,0:T(8,128)(2,1)S(1)}, u32[]{:S(2)}, u32[]{:S(2)}) collective-permute-start(bf16[4,8,128]{2,1,0:T(8,128)(2,1)} %bitcast.6), channel_id=1, source_target_pairs={{0,1},{1,0},{2,3},{3,2},{4,5},{5,4},{6,7},{7,6},{8,9},{9,8},{10,11... | collective-permute-start | bytes 24584 | tf_op jit(solution)/shard_map/ppermute | solution.py:327
  8.2 0.0 copy-start
  8.2 2.3 %shard_map.73 = (bf16[144,256]{1,0:T(8,128)(2,1)S(1)}, f32[72,512]{1,0:T(8,128)S(1)}, f32[72,512]{1,0:T(8,128)S(1)}, bf16[144,1024]{1,0:T(8,128)(2,1)S(1)}, f32[4,8,128]{2,1,0:T(8,128)S(1)}) custom-call(s32[2,96]{1,0:T(2,128)} %bitcast.8, bf16[3,3,8,1024]{3,2,1,0:T(8,128)(2,1)} %conv_in_hbm.1, bf16[3,3,8,1024]{3,2,1,0:T(8,128)(2,1)} %conv_out_hbm.1, ...), custom_call_target="tpu_custom_call" | custom-call | flops 3000000000 | bytes 5000000 | tf_op jit(solution)/shard_map/pallas_call | solution.py:340
  10.5 0.0 collective-permute-done.1.second
  10.5 0.0 collective-permute-done.first
  10.5 0.0 copy-done
  10.5 9.1 %collective-permute-start.2 = (bf16[2,3,8,128]{3,2,1,0:T(8,128)(2,1)S(1)}, bf16[2,3,8,128]{3,2,1,0:T(8,128)(2,1)S(1)}, u32[]{:S(2)}, u32[]{:S(2)}) collective-permute-start(bf16[2,3,8,128]{3,2,1,0:T(8,128)(2,1)S(1)} %get-tuple-element.22), channel_id=1, source_target_pairs={{0,32},{32,64},{64,96},{96,128},{128,160},{160,192},{192,224},{224... | collective-permute-start | bytes 36872 | tf_op jit(solution)/shard_map/ppermute | solution.py:370
  19.7 5.4 %collective-permute-start.3 = (bf16[2,3,8,128]{3,2,1,0:T(8,128)(2,1)S(1)}, bf16[2,3,8,128]{3,2,1,0:T(8,128)(2,1)S(1)}, u32[]{:S(2)}, u32[]{:S(2)}) collective-permute-start(bf16[2,3,8,128]{3,2,1,0:T(8,128)(2,1)S(1)} %get-tuple-element.23), channel_id=1, source_target_pairs={{32,0},{64,32},{96,64},{128,96},{160,128},{192,160},{224,192},{256... | collective-permute-start | bytes 36872 | tf_op jit(solution)/shard_map/ppermute | solution.py:371
  25.0 4.4 %shard_map.75 = (bf16[4,256,1024]{2,1,0:T(8,128)(2,1)S(1)}, f32[72,512]{1,0:T(8,128)S(1)}, bf16[4,144,144]{2,1,0:T(8,128)(2,1)S(1)}, f32[4,1024]{1,0:T(4,128)S(1)}, f32[4,80,1024]{2,1,0:T(8,128)S(1)}) custom-call(bf16[4,3,8,128]{3,2,1,0:T(8,128)(2,1)S(1)} %get-tuple-element.25.rows, bf16[144,256]{1,0:T(8,128)(2,1)S(1)} %get-tuple-element.24.gc, ...), custom_call_target="tpu_custom_call" | custom-call | flops 4000000000 | bytes 1000000 | tf_op jit(solution)/shard_map/pallas_call | solution.py:377
  29.5 0.0 collective-permute-done.2.prev
  29.5 0.0 collective-permute-done.3.nxt
  29.5 2.2 %shard_map.76 = (f32[4,8,128]{2,1,0:T(8,128)S(1)}, f32[4,8,128]{2,1,0:T(8,128)S(1)}, f32[4,8,128]{2,1,0:T(8,128)S(1)}) custom-call(bf16[2,3,8,128]{3,2,1,0:T(8,128)(2,1)S(1)} %collective-permute-done.2.prev, bf16[2,3,8,128]{3,2,1,0:T(8,128)(2,1)S(1)} %collective-permute-done.3.nxt, bf16[144,256]{1,0:T(8,128)(2,1)S(1)} %get-tuple-element.24.gc, ...), custom_call_target="tpu_custom_call" | custom-call | flops 3000000000 | bytes 1000000 | tf_op jit(solution)/shard_map/pallas_call | solution.py:405
  31.7 4.4 %collective-permute-start.4 = (f32[4,8,128]{2,1,0:T(8,128)S(1)}, f32[4,8,128]{2,1,0:T(8,128)S(1)}, u32[]{:S(2)}, u32[]{:S(2)}) collective-permute-start(f32[4,8,128]{2,1,0:T(8,128)S(1)} %get-tuple-element.34), channel_id=1, source_target_pairs={{1,2},{2,1},{3,4},{4,3},{5,6},{6,5},{7,8},{8,7},{9,10},{10,9},{11,... | collective-permute-start | bytes 49160 | tf_op jit(solution)/shard_map/ppermute | solution.py:424
  36.1 1.9 %collective-permute-start.5 = (f32[4,8,128]{2,1,0:T(8,128)S(1)}, f32[4,8,128]{2,1,0:T(8,128)S(1)}, u32[]{:S(2)}, u32[]{:S(2)}) collective-permute-start(f32[4,8,128]{2,1,0:T(8,128)S(1)} %get-tuple-element.36), channel_id=1, source_target_pairs={{0,1},{1,0},{2,3},{3,2},{4,5},{5,4},{6,7},{7,6},{8,9},{9,8},{10,11... | collective-permute-start | bytes 49160 | tf_op jit(solution)/shard_map/ppermute | solution.py:425
  38.0 1.4 %collective-permute-done.4 = f32[4,8,128]{2,1,0:T(8,128)S(1)} collective-permute-done((f32[4,8,128]{2,1,0:T(8,128)S(1)}, f32[4,8,128]{2,1,0:T(8,128)S(1)}, u32[]{:S(2)}, u32[]{:S(2)}) %collective-permute-start.4) | collective-permute-done | bytes 16416 | tf_op jit(solution)/shard_map/ppermute | solution.py:424
  39.4 0.0 collective-permute-done.5
  39.4 0.6 %add_add_fusion = f32[4,8,128]{2,1,0:T(8,128)} fusion(f32[4,8,128]{2,1,0:T(8,128)S(1)} %collective-permute-done.5, f32[4,8,128]{2,1,0:T(8,128)S(1)} %collective-permute-done.4, f32[4,8,128]{2,1,0:T(8,128)S(1)} %get-tuple-element.35), kind=kLoop, calls=%fused_computation | loop fusion | flops 8192 | bytes 65536 | tf_op jit(solution)/shard_map/add | solution.py:426
  (1 shorter events, 0.0 us)
Async XLA Ops:
  0.0 10.5 %collective-permute-start.1 = (bf16[4,8,128]{2,1,0:T(8,128)(2,1)}, bf16[4,8,128]{2,1,0:T(8,128)(2,1)S(1)}, u32[]{:S(2)}, u32[]{:S(2)}) collective-permute-start(bf16[4,8,128]{2,1,0:T(8,128)(2,1)} %bitcast.5), channel_id=1, source_target_pairs={{1,2},{2,1},{3,4},{4,3},{5,6},{6,5},{7,8},{8,7},{9,10},{10,9},{11,... | collective-permute-start | bytes 24584 | tf_op jit(solution)/shard_map/ppermute | solution.py:328
  6.2 4.3 %collective-permute-start = (bf16[4,8,128]{2,1,0:T(8,128)(2,1)}, bf16[4,8,128]{2,1,0:T(8,128)(2,1)S(1)}, u32[]{:S(2)}, u32[]{:S(2)}) collective-permute-start(bf16[4,8,128]{2,1,0:T(8,128)(2,1)} %bitcast.6), channel_id=1, source_target_pairs={{0,1},{1,0},{2,3},{3,2},{4,5},{5,4},{6,7},{7,6},{8,9},{9,8},{10,11... | collective-permute-start | bytes 24584 | tf_op jit(solution)/shard_map/ppermute | solution.py:327
  8.2 2.3 %copy-start = (bf16[4,8,1,128]{3,1,2,0:T(8,128)(2,1)S(1)}, bf16[4,8,1,128]{3,1,2,0:T(8,128)(2,1)}, u32[]{:S(2)}) copy-start(bf16[4,8,1,128]{3,1,2,0:T(8,128)(2,1)} %param.7) | copy-start | bytes 24580
  10.5 18.9 %collective-permute-start.2 = (bf16[2,3,8,128]{3,2,1,0:T(8,128)(2,1)S(1)}, bf16[2,3,8,128]{3,2,1,0:T(8,128)(2,1)S(1)}, u32[]{:S(2)}, u32[]{:S(2)}) collective-permute-start(bf16[2,3,8,128]{3,2,1,0:T(8,128)(2,1)S(1)} %get-tuple-element.22), channel_id=1, source_target_pairs={{0,32},{32,64},{64,96},{96,128},{128,160},{160,192},{192,224},{224... | collective-permute-start | bytes 36872 | tf_op jit(solution)/shard_map/ppermute | solution.py:370
  19.7 9.8 %collective-permute-start.3 = (bf16[2,3,8,128]{3,2,1,0:T(8,128)(2,1)S(1)}, bf16[2,3,8,128]{3,2,1,0:T(8,128)(2,1)S(1)}, u32[]{:S(2)}, u32[]{:S(2)}) collective-permute-start(bf16[2,3,8,128]{3,2,1,0:T(8,128)(2,1)S(1)} %get-tuple-element.23), channel_id=1, source_target_pairs={{32,0},{64,32},{96,64},{128,96},{160,128},{192,160},{224,192},{256... | collective-permute-start | bytes 36872 | tf_op jit(solution)/shard_map/ppermute | solution.py:371
  31.7 7.8 %collective-permute-start.4 = (f32[4,8,128]{2,1,0:T(8,128)S(1)}, f32[4,8,128]{2,1,0:T(8,128)S(1)}, u32[]{:S(2)}, u32[]{:S(2)}) collective-permute-start(f32[4,8,128]{2,1,0:T(8,128)S(1)} %get-tuple-element.34), channel_id=1, source_target_pairs={{1,2},{2,1},{3,4},{4,3},{5,6},{6,5},{7,8},{8,7},{9,10},{10,9},{11,... | collective-permute-start | bytes 49160 | tf_op jit(solution)/shard_map/ppermute | solution.py:424
  36.1 3.4 %collective-permute-start.5 = (f32[4,8,128]{2,1,0:T(8,128)S(1)}, f32[4,8,128]{2,1,0:T(8,128)S(1)}, u32[]{:S(2)}, u32[]{:S(2)}) collective-permute-start(f32[4,8,128]{2,1,0:T(8,128)S(1)} %get-tuple-element.36), channel_id=1, source_target_pairs={{0,1},{1,0},{2,3},{3,2},{4,5},{5,4},{6,7},{7,6},{8,9},{9,8},{10,11... | collective-permute-start | bytes 49160 | tf_op jit(solution)/shard_map/ppermute | solution.py:425

commit v5 on v4

--- a/solution.py
+++ b/solution.py
@@ -226,6 +226,11 @@
     for v in range(local):
         if v + 1 < local:
             scored(v + 1)
+        if v == local // 2:
+            copies[0].wait()
+            copies[1].wait()
+            mv = jnp.dot(taps[0:TAPS, :], wv[...], preferred_element_type=jnp.float32)
+            value_products(mv, nt_dot(taps[TAPS:, :], wo[...]), bb)
         lo, hi = spans[v]
         for head in range(HEADS):
             cols = slice(head * w, (head + 1) * w)
@@ -238,17 +243,13 @@
         )
         acc[v, 0:TAPS, :] = gathered[0:TAPS] + gathered[TAPS + 8 :]
         acc[v, TAPS:, :] = gathered[TAPS : TAPS + 8]
-    copies[0].wait()
-    mv = jnp.dot(taps[0:TAPS, :], wv[...], preferred_element_type=jnp.float32)
-    copies[1].wait()
-    value_products(mv, nt_dot(taps[TAPS:, :], wo[...]), bb)
-
 
 def mix_kernel(
     prev, nxt, gc, bb, qr, skip, top, acc,
-    mine, late, early, p3, kl, vl, uh, ul, sc, ex,
+    mine, late, early, p3, kl, vl, sc, ex,
 ):
     local, _, w = mine.shape
+    even = is_even("space")
     for u in range(REACH):
         p3[:, u * w : (u + 1) * w] = patch_stack([prev[u, i] for i in range(3)])
         p3[:, (REACH + u) * w : (REACH + u + 1) * w] = patch_stack([nxt[u, i] for i in range(3)])
@@ -265,7 +266,8 @@
         sc[v, 0 : hi - lo, :] = jnp.dot(
             kl[lo:hi, :], qr[v], preferred_element_type=jnp.float32
         )
-    for v, (lo, hi) in enumerate(spans):
+    for v in sorted(range(local), key=lambda v: spans[v][0] - spans[v][1]):
+        lo, hi = spans[v]
         fades = []
         for head in range(HEADS):
             cols = slice(head * w, (head + 1) * w)
@@ -281,22 +283,18 @@
         weight = gathered[TAPS : TAPS + 1] + acc[v, TAPS : TAPS + 1, :] * fade
         mixed = gathered[0:TAPS] + gathered[TAPS + 8 :] + acc[v, 0:TAPS, :] * fade
         mixed = mixed * (1.0 / weight)
+        z = skip[:, v * w : (v + 1) * w]
         for g in range(HEADS // 2):
             pair = mixed[:, g * 2 * w : (g + 1) * 2 * w]
             pair = jnp.concatenate([pair[:, :w], pair[:, w:]], axis=0)
             h = pair.astype(jnp.bfloat16)
-            uh[g, :, v * w : (v + 1) * w] = h
-            ul[g, :, v * w : (v + 1) * w] = (pair - h.astype(jnp.float32)).astype(jnp.bfloat16)
-    z = skip[...]
-    for g in range(HEADS // 2):
-        y = jnp.dot(bb[g], uh[g], preferred_element_type=jnp.float32)
-        z = z + y[:TAPS] + y[TAPS:]
-        z = z + jnp.dot(bb[g, 0:TAPS, :], ul[g], preferred_element_type=jnp.float32)
-    even = is_even("space")
-    for v in range(local):
+            r = (pair - h.astype(jnp.float32)).astype(jnp.bfloat16)
+            y = jnp.dot(bb[g], h, preferred_element_type=jnp.float32)
+            z = z + y[:TAPS] + y[TAPS:]
+            z = z + jnp.dot(bb[g, 0:TAPS, :], r, preferred_element_type=jnp.float32)
         parts = []
         for i in range(3):
-            rows = z[i * 24 : (i + 1) * 24, v * w : (v + 1) * w]
+            rows = z[i * 24 : (i + 1) * 24]
             parts.append(shifted(rows[0:8], 1) + rows[8:16] + shifted(rows[16:24], -1))
         below, mine[v], above = parts
         early[v] = jnp.where(even, below, above)
@@ -410,8 +408,6 @@
         scratch_shapes=[
             pltpu.VMEM((DEEP, 2 * REACH * w), bf16),
             *keys_scratch,
-            pltpu.VMEM((HEADS // 2, 2 * TAPS, local * w), bf16),
-            pltpu.VMEM((HEADS // 2, 2 * TAPS, local * w), bf16),
             pltpu.VMEM((local, REACH * w, HEADS * w), f32),
             pltpu.VMEM((local, REACH * w, HEADS * w), bf16),
         ],

time: 40.3 us -> 40.7 us (level)
  no operation moved by 1% of the time
where the time goes in v5:
time: 40.7 us; the launch traced here: 40.4 us
  starting transfers between devices  28.9 us (71%)
  Pallas kernels  9.33 us (23%)
  waiting for transfers between devices  1.44 us (4%)
  other arithmetic  0.61 us (1%)
    ppermute x1, starting transfers between devices, on_device(): lax.ppermute(tail, 'view', [(i, (i + 1) % views) for i in range(views)])  9.1 us
    ppermute x1, starting transfers between devices, on_device(): row_second = lax.ppermute(x, 'space', pairs(space, 1))  6.23 us
    ppermute x1, starting transfers between devices, on_device(): lax.ppermute(lead, 'view', [((i + 1) % views, i) for i in range(views)])  5.36 us
    pallas_call x1, Pallas kernels, on_device(): pl.pallas_call(own_kernel, in_specs=[whole] * 6 + [far] * 2, out_specs=[w...  4.44 us
    ppermute x1, starting transfers between devices, on_device(): row_second = lax.ppermute(late, 'space', pairs(space, 1))  4.39 us
    pallas_call x1, Pallas kernels, on_device(): pl.pallas_call(mix_kernel, in_specs=[whole] * 8, out_specs=[whole] * 3, o...  2.56 us
    pallas_call x1, Pallas kernels, on_device(): pl.pallas_call(functools.partial(prepare_kernel, views), in_specs=[far] *...  2.3 us
    ppermute x1, starting transfers between devices, on_device(): row_first = lax.ppermute(early, 'space', pairs(space, 0))  1.92 us
  transfers between devices with their start and end apart: 6, of which 1 were waited for; matrix products, arithmetic and copies ran while one was open for 0% of the time, Pallas kernels for 17%

profile of v5, /device:TPU:6, one launch (start us, length us, event | category | flops | bytes accessed | tf_op | source)
XLA Modules:
  0.0 40.4 jit_solution(658303904512969968)
XLA Ops:
  0.0 6.2 %collective-permute-start.1 = (bf16[4,8,128]{2,1,0:T(8,128)(2,1)}, bf16[4,8,128]{2,1,0:T(8,128)(2,1)S(1)}, u32[]{:S(2)}, u32[]{:S(2)}) collective-permute-start(bf16[4,8,128]{2,1,0:T(8,128)(2,1)} %bitcast.5), channel_id=1, source_target_pairs={{1,2},{2,1},{3,4},{4,3},{5,6},{6,5},{7,8},{8,7},{9,10},{10,9},{11,... | collective-permute-start | bytes 24584 | tf_op jit(solution)/shard_map/ppermute | solution.py:326
  6.2 1.9 %collective-permute-start = (bf16[4,8,128]{2,1,0:T(8,128)(2,1)}, bf16[4,8,128]{2,1,0:T(8,128)(2,1)S(1)}, u32[]{:S(2)}, u32[]{:S(2)}) collective-permute-start(bf16[4,8,128]{2,1,0:T(8,128)(2,1)} %bitcast.6), channel_id=1, source_target_pairs={{0,1},{1,0},{2,3},{3,2},{4,5},{5,4},{6,7},{7,6},{8,9},{9,8},{10,11... | collective-permute-start | bytes 24584 | tf_op jit(solution)/shard_map/ppermute | solution.py:325
  8.2 0.0 copy-start
  8.2 2.3 %shard_map.73 = (bf16[144,256]{1,0:T(8,128)(2,1)S(1)}, f32[72,512]{1,0:T(8,128)S(1)}, f32[72,512]{1,0:T(8,128)S(1)}, bf16[144,1024]{1,0:T(8,128)(2,1)S(1)}, f32[4,8,128]{2,1,0:T(8,128)S(1)}) custom-call(s32[2,96]{1,0:T(2,128)} %bitcast.8, bf16[3,3,8,1024]{3,2,1,0:T(8,128)(2,1)} %conv_in_hbm.1, bf16[3,3,8,1024]{3,2,1,0:T(8,128)(2,1)} %conv_out_hbm.1, ...), custom_call_target="tpu_custom_call" | custom-call | flops 3000000000 | bytes 5000000 | tf_op jit(solution)/shard_map/pallas_call | solution.py:338
  10.5 0.0 collective-permute-done.1.second
  10.5 0.0 collective-permute-done.first
  10.5 0.0 copy-done
  10.5 9.1 %collective-permute-start.2 = (bf16[2,3,8,128]{3,2,1,0:T(8,128)(2,1)S(1)}, bf16[2,3,8,128]{3,2,1,0:T(8,128)(2,1)S(1)}, u32[]{:S(2)}, u32[]{:S(2)}) collective-permute-start(bf16[2,3,8,128]{3,2,1,0:T(8,128)(2,1)S(1)} %get-tuple-element.22), channel_id=1, source_target_pairs={{0,32},{32,64},{64,96},{96,128},{128,160},{160,192},{192,224},{224... | collective-permute-start | bytes 36872 | tf_op jit(solution)/shard_map/ppermute | solution.py:368
  19.7 5.4 %collective-permute-start.3 = (bf16[2,3,8,128]{3,2,1,0:T(8,128)(2,1)S(1)}, bf16[2,3,8,128]{3,2,1,0:T(8,128)(2,1)S(1)}, u32[]{:S(2)}, u32[]{:S(2)}) collective-permute-start(bf16[2,3,8,128]{3,2,1,0:T(8,128)(2,1)S(1)} %get-tuple-element.23), channel_id=1, source_target_pairs={{32,0},{64,32},{96,64},{128,96},{160,128},{192,160},{224,192},{256... | collective-permute-start | bytes 36872 | tf_op jit(solution)/shard_map/ppermute | solution.py:369
  25.0 4.4 %shard_map.75 = (bf16[4,256,1024]{2,1,0:T(8,128)(2,1)S(1)}, f32[72,512]{1,0:T(8,128)S(1)}, bf16[4,144,144]{2,1,0:T(8,128)(2,1)S(1)}, f32[4,1024]{1,0:T(4,128)S(1)}, f32[4,80,1024]{2,1,0:T(8,128)S(1)}) custom-call(bf16[4,3,8,128]{3,2,1,0:T(8,128)(2,1)S(1)} %get-tuple-element.25.rows, bf16[144,256]{1,0:T(8,128)(2,1)S(1)} %get-tuple-element.24.gc, ...), custom_call_target="tpu_custom_call" | custom-call | flops 4000000000 | bytes 1000000 | tf_op jit(solution)/shard_map/pallas_call | solution.py:375
  29.5 0.0 collective-permute-done.2.prev
  29.5 0.0 collective-permute-done.3.nxt
  29.5 2.6 %shard_map.76 = (f32[4,8,128]{2,1,0:T(8,128)S(1)}, f32[4,8,128]{2,1,0:T(8,128)S(1)}, f32[4,8,128]{2,1,0:T(8,128)S(1)}) custom-call(bf16[2,3,8,128]{3,2,1,0:T(8,128)(2,1)S(1)} %collective-permute-done.2.prev, bf16[2,3,8,128]{3,2,1,0:T(8,128)(2,1)S(1)} %collective-permute-done.3.nxt, bf16[144,256]{1,0:T(8,128)(2,1)S(1)} %get-tuple-element.24.gc, ...), custom_call_target="tpu_custom_call" | custom-call | flops 3000000000 | bytes 1000000 | tf_op jit(solution)/shard_map/pallas_call | solution.py:403
  32.0 4.4 %collective-permute-start.4 = (f32[4,8,128]{2,1,0:T(8,128)S(1)}, f32[4,8,128]{2,1,0:T(8,128)S(1)}, u32[]{:S(2)}, u32[]{:S(2)}) collective-permute-start(f32[4,8,128]{2,1,0:T(8,128)S(1)} %get-tuple-element.34), channel_id=1, source_target_pairs={{1,2},{2,1},{3,4},{4,3},{5,6},{6,5},{7,8},{8,7},{9,10},{10,9},{11,... | collective-permute-start | bytes 49160 | tf_op jit(solution)/shard_map/ppermute | solution.py:420
  36.4 1.9 %collective-permute-start.5 = (f32[4,8,128]{2,1,0:T(8,128)S(1)}, f32[4,8,128]{2,1,0:T(8,128)S(1)}, u32[]{:S(2)}, u32[]{:S(2)}) collective-permute-start(f32[4,8,128]{2,1,0:T(8,128)S(1)} %get-tuple-element.36), channel_id=1, source_target_pairs={{0,1},{1,0},{2,3},{3,2},{4,5},{5,4},{6,7},{7,6},{8,9},{9,8},{10,11... | collective-permute-start | bytes 49160 | tf_op jit(solution)/shard_map/ppermute | solution.py:421
  38.4 1.4 %collective-permute-done.4 = f32[4,8,128]{2,1,0:T(8,128)S(1)} collective-permute-done((f32[4,8,128]{2,1,0:T(8,128)S(1)}, f32[4,8,128]{2,1,0:T(8,128)S(1)}, u32[]{:S(2)}, u32[]{:S(2)}) %collective-permute-start.4) | collective-permute-done | bytes 16416 | tf_op jit(solution)/shard_map/ppermute | solution.py:420
  39.8 0.0 collective-permute-done.5
  39.8 0.6 %add_add_fusion = f32[4,8,128]{2,1,0:T(8,128)} fusion(f32[4,8,128]{2,1,0:T(8,128)S(1)} %collective-permute-done.5, f32[4,8,128]{2,1,0:T(8,128)S(1)} %collective-permute-done.4, f32[4,8,128]{2,1,0:T(8,128)S(1)} %get-tuple-element.35), kind=kLoop, calls=%fused_computation | loop fusion | flops 8192 | bytes 65536 | tf_op jit(solution)/shard_map/add | solution.py:422
  (1 shorter events, 0.0 us)
Async XLA Ops:
  0.0 10.5 %collective-permute-start.1 = (bf16[4,8,128]{2,1,0:T(8,128)(2,1)}, bf16[4,8,128]{2,1,0:T(8,128)(2,1)S(1)}, u32[]{:S(2)}, u32[]{:S(2)}) collective-permute-start(bf16[4,8,128]{2,1,0:T(8,128)(2,1)} %bitcast.5), channel_id=1, source_target_pairs={{1,2},{2,1},{3,4},{4,3},{5,6},{6,5},{7,8},{8,7},{9,10},{10,9},{11,... | collective-permute-start | bytes 24584 | tf_op jit(solution)/shard_map/ppermute | solution.py:326
  6.2 4.3 %collective-permute-start = (bf16[4,8,128]{2,1,0:T(8,128)(2,1)}, bf16[4,8,128]{2,1,0:T(8,128)(2,1)S(1)}, u32[]{:S(2)}, u32[]{:S(2)}) collective-permute-start(bf16[4,8,128]{2,1,0:T(8,128)(2,1)} %bitcast.6), channel_id=1, source_target_pairs={{0,1},{1,0},{2,3},{3,2},{4,5},{5,4},{6,7},{7,6},{8,9},{9,8},{10,11... | collective-permute-start | bytes 24584 | tf_op jit(solution)/shard_map/ppermute | solution.py:325
  8.2 2.3 %copy-start = (bf16[4,8,1,128]{3,1,2,0:T(8,128)(2,1)S(1)}, bf16[4,8,1,128]{3,1,2,0:T(8,128)(2,1)}, u32[]{:S(2)}) copy-start(bf16[4,8,1,128]{3,1,2,0:T(8,128)(2,1)} %param.7) | copy-start | bytes 24580
  10.5 18.9 %collective-permute-start.2 = (bf16[2,3,8,128]{3,2,1,0:T(8,128)(2,1)S(1)}, bf16[2,3,8,128]{3,2,1,0:T(8,128)(2,1)S(1)}, u32[]{:S(2)}, u32[]{:S(2)}) collective-permute-start(bf16[2,3,8,128]{3,2,1,0:T(8,128)(2,1)S(1)} %get-tuple-element.22), channel_id=1, source_target_pairs={{0,32},{32,64},{64,96},{96,128},{128,160},{160,192},{192,224},{224... | collective-permute-start | bytes 36872 | tf_op jit(solution)/shard_map/ppermute | solution.py:368
  19.7 9.8 %collective-permute-start.3 = (bf16[2,3,8,128]{3,2,1,0:T(8,128)(2,1)S(1)}, bf16[2,3,8,128]{3,2,1,0:T(8,128)(2,1)S(1)}, u32[]{:S(2)}, u32[]{:S(2)}) collective-permute-start(bf16[2,3,8,128]{3,2,1,0:T(8,128)(2,1)S(1)} %get-tuple-element.23), channel_id=1, source_target_pairs={{32,0},{64,32},{96,64},{128,96},{160,128},{192,160},{224,192},{256... | collective-permute-start | bytes 36872 | tf_op jit(solution)/shard_map/ppermute | solution.py:369
  32.0 7.8 %collective-permute-start.4 = (f32[4,8,128]{2,1,0:T(8,128)S(1)}, f32[4,8,128]{2,1,0:T(8,128)S(1)}, u32[]{:S(2)}, u32[]{:S(2)}) collective-permute-start(f32[4,8,128]{2,1,0:T(8,128)S(1)} %get-tuple-element.34), channel_id=1, source_target_pairs={{1,2},{2,1},{3,4},{4,3},{5,6},{6,5},{7,8},{8,7},{9,10},{10,9},{11,... | collective-permute-start | bytes 49160 | tf_op jit(solution)/shard_map/ppermute | solution.py:420
  36.4 3.4 %collective-permute-start.5 = (f32[4,8,128]{2,1,0:T(8,128)S(1)}, f32[4,8,128]{2,1,0:T(8,128)S(1)}, u32[]{:S(2)}, u32[]{:S(2)}) collective-permute-start(f32[4,8,128]{2,1,0:T(8,128)S(1)} %get-tuple-element.36), channel_id=1, source_target_pairs={{0,1},{1,0},{2,3},{3,2},{4,5},{5,4},{6,7},{7,6},{8,9},{9,8},{10,11... | collective-permute-start | bytes 49160 | tf_op jit(solution)/shard_map/ppermute | solution.py:421

commit v6 on v3

--- a/solution.py
+++ b/solution.py
@@ -102,24 +102,33 @@
     return nt_dot(left, right)
 
 
-def head_products(mq_ref, mkv_ref, nt, aq, bb):
+def head_pair(g):
     lane = lax.broadcasted_iota(jnp.int32, (TAPS, 2 * HD), 1)
     even = (lane < HD).astype(jnp.float32)
-    odd = 1.0 - even
-    hpad = jnp.zeros((DEEP - 3 * TAPS, 2 * HD), jnp.float32)
+    return slice(g * 2 * HD, (g + 1) * 2 * HD), even, 1.0 - even
+
+
+def score_products(mq, mk, aq):
     scale = math.log2(math.e) / math.sqrt(HD)
+    lane = lax.broadcasted_iota(jnp.int32, (2 * TAPS, 2 * TAPS), 1)
     for g in range(HEADS // 2):
-        cols = slice(g * 2 * HD, (g + 1) * 2 * HD)
-        vcols = slice(HEADS * HD + g * 2 * HD, HEADS * HD + (g + 1) * 2 * HD)
-        q = mq_ref[:, cols] * scale
-        k = mkv_ref[:, cols]
-        v = mkv_ref[:, vcols]
-        q3 = jnp.concatenate([q, q, q, hpad], axis=0)
+        cols, even, odd = head_pair(g)
+        q = mq[:, cols] * scale
+        k = mk[:, cols]
+        q2 = jnp.concatenate([q, q], axis=0)
         k2 = jnp.concatenate([k * even, k * odd], axis=0)
+        a = nt_dot_parts(k2, q2)
+        ah = high(a)
+        aq[g * 2 * TAPS : (g + 1) * 2 * TAPS, :] = jnp.where(lane < TAPS, ah, a - ah).astype(
+            jnp.bfloat16
+        )
+
+
+def value_products(mkv, nt, bb):
+    for g in range(HEADS // 2):
+        cols, even, odd = head_pair(g)
+        v = mkv[:, cols.start + HEADS * HD : cols.stop + HEADS * HD]
         v2 = jnp.concatenate([v * even, v * odd], axis=0)
-        aq[(g + 1) * 2 * TAPS : (g + 2) * 2 * TAPS, :] = split_lanes(
-            nt_dot_parts(k2, q3)
-        )
         b = nt_dot_parts(nt[:, cols], v2)
         bh = high(b)
         bb[g] = jnp.concatenate([bh, b - bh], axis=0).astype(jnp.bfloat16)
@@ -188,21 +197,24 @@
 
 
 def own_kernel(
-    rows, gc, mq, mkv, wt, wo, bias, qr, skip, bb, top, acc, p3, aq, kl, vl, sc, ex
+    rows, gc, mq, mkv, wt, bias, wo_hbm,
+    qr, skip, bb, top, acc, p3, aq, kl, vl, sc, ex, wo, sem,
 ):
     local, _, _, w = rows.shape
-    aq[0 : 2 * TAPS, :] = gc[...]
-    head_products(mq, mkv, nt_dot(wt[...], wo[...]), aq, bb)
+    copy = pltpu.make_async_copy(wo_hbm, wo, sem)
+    copy.start()
+    score_products(mq, mkv, aq)
     for v in range(local):
         p3[:, v * w : (v + 1) * w] = patch_stack([rows[v, i] for i in range(3)])
-    asked = jnp.dot(aq[...], p3[...], preferred_element_type=jnp.float32)
+    base = jnp.dot(gc[...], p3[...], preferred_element_type=jnp.float32)
+    asked = jnp.dot(aq[...], p3[0 : 2 * TAPS, :], preferred_element_type=jnp.float32)
     patches = p3[0:TAPS, :].astype(jnp.float32)
-    rate = token_rate(asked[0:TAPS], patches)
-    skip[...] = asked[TAPS : 2 * TAPS]
+    rate = token_rate(base[0:TAPS], patches)
+    skip[...] = base[TAPS:]
     store_keys(patches * rate, range(REACH, REACH + local), kl, vl)
     for v in range(local):
         for head in range(HEADS):
-            q = asked[(head + 2) * TAPS : (head + 3) * TAPS, v * w : (v + 1) * w]
+            q = asked[head * TAPS : (head + 1) * TAPS, v * w : (v + 1) * w]
             q = q * rate[:, v * w : (v + 1) * w]
             h = high(q)
             qr[v, :, head * w : (head + 1) * w] = jnp.concatenate(
@@ -226,12 +238,14 @@
             scores = sc[v % 2, 0 : hi - lo, cols]
             largest = jnp.max(scores, axis=0, keepdims=True)
             top[v : v + 1, cols] = largest
-            ex[v % 2, 0 : hi - lo, cols] = jnp.exp2(scores - largest).astype(jnp.bfloat16)
+            ex[v % 2, 0 : hi - lo, cols] = jnp.exp2((scores - largest).astype(jnp.bfloat16))
         gathered = jnp.dot(
             vl[:, lo:hi], ex[v % 2, 0 : hi - lo, :], preferred_element_type=jnp.float32
         )
         acc[v, 0:TAPS, :] = gathered[0:TAPS] + gathered[TAPS + 8 :]
         acc[v, TAPS:, :] = gathered[TAPS : TAPS + 8]
+    copy.wait()
+    value_products(mkv, nt_dot(wt[...], wo[...]), bb)
 
 
 def mix_kernel(
@@ -263,7 +277,7 @@
             before = top[v : v + 1, cols]
             largest = jnp.maximum(jnp.max(scores, axis=0, keepdims=True), before)
             fades.append(jnp.exp2(before - largest))
-            ex[v, 0 : hi - lo, cols] = jnp.exp2(scores - largest).astype(jnp.bfloat16)
+            ex[v, 0 : hi - lo, cols] = jnp.exp2((scores - largest).astype(jnp.bfloat16))
         fade = jnp.concatenate(fades, axis=1)
         gathered = jnp.dot(
             vl[:, lo:hi], ex[v, 0 : hi - lo, :], preferred_element_type=jnp.float32
@@ -354,7 +368,7 @@
         pack_kernel,
         in_specs=[whole] * 3 + [pl.BlockSpec(memory_space=pl.ANY)],
         out_specs=[whole] * 3,
-        out_shape=[jax.ShapeDtypeStruct((local, 3, channels, w), bf16), part, part],
+        out_shape=[pltpu.VMEM((local, 3, channels, w), bf16), part, part],
         compiler_params=pltpu.CompilerParams(vmem_limit_bytes=4 * MIB),
     )(x, row_first, row_second, bias)
     prev = lax.ppermute(tail, "view", [(i, (i + 1) % views) for i in range(views)])
@@ -366,27 +380,29 @@
     ]
     qr, skip, bb, top, acc = pl.pallas_call(
         own_kernel,
-        in_specs=[whole] * 7,
+        in_specs=[whole] * 6 + [far],
         out_specs=[whole] * 5,
         out_shape=[
-            jax.ShapeDtypeStruct((local, DEEP, HEADS * w), bf16),
-            jax.ShapeDtypeStruct((TAPS, local * w), f32),
-            jax.ShapeDtypeStruct((HEADS // 2, 2 * TAPS, 2 * TAPS), bf16),
-            jax.ShapeDtypeStruct((local, HEADS * w), f32),
-            jax.ShapeDtypeStruct((local, TAPS + 8, HEADS * w), f32),
+            pltpu.VMEM((local, DEEP, HEADS * w), bf16),
+            pltpu.VMEM((TAPS, local * w), f32),
+            pltpu.VMEM((HEADS // 2, 2 * TAPS, 2 * TAPS), bf16),
+            pltpu.VMEM((local, HEADS * w), f32),
+            pltpu.VMEM((local, TAPS + 8, HEADS * w), f32),
         ],
         scratch_shapes=[
             pltpu.VMEM((DEEP, local * w), bf16),
-            pltpu.VMEM(((HEADS + 2) * TAPS, DEEP), bf16),
+            pltpu.VMEM((HEADS * TAPS, 2 * TAPS), bf16),
             *keys_scratch,
             pltpu.VMEM((2, local * w, HEADS * w), f32),
             pltpu.VMEM((2, local * w, HEADS * w), bf16),
+            pltpu.VMEM(out_weight.shape, bf16),
+            pltpu.SemaphoreType.DMA,
         ],
-        compiler_params=pltpu.CompilerParams(vmem_limit_bytes=24 * MIB),
+        compiler_params=pltpu.CompilerParams(vmem_limit_bytes=49 * MIB),
         cost_estimate=pl.CostEstimate(
             flops=4_000_000_000, bytes_accessed=1_000_000, transcendentals=2_000_000
         ),
-    )(rows, gc, mq, mkv, wt, out_weight, bias)
+    )(rows, gc, mq, mkv, wt, bias, out_weight)
 
     plane = jax.ShapeDtypeStruct((local, channels, w), f32)
     mine, late, early = pl.pallas_call(

time: 40.5 us -> 41.2 us (1.017)
  Pallas kernels: 8.81 us -> 9.81 us
  waiting for transfers between devices: 2.18 us -> 1.38 us
    pallas_call x1, Pallas kernels: 3.74 us -> 4.66 us  [on_device(): pl.pallas_call(own_kernel, in_specs=[whole] * 6 + [far], out_specs=[whole...]
  transfers between devices with their start and end apart: 6 -> 6, of which waited for: 2 -> 1; matrix products, arithmetic and copies ran while one was open for 0% -> 0% of each run, Pallas kernels for 16% -> 18%
where the time goes in v6:
time: 41.2 us; the launch traced here: 40.9 us
  starting transfers between devices  28.9 us (70%)
  Pallas kernels  9.81 us (24%)
  waiting for transfers between devices  1.38 us (3%)
  other arithmetic  0.61 us (1%)
    ppermute x1, starting transfers between devices, on_device(): lax.ppermute(tail, 'view', [(i, (i + 1) % views) for i in range(views)])  9.1 us
    ppermute x1, starting transfers between devices, on_device(): row_second = lax.ppermute(x, 'space', pairs(space, 1))  6.23 us
    ppermute x1, starting transfers between devices, on_device(): lax.ppermute(lead, 'view', [((i + 1) % views, i) for i in range(views)])  5.31 us
    pallas_call x1, Pallas kernels, on_device(): pl.pallas_call(own_kernel, in_specs=[whole] * 6 + [far], out_specs=[whole...  4.66 us
    ppermute x1, starting transfers between devices, on_device(): row_second = lax.ppermute(late, 'space', pairs(space, 1))  4.45 us
    pallas_call x1, Pallas kernels, on_device(): pl.pallas_call(functools.partial(prepare_kernel, views), in_specs=[far] *...  2.81 us
    pallas_call x1, Pallas kernels, on_device(): pl.pallas_call(mix_kernel, in_specs=[whole] * 8, out_specs=[whole] * 3, o...  2.3 us
    ppermute x1, starting transfers between devices, on_device(): row_first = lax.ppermute(early, 'space', pairs(space, 0))  1.92 us
  transfers between devices with their start and end apart: 6, of which 1 were waited for; matrix products, arithmetic and copies ran while one was open for 0% of the time, Pallas kernels for 18%

profile of v6, /device:TPU:6, one launch (start us, length us, event | category | flops | bytes accessed | tf_op | source)
XLA Modules:
  0.0 40.9 jit_solution(15265464835832652907)
XLA Ops:
  0.0 6.2 %collective-permute-start.1 = (bf16[4,8,128]{2,1,0:T(8,128)(2,1)}, bf16[4,8,128]{2,1,0:T(8,128)(2,1)S(1)}, u32[]{:S(2)}, u32[]{:S(2)}) collective-permute-start(bf16[4,8,128]{2,1,0:T(8,128)(2,1)} %bitcast.5), channel_id=1, source_target_pairs={{1,2},{2,1},{3,4},{4,3},{5,6},{6,5},{7,8},{8,7},{9,10},{10,9},{11,... | collective-permute-start | bytes 24584 | tf_op jit(solution)/shard_map/ppermute | solution.py:332
  6.2 1.9 %collective-permute-start = (bf16[4,8,128]{2,1,0:T(8,128)(2,1)}, bf16[4,8,128]{2,1,0:T(8,128)(2,1)S(1)}, u32[]{:S(2)}, u32[]{:S(2)}) collective-permute-start(bf16[4,8,128]{2,1,0:T(8,128)(2,1)} %bitcast.6), channel_id=1, source_target_pairs={{0,1},{1,0},{2,3},{3,2},{4,5},{5,4},{6,7},{7,6},{8,9},{9,8},{10,11... | collective-permute-start | bytes 24584 | tf_op jit(solution)/shard_map/ppermute | solution.py:331
  8.2 0.0 copy-start
  8.2 2.8 %shard_map.73 = (bf16[144,256]{1,0:T(8,128)(2,1)S(1)}, f32[72,512]{1,0:T(8,128)S(1)}, f32[72,1024]{1,0:T(8,128)S(1)}, bf16[72,1024]{1,0:T(8,128)(2,1)S(1)}, f32[4,8,128]{2,1,0:T(8,128)S(1)}) custom-call(s32[2,96]{1,0:T(2,128)} %bitcast.8, bf16[3,3,8,1024]{3,2,1,0:T(8,128)(2,1)} %conv_in_hbm.1, bf16[3,3,8,1024]{3,2,1,0:T(8,128)(2,1)} %conv_out_hbm.1, ...), custom_call_target="tpu_custom_call" | custom-call | flops 3000000000 | bytes 5000000 | tf_op jit(solution)/shard_map/pallas_call | solution.py:344
  11.0 0.0 collective-permute-done.1.second
  11.0 0.0 collective-permute-done.first
  11.0 0.0 copy-done
  11.1 9.1 %collective-permute-start.2 = (bf16[2,3,8,128]{3,2,1,0:T(8,128)(2,1)S(1)}, bf16[2,3,8,128]{3,2,1,0:T(8,128)(2,1)S(1)}, u32[]{:S(2)}, u32[]{:S(2)}) collective-permute-start(bf16[2,3,8,128]{3,2,1,0:T(8,128)(2,1)S(1)} %get-tuple-element.22), channel_id=1, source_target_pairs={{0,32},{32,64},{64,96},{96,128},{128,160},{160,192},{192,224},{224... | collective-permute-start | bytes 36872 | tf_op jit(solution)/shard_map/ppermute | solution.py:374
  20.2 5.3 %collective-permute-start.3 = (bf16[2,3,8,128]{3,2,1,0:T(8,128)(2,1)S(1)}, bf16[2,3,8,128]{3,2,1,0:T(8,128)(2,1)S(1)}, u32[]{:S(2)}, u32[]{:S(2)}) collective-permute-start(bf16[2,3,8,128]{3,2,1,0:T(8,128)(2,1)S(1)} %get-tuple-element.23), channel_id=1, source_target_pairs={{32,0},{64,32},{96,64},{128,96},{160,128},{192,160},{224,192},{256... | collective-permute-start | bytes 36872 | tf_op jit(solution)/shard_map/ppermute | solution.py:375
  25.5 4.7 %shard_map.75 = (bf16[4,256,1024]{2,1,0:T(8,128)(2,1)S(1)}, f32[72,512]{1,0:T(8,128)S(1)}, bf16[4,144,144]{2,1,0:T(8,128)(2,1)S(1)}, f32[4,1024]{1,0:T(4,128)S(1)}, f32[4,80,1024]{2,1,0:T(8,128)S(1)}) custom-call(bf16[4,3,8,128]{3,2,1,0:T(8,128)(2,1)S(1)} %get-tuple-element.25.rows, bf16[144,256]{1,0:T(8,128)(2,1)S(1)} %get-tuple-element.24.gc, ...), custom_call_target="tpu_custom_call" | custom-call | flops 4000000000 | bytes 1000000 | tf_op jit(solution)/shard_map/pallas_call | solution.py:381
  30.2 0.0 collective-permute-done.2.prev
  30.2 0.0 collective-permute-done.3.nxt
  30.2 2.3 %shard_map.76 = (f32[4,8,128]{2,1,0:T(8,128)S(1)}, f32[4,8,128]{2,1,0:T(8,128)S(1)}, f32[4,8,128]{2,1,0:T(8,128)S(1)}) custom-call(bf16[2,3,8,128]{3,2,1,0:T(8,128)(2,1)S(1)} %collective-permute-done.2.prev, bf16[2,3,8,128]{3,2,1,0:T(8,128)(2,1)S(1)} %collective-permute-done.3.nxt, bf16[144,256]{1,0:T(8,128)(2,1)S(1)} %get-tuple-element.24.gc, ...), custom_call_target="tpu_custom_call" | custom-call | flops 3000000000 | bytes 1000000 | tf_op jit(solution)/shard_map/pallas_call | solution.py:408
  32.5 4.4 %collective-permute-start.4 = (f32[4,8,128]{2,1,0:T(8,128)S(1)}, f32[4,8,128]{2,1,0:T(8,128)S(1)}, u32[]{:S(2)}, u32[]{:S(2)}) collective-permute-start(f32[4,8,128]{2,1,0:T(8,128)S(1)} %get-tuple-element.34), channel_id=1, source_target_pairs={{1,2},{2,1},{3,4},{4,3},{5,6},{6,5},{7,8},{8,7},{9,10},{10,9},{11,... | collective-permute-start | bytes 49160 | tf_op jit(solution)/shard_map/ppermute | solution.py:427
  36.9 1.9 %collective-permute-start.5 = (f32[4,8,128]{2,1,0:T(8,128)S(1)}, f32[4,8,128]{2,1,0:T(8,128)S(1)}, u32[]{:S(2)}, u32[]{:S(2)}) collective-permute-start(f32[4,8,128]{2,1,0:T(8,128)S(1)} %get-tuple-element.36), channel_id=1, source_target_pairs={{0,1},{1,0},{2,3},{3,2},{4,5},{5,4},{6,7},{7,6},{8,9},{9,8},{10,11... | collective-permute-start | bytes 49160 | tf_op jit(solution)/shard_map/ppermute | solution.py:428
  38.9 1.4 %collective-permute-done.4 = f32[4,8,128]{2,1,0:T(8,128)S(1)} collective-permute-done((f32[4,8,128]{2,1,0:T(8,128)S(1)}, f32[4,8,128]{2,1,0:T(8,128)S(1)}, u32[]{:S(2)}, u32[]{:S(2)}) %collective-permute-start.4) | collective-permute-done | bytes 16416 | tf_op jit(solution)/shard_map/ppermute | solution.py:427
  40.2 0.0 collective-permute-done.5
  40.2 0.6 %add_add_fusion = f32[4,8,128]{2,1,0:T(8,128)} fusion(f32[4,8,128]{2,1,0:T(8,128)S(1)} %collective-permute-done.5, f32[4,8,128]{2,1,0:T(8,128)S(1)} %collective-permute-done.4, f32[4,8,128]{2,1,0:T(8,128)S(1)} %get-tuple-element.35), kind=kLoop, calls=%fused_computation | loop fusion | flops 8192 | bytes 65536 | tf_op jit(solution)/shard_map/add | solution.py:429
  (1 shorter events, 0.0 us)
Async XLA Ops:
  0.0 11.0 %collective-permute-start.1 = (bf16[4,8,128]{2,1,0:T(8,128)(2,1)}, bf16[4,8,128]{2,1,0:T(8,128)(2,1)S(1)}, u32[]{:S(2)}, u32[]{:S(2)}) collective-permute-start(bf16[4,8,128]{2,1,0:T(8,128)(2,1)} %bitcast.5), channel_id=1, source_target_pairs={{1,2},{2,1},{3,4},{4,3},{5,6},{6,5},{7,8},{8,7},{9,10},{10,9},{11,... | collective-permute-start | bytes 24584 | tf_op jit(solution)/shard_map/ppermute | solution.py:332
  6.2 4.8 %collective-permute-start = (bf16[4,8,128]{2,1,0:T(8,128)(2,1)}, bf16[4,8,128]{2,1,0:T(8,128)(2,1)S(1)}, u32[]{:S(2)}, u32[]{:S(2)}) collective-permute-start(bf16[4,8,128]{2,1,0:T(8,128)(2,1)} %bitcast.6), channel_id=1, source_target_pairs={{0,1},{1,0},{2,3},{3,2},{4,5},{5,4},{6,7},{7,6},{8,9},{9,8},{10,11... | collective-permute-start | bytes 24584 | tf_op jit(solution)/shard_map/ppermute | solution.py:331
  8.2 2.9 %copy-start = (bf16[4,8,1,128]{3,1,2,0:T(8,128)(2,1)S(1)}, bf16[4,8,1,128]{3,1,2,0:T(8,128)(2,1)}, u32[]{:S(2)}) copy-start(bf16[4,8,1,128]{3,1,2,0:T(8,128)(2,1)} %param.7) | copy-start | bytes 24580
  11.1 19.1 %collective-permute-start.2 = (bf16[2,3,8,128]{3,2,1,0:T(8,128)(2,1)S(1)}, bf16[2,3,8,128]{3,2,1,0:T(8,128)(2,1)S(1)}, u32[]{:S(2)}, u32[]{:S(2)}) collective-permute-start(bf16[2,3,8,128]{3,2,1,0:T(8,128)(2,1)S(1)} %get-tuple-element.22), channel_id=1, source_target_pairs={{0,32},{32,64},{64,96},{96,128},{128,160},{160,192},{192,224},{224... | collective-permute-start | bytes 36872 | tf_op jit(solution)/shard_map/ppermute | solution.py:374
  20.2 10.0 %collective-permute-start.3 = (bf16[2,3,8,128]{3,2,1,0:T(8,128)(2,1)S(1)}, bf16[2,3,8,128]{3,2,1,0:T(8,128)(2,1)S(1)}, u32[]{:S(2)}, u32[]{:S(2)}) collective-permute-start(bf16[2,3,8,128]{3,2,1,0:T(8,128)(2,1)S(1)} %get-tuple-element.23), channel_id=1, source_target_pairs={{32,0},{64,32},{96,64},{128,96},{160,128},{192,160},{224,192},{256... | collective-permute-start | bytes 36872 | tf_op jit(solution)/shard_map/ppermute | solution.py:375
  32.5 7.8 %collective-permute-start.4 = (f32[4,8,128]{2,1,0:T(8,128)S(1)}, f32[4,8,128]{2,1,0:T(8,128)S(1)}, u32[]{:S(2)}, u32[]{:S(2)}) collective-permute-start(f32[4,8,128]{2,1,0:T(8,128)S(1)} %get-tuple-element.34), channel_id=1, source_target_pairs={{1,2},{2,1},{3,4},{4,3},{5,6},{6,5},{7,8},{8,7},{9,10},{10,9},{11,... | collective-permute-start | bytes 49160 | tf_op jit(solution)/shard_map/ppermute | solution.py:427
  36.9 3.3 %collective-permute-start.5 = (f32[4,8,128]{2,1,0:T(8,128)S(1)}, f32[4,8,128]{2,1,0:T(8,128)S(1)}, u32[]{:S(2)}, u32[]{:S(2)}) collective-permute-start(f32[4,8,128]{2,1,0:T(8,128)S(1)} %get-tuple-element.36), channel_id=1, source_target_pairs={{0,1},{1,0},{2,3},{3,2},{4,5},{5,4},{6,7},{7,6},{8,9},{9,8},{10,11... | collective-permute-start | bytes 49160 | tf_op jit(solution)/shard_map/ppermute | solution.py:428

commit v7 on v4

--- a/solution.py
+++ b/solution.py
@@ -103,15 +103,19 @@
 
 
 def score_products(mq, mk, aq):
-    pad = jnp.zeros((DEEP - 3 * TAPS, 2 * HD), jnp.float32)
     scale = math.log2(math.e) / math.sqrt(HD)
+    lane = lax.broadcasted_iota(jnp.int32, (2 * TAPS, 2 * TAPS), 1)
     for g in range(HEADS // 2):
         cols, even, odd = head_pair(g)
         q = mq[:, cols] * scale
         k = mk[:, cols]
-        q3 = jnp.concatenate([q, q, q, pad], axis=0)
+        q2 = jnp.concatenate([q, q], axis=0)
         k2 = jnp.concatenate([k * even, k * odd], axis=0)
-        aq[(g + 1) * 2 * TAPS : (g + 2) * 2 * TAPS, :] = split_lanes(nt_dot_parts(k2, q3))
+        a = nt_dot_parts(k2, q2)
+        ah = high(a)
+        aq[g * 2 * TAPS : (g + 1) * 2 * TAPS, :] = jnp.where(lane < TAPS, ah, a - ah).astype(
+            jnp.bfloat16
+        )
 
 
 def value_products(mv, nt, bb):
@@ -187,28 +191,23 @@
 
 
 def own_kernel(
-    rows, gc, mq, mk, taps, bias, wkv_hbm, wo_hbm,
-    qr, skip, bb, top, acc, p3, aq, kl, vl, sc, ex, wv, wo, sems,
+    rows, gc, mq, mk, taps, bias, wkv, wo, qr, skip, bb, top, acc, p3, aq, kl, vl, sc, ex
 ):
     local, _, _, w = rows.shape
-    copies = [
-        pltpu.make_async_copy(wkv_hbm.at[:, HEADS * HD :], wv, sems.at[0]),
-        pltpu.make_async_copy(wo_hbm, wo, sems.at[1]),
-    ]
-    for copy in copies:
-        copy.start()
-    aq[0 : 2 * TAPS, :] = gc[...]
     score_products(mq, mk, aq)
+    mv = jnp.dot(taps[0:TAPS, :], wkv[:, HEADS * HD :], preferred_element_type=jnp.float32)
+    value_products(mv, nt_dot(taps[TAPS:, :], wo[...]), bb)
     for v in range(local):
         p3[:, v * w : (v + 1) * w] = patch_stack([rows[v, i] for i in range(3)])
-    asked = jnp.dot(aq[...], p3[...], preferred_element_type=jnp.float32)
+    base = jnp.dot(gc[...], p3[...], preferred_element_type=jnp.float32)
+    asked = jnp.dot(aq[...], p3[0 : 2 * TAPS, :], preferred_element_type=jnp.float32)
     patches = p3[0:TAPS, :].astype(jnp.float32)
-    rate = token_rate(asked[0:TAPS], patches)
-    skip[...] = asked[TAPS : 2 * TAPS]
+    rate = token_rate(base[0:TAPS], patches)
+    skip[...] = base[TAPS:]
     store_keys(patches * rate, range(REACH, REACH + local), kl, vl)
     for v in range(local):
         for head in range(HEADS):
-            q = asked[(head + 2) * TAPS : (head + 3) * TAPS, v * w : (v + 1) * w]
+            q = asked[head * TAPS : (head + 1) * TAPS, v * w : (v + 1) * w]
             q = q * rate[:, v * w : (v + 1) * w]
             h = high(q)
             qr[v, :, head * w : (head + 1) * w] = jnp.concatenate(
@@ -238,11 +237,6 @@
         )
         acc[v, 0:TAPS, :] = gathered[0:TAPS] + gathered[TAPS + 8 :]
         acc[v, TAPS:, :] = gathered[TAPS : TAPS + 8]
-    copies[0].wait()
-    mv = jnp.dot(taps[0:TAPS, :], wv[...], preferred_element_type=jnp.float32)
-    copies[1].wait()
-    value_products(mv, nt_dot(taps[TAPS:, :], wo[...]), bb)
-
 
 def mix_kernel(
     prev, nxt, gc, bb, qr, skip, top, acc,
@@ -376,7 +370,7 @@
     ]
     qr, skip, bb, top, acc = pl.pallas_call(
         own_kernel,
-        in_specs=[whole] * 6 + [far] * 2,
+        in_specs=[whole] * 8,
         out_specs=[whole] * 5,
         out_shape=[
             pltpu.VMEM((local, DEEP, HEADS * w), bf16),
@@ -387,15 +381,12 @@
         ],
         scratch_shapes=[
             pltpu.VMEM((DEEP, local * w), bf16),
-            pltpu.VMEM(((HEADS + 2) * TAPS, DEEP), bf16),
+            pltpu.VMEM((HEADS * TAPS, 2 * TAPS), bf16),
             *keys_scratch,
             pltpu.VMEM((2, local * w, HEADS * w), f32),
             pltpu.VMEM((2, local * w, HEADS * w), bf16),
-            pltpu.VMEM(query_weight.shape, bf16),
-            pltpu.VMEM(out_weight.shape, bf16),
-            pltpu.SemaphoreType.DMA((2,)),
         ],
-        compiler_params=pltpu.CompilerParams(vmem_limit_bytes=49 * MIB),
+        compiler_params=pltpu.CompilerParams(vmem_limit_bytes=24 * MIB),
         cost_estimate=pl.CostEstimate(
             flops=4_000_000_000, bytes_accessed=1_000_000, transcendentals=2_000_000
         ),

time: 40.3 us -> 40.1 us (level)
  transfers between devices with their start and end apart: 6 -> 6, of which waited for: 1 -> 2; matrix products, arithmetic and copies ran while one was open for 0% -> 0% of each run, Pallas kernels for 17% -> 16%
where the time goes in v7:
time: 40.1 us; the launch traced here: 39.8 us
  starting transfers between devices  28.8 us (72%)
  Pallas kernels  8.67 us (22%)
  waiting for transfers between devices  1.57 us (4%)
  other arithmetic  0.61 us (2%)
    ppermute x1, starting transfers between devices, on_device(): lax.ppermute(tail, 'view', [(i, (i + 1) % views) for i in range(views)])  9.1 us
    ppermute x1, starting transfers between devices, on_device(): row_second = lax.ppermute(x, 'space', pairs(space, 1))  6.23 us
    ppermute x1, starting transfers between devices, on_device(): lax.ppermute(lead, 'view', [((i + 1) % views, i) for i in range(views)])  5.31 us
    ppermute x1, starting transfers between devices, on_device(): row_second = lax.ppermute(late, 'space', pairs(space, 1))  4.35 us
    pallas_call x1, Pallas kernels, on_device(): pl.pallas_call(own_kernel, in_specs=[whole] * 8, out_specs=[whole] * 5, o...  4.05 us
    pallas_call x1, Pallas kernels, on_device(): pl.pallas_call(functools.partial(prepare_kernel, views), in_specs=[far] *...  2.43 us
    pallas_call x1, Pallas kernels, on_device(): pl.pallas_call(mix_kernel, in_specs=[whole] * 8, out_specs=[whole] * 3, o...  2.16 us
    ppermute x1, starting transfers between devices, on_device(): row_first = lax.ppermute(early, 'space', pairs(space, 0))  1.92 us
  transfers between devices with their start and end apart: 6, of which 2 were waited for; matrix products, arithmetic and copies ran while one was open for 0% of the time, Pallas kernels for 16%

profile of v7, /device:TPU:6, one launch (start us, length us, event | category | flops | bytes accessed | tf_op | source)
XLA Modules:
  0.0 39.8 jit_solution(17176916152862700936)
XLA Ops:
  0.0 6.2 %collective-permute-start.1 = (bf16[4,8,128]{2,1,0:T(8,128)(2,1)}, bf16[4,8,128]{2,1,0:T(8,128)(2,1)S(1)}, u32[]{:S(2)}, u32[]{:S(2)}) collective-permute-start(bf16[4,8,128]{2,1,0:T(8,128)(2,1)} %bitcast.5), channel_id=1, source_target_pairs={{1,2},{2,1},{3,4},{4,3},{5,6},{6,5},{7,8},{8,7},{9,10},{10,9},{11,... | collective-permute-start | bytes 24584 | tf_op jit(solution)/shard_map/ppermute | solution.py:322
  6.2 1.9 %collective-permute-start = (bf16[4,8,128]{2,1,0:T(8,128)(2,1)}, bf16[4,8,128]{2,1,0:T(8,128)(2,1)S(1)}, u32[]{:S(2)}, u32[]{:S(2)}) collective-permute-start(bf16[4,8,128]{2,1,0:T(8,128)(2,1)} %bitcast.6), channel_id=1, source_target_pairs={{0,1},{1,0},{2,3},{3,2},{4,5},{5,4},{6,7},{7,6},{8,9},{9,8},{10,11... | collective-permute-start | bytes 24584 | tf_op jit(solution)/shard_map/ppermute | solution.py:321
  8.2 0.0 copy-start
  8.2 0.0 copy-start.1
  8.2 0.0 copy-start.2
  8.2 2.4 %shard_map.73 = (bf16[144,256]{1,0:T(8,128)(2,1)S(1)}, f32[72,512]{1,0:T(8,128)S(1)}, f32[72,512]{1,0:T(8,128)S(1)}, bf16[144,1024]{1,0:T(8,128)(2,1)S(1)}, f32[4,8,128]{2,1,0:T(8,128)S(1)}) custom-call(s32[2,96]{1,0:T(2,128)} %bitcast.8, bf16[3,3,8,1024]{3,2,1,0:T(8,128)(2,1)} %conv_in_hbm.1, bf16[3,3,8,1024]{3,2,1,0:T(8,128)(2,1)} %conv_out_hbm.1, ...), custom_call_target="tpu_custom_call" | custom-call | flops 3000000000 | bytes 5000000 | tf_op jit(solution)/shard_map/pallas_call | solution.py:334
  10.6 0.0 collective-permute-done.1.second
  10.6 0.0 collective-permute-done.first
  10.7 0.0 copy-done
  10.7 9.1 %collective-permute-start.2 = (bf16[2,3,8,128]{3,2,1,0:T(8,128)(2,1)S(1)}, bf16[2,3,8,128]{3,2,1,0:T(8,128)(2,1)S(1)}, u32[]{:S(2)}, u32[]{:S(2)}) collective-permute-start(bf16[2,3,8,128]{3,2,1,0:T(8,128)(2,1)S(1)} %get-tuple-element.22), channel_id=1, source_target_pairs={{0,32},{32,64},{64,96},{96,128},{128,160},{160,192},{192,224},{224... | collective-permute-start | bytes 36872 | tf_op jit(solution)/shard_map/ppermute | solution.py:364
  19.8 5.3 %collective-permute-start.3 = (bf16[2,3,8,128]{3,2,1,0:T(8,128)(2,1)S(1)}, bf16[2,3,8,128]{3,2,1,0:T(8,128)(2,1)S(1)}, u32[]{:S(2)}, u32[]{:S(2)}) collective-permute-start(bf16[2,3,8,128]{3,2,1,0:T(8,128)(2,1)S(1)} %get-tuple-element.23), channel_id=1, source_target_pairs={{32,0},{64,32},{96,64},{128,96},{160,128},{192,160},{224,192},{256... | collective-permute-start | bytes 36872 | tf_op jit(solution)/shard_map/ppermute | solution.py:365
  25.1 0.0 copy-done.1
  25.1 0.0 copy-done.2
  25.1 4.0 %shard_map.75 = (bf16[4,256,1024]{2,1,0:T(8,128)(2,1)S(1)}, f32[72,512]{1,0:T(8,128)S(1)}, bf16[4,144,144]{2,1,0:T(8,128)(2,1)S(1)}, f32[4,1024]{1,0:T(4,128)S(1)}, f32[4,80,1024]{2,1,0:T(8,128)S(1)}) custom-call(bf16[4,3,8,128]{3,2,1,0:T(8,128)(2,1)S(1)} %get-tuple-element.25.rows, bf16[144,256]{1,0:T(8,128)(2,1)S(1)} %get-tuple-element.24.gc, ...), custom_call_target="tpu_custom_call" | custom-call | flops 4000000000 | bytes 1000000 | tf_op jit(solution)/shard_map/pallas_call | solution.py:371
  29.2 0.0 collective-permute-done.2.prev
  29.2 0.1 collective-permute-done.3.nxt
  29.3 2.2 %shard_map.76 = (f32[4,8,128]{2,1,0:T(8,128)S(1)}, f32[4,8,128]{2,1,0:T(8,128)S(1)}, f32[4,8,128]{2,1,0:T(8,128)S(1)}) custom-call(bf16[2,3,8,128]{3,2,1,0:T(8,128)(2,1)S(1)} %collective-permute-done.2.prev, bf16[2,3,8,128]{3,2,1,0:T(8,128)(2,1)S(1)} %collective-permute-done.3.nxt, bf16[144,256]{1,0:T(8,128)(2,1)S(1)} %get-tuple-element.24.gc, ...), custom_call_target="tpu_custom_call" | custom-call | flops 3000000000 | bytes 1000000 | tf_op jit(solution)/shard_map/pallas_call | solution.py:396
  31.5 4.3 %collective-permute-start.4 = (f32[4,8,128]{2,1,0:T(8,128)S(1)}, f32[4,8,128]{2,1,0:T(8,128)S(1)}, u32[]{:S(2)}, u32[]{:S(2)}) collective-permute-start(f32[4,8,128]{2,1,0:T(8,128)S(1)} %get-tuple-element.34), channel_id=1, source_target_pairs={{1,2},{2,1},{3,4},{4,3},{5,6},{6,5},{7,8},{8,7},{9,10},{10,9},{11,... | collective-permute-start | bytes 49160 | tf_op jit(solution)/shard_map/ppermute | solution.py:415
  35.8 1.9 %collective-permute-start.5 = (f32[4,8,128]{2,1,0:T(8,128)S(1)}, f32[4,8,128]{2,1,0:T(8,128)S(1)}, u32[]{:S(2)}, u32[]{:S(2)}) collective-permute-start(f32[4,8,128]{2,1,0:T(8,128)S(1)} %get-tuple-element.36), channel_id=1, source_target_pairs={{0,1},{1,0},{2,3},{3,2},{4,5},{5,4},{6,7},{7,6},{8,9},{9,8},{10,11... | collective-permute-start | bytes 49160 | tf_op jit(solution)/shard_map/ppermute | solution.py:416
  37.8 1.5 %collective-permute-done.4 = f32[4,8,128]{2,1,0:T(8,128)S(1)} collective-permute-done((f32[4,8,128]{2,1,0:T(8,128)S(1)}, f32[4,8,128]{2,1,0:T(8,128)S(1)}, u32[]{:S(2)}, u32[]{:S(2)}) %collective-permute-start.4) | collective-permute-done | bytes 16416 | tf_op jit(solution)/shard_map/ppermute | solution.py:415
  39.2 0.0 collective-permute-done.5
  39.2 0.6 %add_add_fusion = f32[4,8,128]{2,1,0:T(8,128)} fusion(f32[4,8,128]{2,1,0:T(8,128)S(1)} %collective-permute-done.5, f32[4,8,128]{2,1,0:T(8,128)S(1)} %collective-permute-done.4, f32[4,8,128]{2,1,0:T(8,128)S(1)} %get-tuple-element.35), kind=kLoop, calls=%fused_computation | loop fusion | flops 8192 | bytes 65536 | tf_op jit(solution)/shard_map/add | solution.py:417
  (1 shorter events, 0.0 us)
Async XLA Ops:
  0.0 10.6 %collective-permute-start.1 = (bf16[4,8,128]{2,1,0:T(8,128)(2,1)}, bf16[4,8,128]{2,1,0:T(8,128)(2,1)S(1)}, u32[]{:S(2)}, u32[]{:S(2)}) collective-permute-start(bf16[4,8,128]{2,1,0:T(8,128)(2,1)} %bitcast.5), channel_id=1, source_target_pairs={{1,2},{2,1},{3,4},{4,3},{5,6},{6,5},{7,8},{8,7},{9,10},{10,9},{11,... | collective-permute-start | bytes 24584 | tf_op jit(solution)/shard_map/ppermute | solution.py:322
  6.2 4.4 %collective-permute-start = (bf16[4,8,128]{2,1,0:T(8,128)(2,1)}, bf16[4,8,128]{2,1,0:T(8,128)(2,1)S(1)}, u32[]{:S(2)}, u32[]{:S(2)}) collective-permute-start(bf16[4,8,128]{2,1,0:T(8,128)(2,1)} %bitcast.6), channel_id=1, source_target_pairs={{0,1},{1,0},{2,3},{3,2},{4,5},{5,4},{6,7},{7,6},{8,9},{9,8},{10,11... | collective-permute-start | bytes 24584 | tf_op jit(solution)/shard_map/ppermute | solution.py:321
  8.2 2.5 %copy-start = (bf16[4,8,1,128]{3,1,2,0:T(8,128)(2,1)S(1)}, bf16[4,8,1,128]{3,1,2,0:T(8,128)(2,1)}, u32[]{:S(2)}) copy-start(bf16[4,8,1,128]{3,1,2,0:T(8,128)(2,1)} %param.7) | copy-start | bytes 24580
  8.2 16.9 %copy-start.1 = (bf16[1024,1024]{1,0:T(8,128)(2,1)S(1)}, bf16[1024,1024]{1,0:T(8,128)(2,1)}, u32[]{:S(2)}) copy-start(bf16[1024,1024]{1,0:T(8,128)(2,1)} %wkv.1) | copy-start | bytes 6291460
  8.2 16.9 %copy-start.2 = (bf16[512,1024]{1,0:T(8,128)(2,1)S(1)}, bf16[512,1024]{1,0:T(8,128)(2,1)}, u32[]{:S(2)}) copy-start(bf16[512,1024]{1,0:T(8,128)(2,1)} %wo.1) | copy-start | bytes 3145732
  10.7 18.5 %collective-permute-start.2 = (bf16[2,3,8,128]{3,2,1,0:T(8,128)(2,1)S(1)}, bf16[2,3,8,128]{3,2,1,0:T(8,128)(2,1)S(1)}, u32[]{:S(2)}, u32[]{:S(2)}) collective-permute-start(bf16[2,3,8,128]{3,2,1,0:T(8,128)(2,1)S(1)} %get-tuple-element.22), channel_id=1, source_target_pairs={{0,32},{32,64},{64,96},{96,128},{128,160},{160,192},{192,224},{224... | collective-permute-start | bytes 36872 | tf_op jit(solution)/shard_map/ppermute | solution.py:364
  19.8 9.5 %collective-permute-start.3 = (bf16[2,3,8,128]{3,2,1,0:T(8,128)(2,1)S(1)}, bf16[2,3,8,128]{3,2,1,0:T(8,128)(2,1)S(1)}, u32[]{:S(2)}, u32[]{:S(2)}) collective-permute-start(bf16[2,3,8,128]{3,2,1,0:T(8,128)(2,1)S(1)} %get-tuple-element.23), channel_id=1, source_target_pairs={{32,0},{64,32},{96,64},{128,96},{160,128},{192,160},{224,192},{256... | collective-permute-start | bytes 36872 | tf_op jit(solution)/shard_map/ppermute | solution.py:365
  31.5 7.8 %collective-permute-start.4 = (f32[4,8,128]{2,1,0:T(8,128)S(1)}, f32[4,8,128]{2,1,0:T(8,128)S(1)}, u32[]{:S(2)}, u32[]{:S(2)}) collective-permute-start(f32[4,8,128]{2,1,0:T(8,128)S(1)} %get-tuple-element.34), channel_id=1, source_target_pairs={{1,2},{2,1},{3,4},{4,3},{5,6},{6,5},{7,8},{8,7},{9,10},{10,9},{11,... | collective-permute-start | bytes 49160 | tf_op jit(solution)/shard_map/ppermute | solution.py:415
  35.8 3.4 %collective-permute-start.5 = (f32[4,8,128]{2,1,0:T(8,128)S(1)}, f32[4,8,128]{2,1,0:T(8,128)S(1)}, u32[]{:S(2)}, u32[]{:S(2)}) collective-permute-start(f32[4,8,128]{2,1,0:T(8,128)S(1)} %get-tuple-element.36), channel_id=1, source_target_pairs={{0,1},{1,0},{2,3},{3,2},{4,5},{5,4},{6,7},{7,6},{8,9},{9,8},{10,11... | collective-permute-start | bytes 49160 | tf_op jit(solution)/shard_map/ppermute | solution.py:416

commit v8 on v7

--- a/solution.py
+++ b/solution.py
@@ -46,20 +46,29 @@
     gc, mq, mk, taps, bias, edges_ref, conv_in, conv_out, wq, wk, sems,
 ):
     parts = (
+        (conv_in_hbm, conv_in),
+        (conv_out_hbm, conv_out),
         (edges_hbm, edges_ref),
-        (conv_in_hbm, conv_in),
         (wq_hbm, wq),
         (wkv_hbm.at[:, : HEADS * HD], wk),
-        (conv_out_hbm, conv_out),
     )
     copies = [pltpu.make_async_copy(src, dst, sems.at[n]) for n, (src, dst) in enumerate(parts)]
     for copy in copies:
         copy.start()
+    copies[0].wait()
+    wc = flat_taps(conv_in)
+    wcb = wc.astype(jnp.bfloat16)
+    copies[1].wait()
+    wt = flat_taps(conv_out)
+    pad = jnp.zeros((DEEP - 3 * TAPS, wc.shape[1]), jnp.float32)
+    wc3 = jnp.concatenate([wc, wc, wc, pad], axis=0).astype(jnp.bfloat16)
+    taps[...] = jnp.concatenate([wc, wt], axis=0).astype(jnp.bfloat16)
+    gc[...] = split_lanes(nt_dot(taps[...], wc3))
     local = bias.shape[0]
     span = bias.shape[1]
     total = views * local
     first = lax.axis_index("view") * local
-    copies[0].wait()
+    copies[2].wait()
     source = edges_ref[0:1, :]
     target = edges_ref[1:2, :]
     slot = lax.broadcasted_iota(jnp.int32, (span, 1), 0)
@@ -74,19 +83,10 @@
         inside = (slot >= v) & (slot <= v + 2 * REACH)
         allowed = (linked > 0.5) & inside
         bias[v] = jnp.broadcast_to(jnp.where(allowed, 0.0, NEG_FILL), bias.shape[1:])
-    copies[1].wait()
-    wc = flat_taps(conv_in)
-    wcb = wc.astype(jnp.bfloat16)
-    copies[2].wait()
+    copies[3].wait()
     mq[...] = jnp.dot(wcb, wq[...], preferred_element_type=jnp.float32)
-    copies[3].wait()
+    copies[4].wait()
     mk[...] = jnp.dot(wcb, wk[...], preferred_element_type=jnp.float32)
-    copies[4].wait()
-    wt = flat_taps(conv_out)
-    pad = jnp.zeros((DEEP - 3 * TAPS, wc.shape[1]), jnp.float32)
-    wc3 = jnp.concatenate([wc, wc, wc, pad], axis=0).astype(jnp.bfloat16)
-    taps[...] = jnp.concatenate([wc, wt], axis=0).astype(jnp.bfloat16)
-    gc[...] = split_lanes(nt_dot(taps[...], wc3))
 
 
 def nt_dot_parts(a, b):

time: 40.1 us -> 40.1 us (level)
  no operation moved by 1% of the time
where the time goes in v8:
time: 40.1 us; the launch traced here: 39.8 us
  starting transfers between devices  28.8 us (72%)
  Pallas kernels  8.64 us (22%)
  waiting for transfers between devices  1.57 us (4%)
  other arithmetic  0.61 us (2%)
    ppermute x1, starting transfers between devices, on_device(): lax.ppermute(tail, 'view', [(i, (i + 1) % views) for i in range(views)])  9.1 us
    ppermute x1, starting transfers between devices, on_device(): row_second = lax.ppermute(x, 'space', pairs(space, 1))  6.23 us
    ppermute x1, starting transfers between devices, on_device(): lax.ppermute(lead, 'view', [((i + 1) % views, i) for i in range(views)])  5.31 us
    ppermute x1, starting transfers between devices, on_device(): row_second = lax.ppermute(late, 'space', pairs(space, 1))  4.36 us
    pallas_call x1, Pallas kernels, on_device(): pl.pallas_call(own_kernel, in_specs=[whole] * 8, out_specs=[whole] * 5, o...  4.04 us
    pallas_call x1, Pallas kernels, on_device(): pl.pallas_call(functools.partial(prepare_kernel, views), in_specs=[far] *...  2.41 us
    pallas_call x1, Pallas kernels, on_device(): pl.pallas_call(mix_kernel, in_specs=[whole] * 8, out_specs=[whole] * 3, o...  2.16 us
    ppermute x1, starting transfers between devices, on_device(): row_first = lax.ppermute(early, 'space', pairs(space, 0))  1.92 us
  transfers between devices with their start and end apart: 6, of which 2 were waited for; matrix products, arithmetic and copies ran while one was open for 0% of the time, Pallas kernels for 16%

profile of v8, /device:TPU:6, one launch (start us, length us, event | category | flops | bytes accessed | tf_op | source)
XLA Modules:
  0.0 39.8 jit_solution(18337462804584361397)
XLA Ops:
  0.0 6.2 %collective-permute-start.1 = (bf16[4,8,128]{2,1,0:T(8,128)(2,1)}, bf16[4,8,128]{2,1,0:T(8,128)(2,1)S(1)}, u32[]{:S(2)}, u32[]{:S(2)}) collective-permute-start(bf16[4,8,128]{2,1,0:T(8,128)(2,1)} %bitcast.5), channel_id=1, source_target_pairs={{1,2},{2,1},{3,4},{4,3},{5,6},{6,5},{7,8},{8,7},{9,10},{10,9},{11,... | collective-permute-start | bytes 24584 | tf_op jit(solution)/shard_map/ppermute | solution.py:322
  6.2 1.9 %collective-permute-start = (bf16[4,8,128]{2,1,0:T(8,128)(2,1)}, bf16[4,8,128]{2,1,0:T(8,128)(2,1)S(1)}, u32[]{:S(2)}, u32[]{:S(2)}) collective-permute-start(bf16[4,8,128]{2,1,0:T(8,128)(2,1)} %bitcast.6), channel_id=1, source_target_pairs={{0,1},{1,0},{2,3},{3,2},{4,5},{5,4},{6,7},{7,6},{8,9},{9,8},{10,11... | collective-permute-start | bytes 24584 | tf_op jit(solution)/shard_map/ppermute | solution.py:321
  8.2 0.0 copy-start
  8.2 0.0 copy-start.1
  8.2 0.0 copy-start.2
  8.2 2.4 %shard_map.73 = (bf16[144,256]{1,0:T(8,128)(2,1)S(1)}, f32[72,512]{1,0:T(8,128)S(1)}, f32[72,512]{1,0:T(8,128)S(1)}, bf16[144,1024]{1,0:T(8,128)(2,1)S(1)}, f32[4,8,128]{2,1,0:T(8,128)S(1)}) custom-call(s32[2,96]{1,0:T(2,128)} %bitcast.8, bf16[3,3,8,1024]{3,2,1,0:T(8,128)(2,1)} %conv_in_hbm.1, bf16[3,3,8,1024]{3,2,1,0:T(8,128)(2,1)} %conv_out_hbm.1, ...), custom_call_target="tpu_custom_call" | custom-call | flops 3000000000 | bytes 5000000 | tf_op jit(solution)/shard_map/pallas_call | solution.py:334
  10.6 0.0 collective-permute-done.1.second
  10.6 0.0 collective-permute-done.first
  10.6 0.0 copy-done
  10.7 9.1 %collective-permute-start.2 = (bf16[2,3,8,128]{3,2,1,0:T(8,128)(2,1)S(1)}, bf16[2,3,8,128]{3,2,1,0:T(8,128)(2,1)S(1)}, u32[]{:S(2)}, u32[]{:S(2)}) collective-permute-start(bf16[2,3,8,128]{3,2,1,0:T(8,128)(2,1)S(1)} %get-tuple-element.22), channel_id=1, source_target_pairs={{0,32},{32,64},{64,96},{96,128},{128,160},{160,192},{192,224},{224... | collective-permute-start | bytes 36872 | tf_op jit(solution)/shard_map/ppermute | solution.py:364
  19.8 5.3 %collective-permute-start.3 = (bf16[2,3,8,128]{3,2,1,0:T(8,128)(2,1)S(1)}, bf16[2,3,8,128]{3,2,1,0:T(8,128)(2,1)S(1)}, u32[]{:S(2)}, u32[]{:S(2)}) collective-permute-start(bf16[2,3,8,128]{3,2,1,0:T(8,128)(2,1)S(1)} %get-tuple-element.23), channel_id=1, source_target_pairs={{32,0},{64,32},{96,64},{128,96},{160,128},{192,160},{224,192},{256... | collective-permute-start | bytes 36872 | tf_op jit(solution)/shard_map/ppermute | solution.py:365
  25.1 0.0 copy-done.1
  25.1 0.0 copy-done.2
  25.1 4.0 %shard_map.75 = (bf16[4,256,1024]{2,1,0:T(8,128)(2,1)S(1)}, f32[72,512]{1,0:T(8,128)S(1)}, bf16[4,144,144]{2,1,0:T(8,128)(2,1)S(1)}, f32[4,1024]{1,0:T(4,128)S(1)}, f32[4,80,1024]{2,1,0:T(8,128)S(1)}) custom-call(bf16[4,3,8,128]{3,2,1,0:T(8,128)(2,1)S(1)} %get-tuple-element.25.rows, bf16[144,256]{1,0:T(8,128)(2,1)S(1)} %get-tuple-element.24.gc, ...), custom_call_target="tpu_custom_call" | custom-call | flops 4000000000 | bytes 1000000 | tf_op jit(solution)/shard_map/pallas_call | solution.py:371
  29.2 0.0 collective-permute-done.2.prev
  29.2 0.1 collective-permute-done.3.nxt
  29.3 2.2 %shard_map.76 = (f32[4,8,128]{2,1,0:T(8,128)S(1)}, f32[4,8,128]{2,1,0:T(8,128)S(1)}, f32[4,8,128]{2,1,0:T(8,128)S(1)}) custom-call(bf16[2,3,8,128]{3,2,1,0:T(8,128)(2,1)S(1)} %collective-permute-done.2.prev, bf16[2,3,8,128]{3,2,1,0:T(8,128)(2,1)S(1)} %collective-permute-done.3.nxt, bf16[144,256]{1,0:T(8,128)(2,1)S(1)} %get-tuple-element.24.gc, ...), custom_call_target="tpu_custom_call" | custom-call | flops 3000000000 | bytes 1000000 | tf_op jit(solution)/shard_map/pallas_call | solution.py:396
  31.4 4.4 %collective-permute-start.4 = (f32[4,8,128]{2,1,0:T(8,128)S(1)}, f32[4,8,128]{2,1,0:T(8,128)S(1)}, u32[]{:S(2)}, u32[]{:S(2)}) collective-permute-start(f32[4,8,128]{2,1,0:T(8,128)S(1)} %get-tuple-element.34), channel_id=1, source_target_pairs={{1,2},{2,1},{3,4},{4,3},{5,6},{6,5},{7,8},{8,7},{9,10},{10,9},{11,... | collective-permute-start | bytes 49160 | tf_op jit(solution)/shard_map/ppermute | solution.py:415
  35.8 1.9 %collective-permute-start.5 = (f32[4,8,128]{2,1,0:T(8,128)S(1)}, f32[4,8,128]{2,1,0:T(8,128)S(1)}, u32[]{:S(2)}, u32[]{:S(2)}) collective-permute-start(f32[4,8,128]{2,1,0:T(8,128)S(1)} %get-tuple-element.36), channel_id=1, source_target_pairs={{0,1},{1,0},{2,3},{3,2},{4,5},{5,4},{6,7},{7,6},{8,9},{9,8},{10,11... | collective-permute-start | bytes 49160 | tf_op jit(solution)/shard_map/ppermute | solution.py:416
  37.7 1.5 %collective-permute-done.4 = f32[4,8,128]{2,1,0:T(8,128)S(1)} collective-permute-done((f32[4,8,128]{2,1,0:T(8,128)S(1)}, f32[4,8,128]{2,1,0:T(8,128)S(1)}, u32[]{:S(2)}, u32[]{:S(2)}) %collective-permute-start.4) | collective-permute-done | bytes 16416 | tf_op jit(solution)/shard_map/ppermute | solution.py:415
  39.2 0.0 collective-permute-done.5
  39.2 0.6 %add_add_fusion = f32[4,8,128]{2,1,0:T(8,128)} fusion(f32[4,8,128]{2,1,0:T(8,128)S(1)} %collective-permute-done.5, f32[4,8,128]{2,1,0:T(8,128)S(1)} %collective-permute-done.4, f32[4,8,128]{2,1,0:T(8,128)S(1)} %get-tuple-element.35), kind=kLoop, calls=%fused_computation | loop fusion | flops 8192 | bytes 65536 | tf_op jit(solution)/shard_map/add | solution.py:417
  (1 shorter events, 0.0 us)
Async XLA Ops:
  0.0 10.6 %collective-permute-start.1 = (bf16[4,8,128]{2,1,0:T(8,128)(2,1)}, bf16[4,8,128]{2,1,0:T(8,128)(2,1)S(1)}, u32[]{:S(2)}, u32[]{:S(2)}) collective-permute-start(bf16[4,8,128]{2,1,0:T(8,128)(2,1)} %bitcast.5), channel_id=1, source_target_pairs={{1,2},{2,1},{3,4},{4,3},{5,6},{6,5},{7,8},{8,7},{9,10},{10,9},{11,... | collective-permute-start | bytes 24584 | tf_op jit(solution)/shard_map/ppermute | solution.py:322
  6.2 4.4 %collective-permute-start = (bf16[4,8,128]{2,1,0:T(8,128)(2,1)}, bf16[4,8,128]{2,1,0:T(8,128)(2,1)S(1)}, u32[]{:S(2)}, u32[]{:S(2)}) collective-permute-start(bf16[4,8,128]{2,1,0:T(8,128)(2,1)} %bitcast.6), channel_id=1, source_target_pairs={{0,1},{1,0},{2,3},{3,2},{4,5},{5,4},{6,7},{7,6},{8,9},{9,8},{10,11... | collective-permute-start | bytes 24584 | tf_op jit(solution)/shard_map/ppermute | solution.py:321
  8.2 2.5 %copy-start = (bf16[4,8,1,128]{3,1,2,0:T(8,128)(2,1)S(1)}, bf16[4,8,1,128]{3,1,2,0:T(8,128)(2,1)}, u32[]{:S(2)}) copy-start(bf16[4,8,1,128]{3,1,2,0:T(8,128)(2,1)} %param.7) | copy-start | bytes 24580
  8.2 16.9 %copy-start.1 = (bf16[1024,1024]{1,0:T(8,128)(2,1)S(1)}, bf16[1024,1024]{1,0:T(8,128)(2,1)}, u32[]{:S(2)}) copy-start(bf16[1024,1024]{1,0:T(8,128)(2,1)} %wkv.1) | copy-start | bytes 6291460
  8.2 16.9 %copy-start.2 = (bf16[512,1024]{1,0:T(8,128)(2,1)S(1)}, bf16[512,1024]{1,0:T(8,128)(2,1)}, u32[]{:S(2)}) copy-start(bf16[512,1024]{1,0:T(8,128)(2,1)} %wo.1) | copy-start | bytes 3145732
  10.7 18.5 %collective-permute-start.2 = (bf16[2,3,8,128]{3,2,1,0:T(8,128)(2,1)S(1)}, bf16[2,3,8,128]{3,2,1,0:T(8,128)(2,1)S(1)}, u32[]{:S(2)}, u32[]{:S(2)}) collective-permute-start(bf16[2,3,8,128]{3,2,1,0:T(8,128)(2,1)S(1)} %get-tuple-element.22), channel_id=1, source_target_pairs={{0,32},{32,64},{64,96},{96,128},{128,160},{160,192},{192,224},{224... | collective-permute-start | bytes 36872 | tf_op jit(solution)/shard_map/ppermute | solution.py:364
  19.8 9.5 %collective-permute-start.3 = (bf16[2,3,8,128]{3,2,1,0:T(8,128)(2,1)S(1)}, bf16[2,3,8,128]{3,2,1,0:T(8,128)(2,1)S(1)}, u32[]{:S(2)}, u32[]{:S(2)}) collective-permute-start(bf16[2,3,8,128]{3,2,1,0:T(8,128)(2,1)S(1)} %get-tuple-element.23), channel_id=1, source_target_pairs={{32,0},{64,32},{96,64},{128,96},{160,128},{192,160},{224,192},{256... | collective-permute-start | bytes 36872 | tf_op jit(solution)/shard_map/ppermute | solution.py:365
  31.4 7.8 %collective-permute-start.4 = (f32[4,8,128]{2,1,0:T(8,128)S(1)}, f32[4,8,128]{2,1,0:T(8,128)S(1)}, u32[]{:S(2)}, u32[]{:S(2)}) collective-permute-start(f32[4,8,128]{2,1,0:T(8,128)S(1)} %get-tuple-element.34), channel_id=1, source_target_pairs={{1,2},{2,1},{3,4},{4,3},{5,6},{6,5},{7,8},{8,7},{9,10},{10,9},{11,... | collective-permute-start | bytes 49160 | tf_op jit(solution)/shard_map/ppermute | solution.py:415
  35.8 3.4 %collective-permute-start.5 = (f32[4,8,128]{2,1,0:T(8,128)S(1)}, f32[4,8,128]{2,1,0:T(8,128)S(1)}, u32[]{:S(2)}, u32[]{:S(2)}) collective-permute-start(f32[4,8,128]{2,1,0:T(8,128)S(1)} %get-tuple-element.36), channel_id=1, source_target_pairs={{0,1},{1,0},{2,3},{3,2},{4,5},{5,4},{6,7},{7,6},{8,9},{9,8},{10,11... | collective-permute-start | bytes 49160 | tf_op jit(solution)/shard_map/ppermute | solution.py:416

commit v9 on v8

--- a/solution.py
+++ b/solution.py
@@ -43,14 +43,14 @@
 
 def prepare_kernel(
     views, edges_hbm, conv_in_hbm, conv_out_hbm, wq_hbm, wkv_hbm,
-    gc, mq, mk, taps, bias, edges_ref, conv_in, conv_out, wq, wk, sems,
+    gc, mq, mk, taps, bias, edges_ref, conv_in, conv_out, wqk, sems,
 ):
     parts = (
         (conv_in_hbm, conv_in),
         (conv_out_hbm, conv_out),
         (edges_hbm, edges_ref),
-        (wq_hbm, wq),
-        (wkv_hbm.at[:, : HEADS * HD], wk),
+        (wq_hbm, wqk.at[:, : HEADS * HD]),
+        (wkv_hbm.at[:, : HEADS * HD], wqk.at[:, HEADS * HD :]),
     )
     copies = [pltpu.make_async_copy(src, dst, sems.at[n]) for n, (src, dst) in enumerate(parts)]
     for copy in copies:
@@ -84,9 +84,10 @@
         allowed = (linked > 0.5) & inside
         bias[v] = jnp.broadcast_to(jnp.where(allowed, 0.0, NEG_FILL), bias.shape[1:])
     copies[3].wait()
-    mq[...] = jnp.dot(wcb, wq[...], preferred_element_type=jnp.float32)
     copies[4].wait()
-    mk[...] = jnp.dot(wcb, wk[...], preferred_element_type=jnp.float32)
+    images = jnp.dot(wcb, wqk[...], preferred_element_type=jnp.float32)
+    mq[...] = images[:, : HEADS * HD]
+    mk[...] = images[:, HEADS * HD :]
 
 
 def nt_dot_parts(a, b):
@@ -344,7 +345,7 @@
         ],
         scratch_shapes=[
             pltpu.VMEM(a.shape, a.dtype)
-            for a in (*loaded[:4], query_weight)
+            for a in (*loaded[:3], key_value_weight)
         ]
         + [pltpu.SemaphoreType.DMA((5,))],
         compiler_params=pltpu.CompilerParams(vmem_limit_bytes=60 * MIB),

time: 40.1 us -> 40.2 us (level)
  no operation moved by 1% of the time
where the time goes in v9:
time: 40.2 us; the launch traced here: 39.9 us
  starting transfers between devices  28.8 us (72%)
  Pallas kernels  8.7 us (22%)
  waiting for transfers between devices  1.56 us (4%)
  other arithmetic  0.61 us (2%)
    ppermute x1, starting transfers between devices, on_device(): lax.ppermute(tail, 'view', [(i, (i + 1) % views) for i in range(views)])  9.1 us
    ppermute x1, starting transfers between devices, on_device(): row_second = lax.ppermute(x, 'space', pairs(space, 1))  6.23 us
    ppermute x1, starting transfers between devices, on_device(): lax.ppermute(lead, 'view', [((i + 1) % views, i) for i in range(views)])  5.31 us
    ppermute x1, starting transfers between devices, on_device(): row_second = lax.ppermute(late, 'space', pairs(space, 1))  4.36 us
    pallas_call x1, Pallas kernels, on_device(): pl.pallas_call(own_kernel, in_specs=[whole] * 8, out_specs=[whole] * 5, o...  4.04 us
    pallas_call x1, Pallas kernels, on_device(): pl.pallas_call(functools.partial(prepare_kernel, views), in_specs=[far] *...  2.48 us
    pallas_call x1, Pallas kernels, on_device(): pl.pallas_call(mix_kernel, in_specs=[whole] * 8, out_specs=[whole] * 3, o...  2.16 us
    ppermute x1, starting transfers between devices, on_device(): row_first = lax.ppermute(early, 'space', pairs(space, 0))  1.92 us
  transfers between devices with their start and end apart: 6, of which 2 were waited for; matrix products, arithmetic and copies ran while one was open for 0% of the time, Pallas kernels for 16%

profile of v9, /device:TPU:6, one launch (start us, length us, event | category | flops | bytes accessed | tf_op | source)
XLA Modules:
  0.0 39.9 jit_solution(12922680995710230587)
XLA Ops:
  0.0 6.2 %collective-permute-start.1 = (bf16[4,8,128]{2,1,0:T(8,128)(2,1)}, bf16[4,8,128]{2,1,0:T(8,128)(2,1)S(1)}, u32[]{:S(2)}, u32[]{:S(2)}) collective-permute-start(bf16[4,8,128]{2,1,0:T(8,128)(2,1)} %bitcast.5), channel_id=1, source_target_pairs={{1,2},{2,1},{3,4},{4,3},{5,6},{6,5},{7,8},{8,7},{9,10},{10,9},{11,... | collective-permute-start | bytes 24584 | tf_op jit(solution)/shard_map/ppermute | solution.py:323
  6.2 1.9 %collective-permute-start = (bf16[4,8,128]{2,1,0:T(8,128)(2,1)}, bf16[4,8,128]{2,1,0:T(8,128)(2,1)S(1)}, u32[]{:S(2)}, u32[]{:S(2)}) collective-permute-start(bf16[4,8,128]{2,1,0:T(8,128)(2,1)} %bitcast.6), channel_id=1, source_target_pairs={{0,1},{1,0},{2,3},{3,2},{4,5},{5,4},{6,7},{7,6},{8,9},{9,8},{10,11... | collective-permute-start | bytes 24584 | tf_op jit(solution)/shard_map/ppermute | solution.py:322
  8.2 0.0 copy-start
  8.2 0.0 copy-start.1
  8.2 0.0 copy-start.2
  8.2 2.5 %shard_map.73 = (bf16[144,256]{1,0:T(8,128)(2,1)S(1)}, f32[72,512]{1,0:T(8,128)S(1)}, f32[72,512]{1,0:T(8,128)S(1)}, bf16[144,1024]{1,0:T(8,128)(2,1)S(1)}, f32[4,8,128]{2,1,0:T(8,128)S(1)}) custom-call(s32[2,96]{1,0:T(2,128)} %bitcast.8, bf16[3,3,8,1024]{3,2,1,0:T(8,128)(2,1)} %conv_in_hbm.1, bf16[3,3,8,1024]{3,2,1,0:T(8,128)(2,1)} %conv_out_hbm.1, ...), custom_call_target="tpu_custom_call" | custom-call | flops 3000000000 | bytes 5000000 | tf_op jit(solution)/shard_map/pallas_call | solution.py:335
  10.7 0.0 collective-permute-done.1.second
  10.7 0.0 collective-permute-done.first
  10.7 0.0 copy-done
  10.7 9.1 %collective-permute-start.2 = (bf16[2,3,8,128]{3,2,1,0:T(8,128)(2,1)S(1)}, bf16[2,3,8,128]{3,2,1,0:T(8,128)(2,1)S(1)}, u32[]{:S(2)}, u32[]{:S(2)}) collective-permute-start(bf16[2,3,8,128]{3,2,1,0:T(8,128)(2,1)S(1)} %get-tuple-element.22), channel_id=1, source_target_pairs={{0,32},{32,64},{64,96},{96,128},{128,160},{160,192},{192,224},{224... | collective-permute-start | bytes 36872 | tf_op jit(solution)/shard_map/ppermute | solution.py:365
  19.8 5.3 %collective-permute-start.3 = (bf16[2,3,8,128]{3,2,1,0:T(8,128)(2,1)S(1)}, bf16[2,3,8,128]{3,2,1,0:T(8,128)(2,1)S(1)}, u32[]{:S(2)}, u32[]{:S(2)}) collective-permute-start(bf16[2,3,8,128]{3,2,1,0:T(8,128)(2,1)S(1)} %get-tuple-element.23), channel_id=1, source_target_pairs={{32,0},{64,32},{96,64},{128,96},{160,128},{192,160},{224,192},{256... | collective-permute-start | bytes 36872 | tf_op jit(solution)/shard_map/ppermute | solution.py:366
  25.2 0.0 copy-done.1
  25.2 0.0 copy-done.2
  25.2 4.0 %shard_map.75 = (bf16[4,256,1024]{2,1,0:T(8,128)(2,1)S(1)}, f32[72,512]{1,0:T(8,128)S(1)}, bf16[4,144,144]{2,1,0:T(8,128)(2,1)S(1)}, f32[4,1024]{1,0:T(4,128)S(1)}, f32[4,80,1024]{2,1,0:T(8,128)S(1)}) custom-call(bf16[4,3,8,128]{3,2,1,0:T(8,128)(2,1)S(1)} %get-tuple-element.25.rows, bf16[144,256]{1,0:T(8,128)(2,1)S(1)} %get-tuple-element.24.gc, ...), custom_call_target="tpu_custom_call" | custom-call | flops 4000000000 | bytes 1000000 | tf_op jit(solution)/shard_map/pallas_call | solution.py:372
  29.2 0.0 collective-permute-done.2.prev
  29.2 0.1 collective-permute-done.3.nxt
  29.3 2.2 %shard_map.76 = (f32[4,8,128]{2,1,0:T(8,128)S(1)}, f32[4,8,128]{2,1,0:T(8,128)S(1)}, f32[4,8,128]{2,1,0:T(8,128)S(1)}) custom-call(bf16[2,3,8,128]{3,2,1,0:T(8,128)(2,1)S(1)} %collective-permute-done.2.prev, bf16[2,3,8,128]{3,2,1,0:T(8,128)(2,1)S(1)} %collective-permute-done.3.nxt, bf16[144,256]{1,0:T(8,128)(2,1)S(1)} %get-tuple-element.24.gc, ...), custom_call_target="tpu_custom_call" | custom-call | flops 3000000000 | bytes 1000000 | tf_op jit(solution)/shard_map/pallas_call | solution.py:397
  31.5 4.4 %collective-permute-start.4 = (f32[4,8,128]{2,1,0:T(8,128)S(1)}, f32[4,8,128]{2,1,0:T(8,128)S(1)}, u32[]{:S(2)}, u32[]{:S(2)}) collective-permute-start(f32[4,8,128]{2,1,0:T(8,128)S(1)} %get-tuple-element.34), channel_id=1, source_target_pairs={{1,2},{2,1},{3,4},{4,3},{5,6},{6,5},{7,8},{8,7},{9,10},{10,9},{11,... | collective-permute-start | bytes 49160 | tf_op jit(solution)/shard_map/ppermute | solution.py:416
  35.9 1.9 %collective-permute-start.5 = (f32[4,8,128]{2,1,0:T(8,128)S(1)}, f32[4,8,128]{2,1,0:T(8,128)S(1)}, u32[]{:S(2)}, u32[]{:S(2)}) collective-permute-start(f32[4,8,128]{2,1,0:T(8,128)S(1)} %get-tuple-element.36), channel_id=1, source_target_pairs={{0,1},{1,0},{2,3},{3,2},{4,5},{5,4},{6,7},{7,6},{8,9},{9,8},{10,11... | collective-permute-start | bytes 49160 | tf_op jit(solution)/shard_map/ppermute | solution.py:417
  37.8 1.5 %collective-permute-done.4 = f32[4,8,128]{2,1,0:T(8,128)S(1)} collective-permute-done((f32[4,8,128]{2,1,0:T(8,128)S(1)}, f32[4,8,128]{2,1,0:T(8,128)S(1)}, u32[]{:S(2)}, u32[]{:S(2)}) %collective-permute-start.4) | collective-permute-done | bytes 16416 | tf_op jit(solution)/shard_map/ppermute | solution.py:416
  39.3 0.0 collective-permute-done.5
  39.3 0.6 %add_add_fusion = f32[4,8,128]{2,1,0:T(8,128)} fusion(f32[4,8,128]{2,1,0:T(8,128)S(1)} %collective-permute-done.5, f32[4,8,128]{2,1,0:T(8,128)S(1)} %collective-permute-done.4, f32[4,8,128]{2,1,0:T(8,128)S(1)} %get-tuple-element.35), kind=kLoop, calls=%fused_computation | loop fusion | flops 8192 | bytes 65536 | tf_op jit(solution)/shard_map/add | solution.py:418
  (1 shorter events, 0.0 us)
Async XLA Ops:
  0.0 10.7 %collective-permute-start.1 = (bf16[4,8,128]{2,1,0:T(8,128)(2,1)}, bf16[4,8,128]{2,1,0:T(8,128)(2,1)S(1)}, u32[]{:S(2)}, u32[]{:S(2)}) collective-permute-start(bf16[4,8,128]{2,1,0:T(8,128)(2,1)} %bitcast.5), channel_id=1, source_target_pairs={{1,2},{2,1},{3,4},{4,3},{5,6},{6,5},{7,8},{8,7},{9,10},{10,9},{11,... | collective-permute-start | bytes 24584 | tf_op jit(solution)/shard_map/ppermute | solution.py:323
  6.2 4.5 %collective-permute-start = (bf16[4,8,128]{2,1,0:T(8,128)(2,1)}, bf16[4,8,128]{2,1,0:T(8,128)(2,1)S(1)}, u32[]{:S(2)}, u32[]{:S(2)}) collective-permute-start(bf16[4,8,128]{2,1,0:T(8,128)(2,1)} %bitcast.6), channel_id=1, source_target_pairs={{0,1},{1,0},{2,3},{3,2},{4,5},{5,4},{6,7},{7,6},{8,9},{9,8},{10,11... | collective-permute-start | bytes 24584 | tf_op jit(solution)/shard_map/ppermute | solution.py:322
  8.2 2.5 %copy-start = (bf16[4,8,1,128]{3,1,2,0:T(8,128)(2,1)S(1)}, bf16[4,8,1,128]{3,1,2,0:T(8,128)(2,1)}, u32[]{:S(2)}) copy-start(bf16[4,8,1,128]{3,1,2,0:T(8,128)(2,1)} %param.7) | copy-start | bytes 24580
  8.2 17.0 %copy-start.1 = (bf16[1024,1024]{1,0:T(8,128)(2,1)S(1)}, bf16[1024,1024]{1,0:T(8,128)(2,1)}, u32[]{:S(2)}) copy-start(bf16[1024,1024]{1,0:T(8,128)(2,1)} %wkv.1) | copy-start | bytes 6291460
  8.2 17.0 %copy-start.2 = (bf16[512,1024]{1,0:T(8,128)(2,1)S(1)}, bf16[512,1024]{1,0:T(8,128)(2,1)}, u32[]{:S(2)}) copy-start(bf16[512,1024]{1,0:T(8,128)(2,1)} %wo.1) | copy-start | bytes 3145732
  10.7 18.5 %collective-permute-start.2 = (bf16[2,3,8,128]{3,2,1,0:T(8,128)(2,1)S(1)}, bf16[2,3,8,128]{3,2,1,0:T(8,128)(2,1)S(1)}, u32[]{:S(2)}, u32[]{:S(2)}) collective-permute-start(bf16[2,3,8,128]{3,2,1,0:T(8,128)(2,1)S(1)} %get-tuple-element.22), channel_id=1, source_target_pairs={{0,32},{32,64},{64,96},{96,128},{128,160},{160,192},{192,224},{224... | collective-permute-start | bytes 36872 | tf_op jit(solution)/shard_map/ppermute | solution.py:365
  19.8 9.5 %collective-permute-start.3 = (bf16[2,3,8,128]{3,2,1,0:T(8,128)(2,1)S(1)}, bf16[2,3,8,128]{3,2,1,0:T(8,128)(2,1)S(1)}, u32[]{:S(2)}, u32[]{:S(2)}) collective-permute-start(bf16[2,3,8,128]{3,2,1,0:T(8,128)(2,1)S(1)} %get-tuple-element.23), channel_id=1, source_target_pairs={{32,0},{64,32},{96,64},{128,96},{160,128},{192,160},{224,192},{256... | collective-permute-start | bytes 36872 | tf_op jit(solution)/shard_map/ppermute | solution.py:366
  31.5 7.8 %collective-permute-start.4 = (f32[4,8,128]{2,1,0:T(8,128)S(1)}, f32[4,8,128]{2,1,0:T(8,128)S(1)}, u32[]{:S(2)}, u32[]{:S(2)}) collective-permute-start(f32[4,8,128]{2,1,0:T(8,128)S(1)} %get-tuple-element.34), channel_id=1, source_target_pairs={{1,2},{2,1},{3,4},{4,3},{5,6},{6,5},{7,8},{8,7},{9,10},{10,9},{11,... | collective-permute-start | bytes 49160 | tf_op jit(solution)/shard_map/ppermute | solution.py:416
  35.9 3.4 %collective-permute-start.5 = (f32[4,8,128]{2,1,0:T(8,128)S(1)}, f32[4,8,128]{2,1,0:T(8,128)S(1)}, u32[]{:S(2)}, u32[]{:S(2)}) collective-permute-start(f32[4,8,128]{2,1,0:T(8,128)S(1)} %get-tuple-element.36), channel_id=1, source_target_pairs={{0,1},{1,0},{2,3},{3,2},{4,5},{5,4},{6,7},{7,6},{8,9},{9,8},{10,11... | collective-permute-start | bytes 49160 | tf_op jit(solution)/shard_map/ppermute | solution.py:417
